TPU v7x, 256 devices: a whole 4x4x8 slice. The times are simulated.
256 devices in a mesh: term: 32 (over y, x, core), sec: 8 (over z).
Axes of the slice: x: 4, y: 4, z: 8, core: 2. Of those that a mesh axis runs over, the one named last changes fastest.
Arguments:
- psi: float32 [2, 1024, 1024], P(None, None, 'sec'), may hold values from -6 to 6
- diag: float32 [2, 1024, 1024], P(None, None, 'sec'), may hold values from 0.5 to 40
- block_dims: int32 [2, 2], replicated, may hold values from 512 to 1024, as said below
- left_env: bfloat16 [32, 2, 1024, 1024], P('term'), may hold values from -0.1875 to 0.1875
- right_env: bfloat16 [32, 2, 1024, 1024], P('term'), may hold values from -0.1875 to 0.1875
Outputs:
- new_psi: float32 [2, 1024, 1024], P(None, None, 'sec')
- energy: float32 [], replicated
Inputs may be any that keep to these rules, and one draw needn't show every extreme that they name: `block_dims`: sector 0 uses the whole padded block; every other sector uses at least half of the rows and half of the columns.
All inputs are finite; a program needn't handle non-finite values.
Results may differ from a plain program's by a relative error of at most 0.0027.
The roundings to bfloat16 on the way count: a program that leaves them out, or rounds other values in their place, can miss the bound.
Values may be sent and summed in bfloat16 or wider, within the bound.
No kernel may reach another device: no remote copies, remote signals or barrier semaphores. Data moves between devices by JAX's collectives and lax.ppermute only.
A program may use at most 64 MiB of HBM per device.

v0:
```python
import jax
import jax.numpy as jnp
from jax import lax
from jax.sharding import PartitionSpec as P

ITERS = 2


def per_device(psi, diag, block_dims, left_env, right_env):
    sectors, rows_all, cols_here = psi.shape
    scale = 1.0 / (rows_all * rows_all)
    positions = jnp.arange(rows_all, dtype=jnp.int32)
    col_ids = lax.axis_index("sec") * cols_here + jnp.arange(cols_here, dtype=jnp.int32)
    row_ok = positions[None, :, None] < block_dims[:, 0][:, None, None]
    col_ok = col_ids[None, None, :] < block_dims[:, 1][:, None, None]
    mask = (row_ok & col_ok).astype(jnp.float32)

    def local_dot(first, second):
        return jnp.sum(first * second) * scale

    def apply_ham(field):
        field_low = field.astype(jnp.bfloat16)
        left = jnp.einsum(
            "wsik,skc->wsic", left_env, field_low, preferred_element_type=jnp.float32
        ).astype(jnp.bfloat16)
        moved = lax.all_to_all(left, "sec", split_axis=2, concat_axis=3, tiled=True)
        partial_sum = jnp.einsum(
            "wsic,wsjc->sij", moved, right_env, preferred_element_type=jnp.float32
        )
        summed = lax.psum(partial_sum, "term")
        back = lax.all_to_all(summed, "sec", split_axis=2, concat_axis=1, tiled=True)
        return back * mask

    start = psi * mask
    start_sum = lax.psum(local_dot(start, start), "sec")
    vector = start / jnp.sqrt(start_sum)
    image = apply_ham(vector)
    theta = jnp.float32(0.0)
    lowest = jnp.float32(0.0)
    for step in range(ITERS):
        theta = lax.psum(local_dot(vector, image), "sec")
        corr = (image - theta * vector) / (1.0 + jnp.abs(diag - theta))
        project = lax.psum(local_dot(vector, corr), "sec")
        orth = corr - project * vector
        orth_sum = lax.psum(local_dot(orth, orth), "sec")
        fresh = orth / jnp.sqrt(orth_sum)
        fresh_image = apply_ham(fresh)
        cross_one, cross_two, corner = lax.psum(
            (
                local_dot(vector, fresh_image),
                local_dot(fresh, image),
                local_dot(fresh, fresh_image),
            ),
            "sec",
        )
        cross = 0.5 * (cross_one + cross_two)
        lowest = 0.5 * (theta + corner) - jnp.sqrt((0.5 * (theta - corner)) ** 2 + cross * cross)
        weight_old = corner - lowest
        weight_new = -cross
        scale_sum = jnp.sqrt(weight_old * weight_old + weight_new * weight_new)
        weight_old = weight_old / scale_sum
        weight_new = weight_new / scale_sum
        vector = weight_old * vector + weight_new * fresh
        image = weight_old * image + weight_new * fresh_image
    return (vector, lowest)


def solution(mesh):
    in_specs = (
        P(None, None, "sec"),
        P(None, None, "sec"),
        P(),
        P("term", None, None, None),
        P("term", None, None, None),
    )
    out_specs = (P(None, None, "sec"), P())
    return jax.shard_map(
        per_device, mesh=mesh, in_specs=in_specs, out_specs=out_specs, check_vma=False
    )
```

profile of v0, /device:TPU:1, one launch (start us, length us, event | category | flops | bytes accessed | tf_op | source)
XLA Modules:
  0.0 739.8 jit_solution(7554786678545811456)
XLA Ops:
  7.2 0.0 all-reduce.6.cloned.1.call-start
  7.2 1.0 slice_reduce_fusion.1
  8.2 0.1 iota_compare_fusion
  8.3 0.1 broadcast_compare_fusion
  8.3 2.2 multiply_reduce_fusion.12
  11.2 17.8 %psum.112 = f32[]{:T(128)} all-reduce(f32[]{:T(128)S(6)} %mul.184), channel_id=1, replica_groups=mesh['term'=32,'sec'=8] {'sec'}, use_global_device_ids=true, to_apply=%region_1.0 | all-reduce | flops 1 | bytes 8 | tf_op jit(solution)/shard_map/psum | solution.py:35
  29.7 4.0 fusion.27
  33.7 0.4 copy.17
  34.1 15.3 %all_to_all.99 = bf16[1,2,1024,128]{3,1,0,2:T(2,128)(2,1)S(1)} all-to-all(bf16[1,2,1024,128]{3,1,0,2:T(2,128)(2,1)S(1)} %copy.17), channel_id=1, replica_groups=mesh['term'=32,'sec'=8] {'sec'}, dimensions={2} | all-to-all | bytes 1048576 | tf_op jit(solution)/shard_map/all_to_all | solution.py:26
  49.5 0.3 copy.39
  49.8 0.2 reshape.95
  50.0 4.7 fusion.4
  54.7 0.0 all-reduce.6.cloned.1.call-update
  54.8 0.0 all-reduce.8.cloned.1.call-start
  54.8 116.7 %all-reduce.6.cloned.1.call-done = f32[2,128,1024]{2,1,0:T(8,128)} async-done(((f32[2,128,1024]{2,1,0:T(8,128)}), f32[2,128,1024]{2,1,0:T(8,128)}) %all-reduce.6.cloned.1.call-update) | async-done | bytes 1048592 | tf_op jit(solution)/shard_map/psum | solution.py:30
  171.5 1.5 copy.19
  173.0 33.7 %all_to_all.100 = f32[2,128,1024]{1,0,2:T(2,128)} all-to-all(f32[2,128,1024]{1,0,2:T(2,128)S(1)} %copy.19), channel_id=1, replica_groups=mesh['term'=32,'sec'=8] {'sec'}, dimensions={2} | all-to-all | bytes 2097152 | tf_op jit(solution)/shard_map/all_to_all | solution.py:31
  206.7 1.5 copy.20
  208.2 1.1 multiply_reduce_fusion.11
  210.0 11.2 %psum.114 = f32[]{:T(128)} all-reduce(f32[]{:T(128)S(6)} %mul.187), channel_id=1, replica_groups=mesh['term'=32,'sec'=8] {'sec'}, use_global_device_ids=true, to_apply=%region_4.0 | all-reduce | flops 1 | bytes 8 | tf_op jit(solution)/shard_map/psum | solution.py:41
  221.1 1.9 multiply_reduce_fusion.10
  223.7 13.0 %psum.115 = f32[]{:T(128)} all-reduce(f32[]{:T(128)S(6)} %mul.191), channel_id=1, replica_groups=mesh['term'=32,'sec'=8] {'sec'}, use_global_device_ids=true, to_apply=%region_6.0 | all-reduce | flops 1 | bytes 8 | tf_op jit(solution)/shard_map/psum | solution.py:43
  236.7 2.7 multiply_reduce_fusion.9
  240.1 11.3 %psum.116 = f32[]{:T(128)} all-reduce(f32[]{:T(128)S(6)} %mul.195), channel_id=1, replica_groups=mesh['term'=32,'sec'=8] {'sec'}, use_global_device_ids=true, to_apply=%region_8.0 | all-reduce | flops 1 | bytes 8 | tf_op jit(solution)/shard_map/psum | solution.py:45
  252.1 0.0 copy-start.6
  252.1 2.3 broadcast_divide_fusion.1
  254.5 1.0 copy-done.8
  255.5 2.3 fusion.24
  257.8 2.0 copy.22
  259.8 16.6 %all_to_all.101 = bf16[1,2,1024,128]{3,1,0,2:T(2,128)(2,1)S(1)} all-to-all(bf16[1,2,1024,128]{3,1,0,2:T(2,128)(2,1)} %copy.22), channel_id=1, replica_groups=mesh['term'=32,'sec'=8] {'sec'}, dimensions={2} | all-to-all | bytes 1048576 | tf_op jit(solution)/shard_map/all_to_all | solution.py:26
  276.4 1.1 copy.38
  277.5 2.1 reshape.97
  279.6 4.8 fusion.2
  284.4 0.0 all-reduce.8.cloned.1.call-update
  284.4 0.0 all-reduce.10.cloned.1.call-start
  284.5 123.3 %all-reduce.8.cloned.1.call-done = f32[2,128,1024]{2,1,0:T(8,128)} async-done(((f32[2,128,1024]{2,1,0:T(8,128)}), f32[2,128,1024]{2,1,0:T(8,128)}) %all-reduce.8.cloned.1.call-update) | async-done | bytes 1048592 | tf_op jit(solution)/shard_map/psum | solution.py:30
  407.8 2.2 copy.24
  410.0 33.9 %all_to_all.102 = f32[2,128,1024]{1,0,2:T(2,128)} all-to-all(f32[2,128,1024]{1,0,2:T(2,128)} %copy.24), channel_id=1, replica_groups=mesh['term'=32,'sec'=8] {'sec'}, dimensions={2} | all-to-all | bytes 2097152 | tf_op jit(solution)/shard_map/all_to_all | solution.py:31
  443.9 2.3 copy.25
  446.2 2.5 multiply_reduce_fusion.8
  450.5 11.3 %all-reduce.1 = (f32[]{:T(128)}, f32[]{:T(128)}) all-reduce(f32[]{:T(128)S(6)} %multiply.18, f32[]{:T(128)S(6)} %mul.198), channel_id=1, replica_groups=mesh['term'=32,'sec'=8] {'sec'}, use_global_device_ids=true, to_apply=%region_13.0 | all-reduce | flops 2 | bytes 16 | tf_op jit(solution)/shard_map/psum | solution.py:48
  467.0 3.5 multiply_reduce_fusion.5
  471.3 13.0 %psum.121 = f32[]{:T(128)} all-reduce(f32[]{:T(128)S(6)} %mul.215), channel_id=1, replica_groups=mesh['term'=32,'sec'=8] {'sec'}, use_global_device_ids=true, to_apply=%region_17.0 | all-reduce | flops 1 | bytes 8 | tf_op jit(solution)/shard_map/psum | solution.py:41
  484.3 3.1 multiply_reduce_fusion.4
  488.0 11.2 %psum.122 = f32[]{:T(128)} all-reduce(f32[]{:T(128)S(6)} %mul.219), channel_id=1, replica_groups=mesh['term'=32,'sec'=8] {'sec'}, use_global_device_ids=true, to_apply=%region_19.0 | all-reduce | flops 1 | bytes 8 | tf_op jit(solution)/shard_map/psum | solution.py:43
  499.2 3.9 multiply_reduce_fusion.3
  503.8 13.1 %psum.123 = f32[]{:T(128)} all-reduce(f32[]{:T(128)S(6)} %mul.223), channel_id=1, replica_groups=mesh['term'=32,'sec'=8] {'sec'}, use_global_device_ids=true, to_apply=%region_21.0 | all-reduce | flops 1 | bytes 8 | tf_op jit(solution)/shard_map/psum | solution.py:45
  517.6 0.0 copy-start.7
  517.6 2.0 broadcast_divide_fusion
  519.6 1.0 copy-done.4
  520.6 1.5 fusion.21
  522.1 0.4 copy.27
  522.5 15.3 %all_to_all.103 = bf16[1,2,1024,128]{3,1,0,2:T(2,128)(2,1)S(1)} all-to-all(bf16[1,2,1024,128]{3,1,0,2:T(2,128)(2,1)S(1)} %copy.27), channel_id=1, replica_groups=mesh['term'=32,'sec'=8] {'sec'}, dimensions={2} | all-to-all | bytes 1048576 | tf_op jit(solution)/shard_map/all_to_all | solution.py:26
  537.9 0.3 copy.37
  538.2 0.2 reshape.98
  538.4 4.7 fusion
  543.2 0.0 all-reduce.10.cloned.1.call-update
  543.2 128.6 %all-reduce.10.cloned.1.call-done = f32[2,128,1024]{2,1,0:T(8,128)} async-done(((f32[2,128,1024]{2,1,0:T(8,128)}), f32[2,128,1024]{2,1,0:T(8,128)}) %all-reduce.10.cloned.1.call-update) | async-done | bytes 1048592 | tf_op jit(solution)/shard_map/psum | solution.py:30
  671.8 2.3 copy.29
  674.1 33.9 %all_to_all.104 = f32[2,128,1024]{1,0,2:T(2,128)} all-to-all(f32[2,128,1024]{1,0,2:T(2,128)} %copy.29), channel_id=1, replica_groups=mesh['term'=32,'sec'=8] {'sec'}, dimensions={2} | all-to-all | bytes 2097152 | tf_op jit(solution)/shard_map/all_to_all | solution.py:31
  708.0 2.3 copy.30
  710.3 2.2 multiply_reduce_fusion.2
  714.3 11.3 %all-reduce = (f32[]{:T(128)}, f32[]{:T(128)}) all-reduce(f32[]{:T(128)S(6)} %multiply.19, f32[]{:T(128)S(6)} %mul.226), channel_id=1, replica_groups=mesh['term'=32,'sec'=8] {'sec'}, use_global_device_ids=true, to_apply=%region_26.0 | all-reduce | flops 2 | bytes 16 | tf_op jit(solution)/shard_map/psum | solution.py:48
  731.1 1.1 multiply_add_fusion
  (15 shorter events, 0.0 us)
Async XLA Ops:
  7.2 164.3 %all-reduce.6.cloned.1.call-start = ((), (), s32[]{:S(2)}) async-start(), calls=%async_computation.6 | async-start | bytes 2097152 | tf_op jit(solution)/shard_map/psum | solution.py:30
  54.7 153.4 %copy-start = (f32[2,1024,128]{2,1,0:T(8,128)S(1)}, f32[2,1024,128]{2,1,0:T(8,128)}, u32[]{:S(2)}) copy-start(f32[2,1024,128]{2,1,0:T(8,128)} %param.5) | copy-start | bytes 3145732
  54.8 166.4 %copy-start.1 = (f32[2,1024,128]{2,1,0:T(8,128)S(1)}, f32[2,1024,128]{2,1,0:T(8,128)}, u32[]{:S(2)}) copy-start(f32[2,1024,128]{2,1,0:T(8,128)} %param.6) | copy-start | bytes 3145732
  54.8 353.0 %all-reduce.8.cloned.1.call-start = ((), (), s32[]{:S(2)}) async-start(), calls=%async_computation.7 | async-start | bytes 2097152 | tf_op jit(solution)/shard_map/psum | solution.py:30
  252.1 3.4 copy-start.6
  254.5 1.0 copy-start.8
  284.4 387.4 %all-reduce.10.cloned.1.call-start = ((), (), s32[]{:S(2)}) async-start(), calls=%async_computation.8 | async-start | bytes 2097152 | tf_op jit(solution)/shard_map/psum | solution.py:30
  470.5 47.1 %copy-start.2 = (f32[2,1024,128]{2,1,0:T(8,128)S(1)}, f32[2,1024,128]{2,1,0:T(8,128)}, u32[]{:S(2)}) copy-start(f32[2,1024,128]{2,1,0:T(8,128)} %get-tuple-element.16) | copy-start | bytes 3145732
  470.5 47.1 %copy-start.3 = (f32[2,1024,128]{2,1,0:T(8,128)S(1)}, f32[2,1024,128]{2,1,0:T(8,128)}, u32[]{:S(2)}) copy-start(f32[2,1024,128]{2,1,0:T(8,128)} %get-tuple-element.15) | copy-start | bytes 3145732
  517.6 3.0 copy-start.7
  519.6 1.0 copy-start.4
  543.2 167.1 %copy-start.5 = (f32[2,1024,128]{2,1,0:T(8,128)S(1)}, f32[2,1024,128]{2,1,0:T(8,128)}, u32[]{:S(2)}) copy-start(f32[2,1024,128]{2,1,0:T(8,128)} %copy-done.4) | copy-start | bytes 3145732
Sparse Core Ops, SparseCore 0:
  54.9 116.5 all-reduce.5
  284.6 123.1 all-reduce.7
  543.3 128.4 all-reduce.9
where the time goes:
time: 746 us; the launch traced here: 740 us
  waiting for transfers between devices  369 us (49%)
  blocking collectives  262 us (35%)
  between operations  36.5 us (5%)
  other arithmetic  28.7 us (4%)
  local copies, waits for them, and re-layouts  22.2 us (3%)
  matrix products  22.1 us (3%)
    psum x3, waiting for transfers between devices, apply_ham(): summed = lax.psum(partial_sum, 'term')  369 us
    all_to_all x3, blocking collectives, apply_ham(): lax.all_to_all(summed, 'sec', split_axis=2, concat_axis=1, tiled=True)  101 us
    all_to_all x3, blocking collectives, apply_ham(): moved = lax.all_to_all(left, 'sec', split_axis=2, concat_axis=3, tiled=True)  47.2 us
    psum x2, blocking collectives, per_device(): orth_sum = lax.psum(local_dot(orth, orth), 'sec')  24.3 us
    psum x2, blocking collectives, per_device(): theta = lax.psum(local_dot(vector, image), 'sec')  24.1 us
    psum x2, blocking collectives, per_device(): project = lax.psum(local_dot(vector, corr), 'sec')  24.1 us
    reduce_sum x9, other arithmetic, local_dot(): return jnp.sum(first * second) * scale  23.1 us
    psum x2, blocking collectives, per_device(): lax.psum((local_dot(vector, fresh_image), local_dot(fresh, image), local_...  22.5 us
  transfers between devices with their start and end apart: 3, of which 3 were waited for; matrix products, arithmetic and copies ran while one was open for 0% of the time, Pallas kernels for 0%

commit v1 on v0

v1 whole, which is shorter than its diff:
```python
import jax
import jax.numpy as jnp
from jax import lax
from jax.sharding import Mesh, PartitionSpec as P

ITERS = 2
XY = ("y", "x")
CZ = ("core", "sec")


def pick(array, index, axis=0):
    return lax.dynamic_index_in_dim(array, index, axis, keepdims=False)


def lanes(values, rows, width):
    lane = lax.broadcasted_iota(jnp.int32, (rows, width), 1)
    tile = jnp.zeros((rows, width), jnp.float32)
    for position, value in enumerate(values):
        tile = jnp.where(lane == position, value, tile)
    return tile


def make(n_y, n_x, n_z):
    n_xy = n_y * n_x

    def per_device(psi, diag, block_dims, left_env, right_env):
        _, size, cols = psi.shape
        sub = cols // n_xy
        scale = 1.0 / (size * size)
        core, z = lax.axis_index("core"), lax.axis_index("sec")
        q = lax.axis_index(XY)
        swap = [(0, 1), (1, 0)]

        left_got = lax.ppermute(pick(left_env[0], 1 - core), "core", swap)
        right_got = lax.ppermute(pick(right_env[0], 1 - core), "core", swap)
        lefts = (pick(left_env[0], core), left_got)
        rights = (pick(right_env[0], core), right_got)

        def a2a(array, axes):
            return lax.all_to_all(array, axes, 0, 0, tiled=True)

        def share_mask(dims):
            row = lax.broadcasted_iota(jnp.int32, (size, cols), 0)
            col = lax.broadcasted_iota(jnp.int32, (size, cols), 1) + z * cols
            return (row < dims[0]) & (col < dims[1])

        dims = pick(block_dims, core)
        shard = (n_z, sub, cols)
        shard_row = z * cols + q * sub + lax.broadcasted_iota(jnp.int32, shard, 1)
        shard_col = lax.broadcasted_iota(jnp.int32, shard, 0) * cols + lax.broadcasted_iota(jnp.int32, shard, 2)
        shard_mask = (shard_row < dims[0]) & (shard_col < dims[1])

        total = jnp.float32(0.0)
        for s in range(psi.shape[0]):
            total = total + jnp.sum(jnp.where(share_mask(block_dims[s]), psi[s] * psi[s], 0.0))
        psi_a = jnp.where(share_mask(dims), pick(psi, core), 0.0)
        diag_a = pick(diag, core)

        def own_rows(array):
            return pick(array.reshape(n_z, n_xy, sub, cols), q, 1)

        first = jnp.concatenate(
            [own_rows(psi_a), own_rows(diag_a), jnp.broadcast_to(total * scale, shard)], axis=1
        )
        first = a2a(first, "sec")
        inverse = 1.0 / jnp.sqrt(jnp.sum(first[:, 2 * sub, 0]))
        u_a, u_b = psi_a * inverse, first[:, :sub] * inverse
        diag_b = first[:, sub : 2 * sub]

        def apply_ham(field):
            field = field.astype(jnp.bfloat16)
            parts = [
                jnp.dot(env, field, preferred_element_type=jnp.float32)
                .astype(jnp.bfloat16)
                .reshape(n_z, 1, cols, cols)
                for env in lefts
            ]
            moved = a2a(jnp.concatenate(parts, axis=1), "sec")
            partial = jnp.zeros((cols, size), jnp.float32)
            for w, env in enumerate(rights):
                rows = moved[:, w].transpose(1, 0, 2).reshape(cols, size)
                partial = partial + lax.dot_general(
                    rows, env, (((1,), (1,)), ((), ())), preferred_element_type=jnp.float32
                )
            got = a2a(partial.reshape(n_xy, sub, size), XY)
            image = jnp.sum(got, axis=0).reshape(sub, n_z, cols).transpose(1, 0, 2)
            return jnp.where(shard_mask, image, 0.0)

        def dot_b(first, second):
            return jnp.sum(first * second) * scale

        def gather(image_b, values):
            block = jnp.concatenate(
                [image_b, jnp.broadcast_to(lanes(values, 8, cols)[None], (n_z, 8, cols))], axis=1
            )
            got = a2a(jnp.broadcast_to(block[None], (2,) + block.shape).reshape(2 * n_z, sub + 8, cols), CZ)
            sums = jnp.sum(got[:, sub:], axis=0)
            mine = pick(got.reshape(2, n_z, sub + 8, cols), core)[:, :sub].reshape(n_z * sub, cols)
            block = jnp.concatenate([mine, sums], axis=0)
            got = a2a(jnp.broadcast_to(block[None], (n_xy,) + block.shape), XY)
            sums = jnp.sum(got[:, n_z * sub], axis=0)
            image_a = got[:, : n_z * sub].reshape(n_xy, n_z, sub, cols).transpose(1, 0, 2, 3)
            return image_a.reshape(size, cols), [sums[k] for k in range(len(values))]

        def sum_cz(values):
            tile = lanes(values, 8, cols)
            got = a2a(jnp.broadcast_to(tile[None], (2 * n_z, 8, cols)), CZ)
            sums = jnp.sum(got[:, 0], axis=0)
            return [sums[k] for k in range(len(values))]

        def sum_all(values):
            tile = lanes(values, 8, cols)
            got = a2a(jnp.broadcast_to(tile[None], (2 * n_z, 8, cols)), CZ)
            got = a2a(jnp.broadcast_to(jnp.sum(got, axis=0)[None], (n_xy, 8, cols)), XY)
            sums = jnp.sum(got[:, 0], axis=0)
            return [sums[k] for k in range(len(values))]

        hu_b = apply_ham(u_a)
        hu_a, (theta,) = gather(hu_b, [dot_b(u_b, hu_b)])
        for step in range(ITERS):
            corr_a = (hu_a - theta * u_a) / (1.0 + jnp.abs(diag_a - theta))
            corr_b = (hu_b - theta * u_b) / (1.0 + jnp.abs(diag_b - theta))
            project, size_corr, size_u = sum_cz(
                [dot_b(u_a, corr_a), dot_b(corr_a, corr_a), dot_b(u_a, u_a)]
            )
            inverse = 1.0 / jnp.sqrt(size_corr - project * project * (2.0 - size_u))
            v_a = (corr_a - project * u_a) * inverse
            v_b = (corr_b - project * u_b) * inverse
            if step == ITERS - 1:
                u_far = lax.ppermute(u_a, "core", swap)
                v_far = lax.ppermute(v_a, "core", swap)
            hv_b = apply_ham(v_a)
            sums = [dot_b(u_b, hv_b), dot_b(v_b, hu_b), dot_b(v_b, hv_b)]
            if step < ITERS - 1:
                hv_a, sums = gather(hv_b, sums)
            else:
                sums = sum_all(sums)
            cross, corner = 0.5 * (sums[0] + sums[1]), sums[2]
            lowest = 0.5 * (theta + corner) - jnp.sqrt((0.5 * (theta - corner)) ** 2 + cross * cross)
            x, y = corner - lowest, -cross
            length = jnp.sqrt(x * x + y * y)
            x, y = x / length, y / length
            theta = x * x * theta + 2.0 * x * y * cross + y * y * corner
            u_a = x * u_a + y * v_a
            if step < ITERS - 1:
                u_b = x * u_b + y * v_b
                hu_a, hu_b = x * hu_a + y * hv_a, x * hu_b + y * hv_b
        far = x * u_far + y * v_far
        out = jnp.stack([jnp.where(core == 0, u_a, far), jnp.where(core == 0, far, u_a)])
        return out, lowest

    return per_device


def solution(mesh):
    n_z = mesh.shape["sec"]
    n_y = n_x = int(round((mesh.shape["term"] // 2) ** 0.5))
    fine = Mesh(mesh.devices.reshape(n_y, n_x, 2, n_z), ("y", "x", "core", "sec"))
    term = ("y", "x", "core")
    in_specs = (
        P(None, None, "sec"),
        P(None, None, "sec"),
        P(),
        P(term, None, None, None),
        P(term, None, None, None),
    )
    out_specs = (P(None, None, "sec"), P())
    return jax.shard_map(
        make(n_y, n_x, n_z), mesh=fine, in_specs=in_specs, out_specs=out_specs, check_vma=False
    )
```

time: 746 us -> 333 us (0.45)
  waiting for transfers between devices: 369 us -> 36.6 us
  blocking collectives: 262 us -> 148 us
  starting transfers between devices: 0.12 us -> 30.6 us
  between operations: 36.5 us -> 25.2 us
  other arithmetic: 28.7 us -> 38.4 us
  matrix products: 22.1 us -> 29.7 us
    psum x3 -> x0, waiting for transfers between devices: 369 us -> none  [apply_ham(): summed = lax.psum(partial_sum, 'term')]
    psum x9 -> x0, blocking collectives: 113 us -> none  [the longest x2 24.3 us: per_device(): orth_sum = lax.psum(local_dot(orth, orth), 'sec')]
    all_to_all x0 -> x5, waiting for transfers between devices: none -> 36.6 us  [a2a(): return lax.all_to_all(array, axes, 0, 0, tiled=True)]
    all_to_all x0 -> x5, starting transfers between devices: none -> 24.6 us  [a2a(): return lax.all_to_all(array, axes, 0, 0, tiled=True)]
    reshape x0 -> x10, local copies, waits for them, and re-layouts: none -> 9.06 us  [the longest x6 7.13 us: apply_ham(): parts = [jnp.dot(env, field, preferred_element_type=jnp.float32).astype(j...]
    all_to_all x6 -> x0, local copies, waits for them, and re-layouts: 7.79 us -> none  [the longest x3 5.97 us: apply_ham(): lax.all_to_all(summed, 'sec', split_axis=2, concat_axis=1, tiled=True)]
    dot_general x6 -> x12, matrix products: 22.1 us -> 29.7 us  [the longest x6 18.3 us: apply_ham(): jnp.dot(env, field, preferred_element_type=jnp.float32).astype(jnp.bfloat16)]
    all_to_all x6 -> x10, blocking collectives: 149 us -> 148 us  [a2a(): return lax.all_to_all(array, axes, 0, 0, tiled=True)]
  transfers between devices with their start and end apart: 3 -> 9, of which waited for: 3 -> 5; matrix products, arithmetic and copies ran while one was open for 0% -> 9% of each run, Pallas kernels for 0% -> 0%
where the time goes in v1:
time: 333 us; the launch traced here: 330 us
  blocking collectives  148 us (44%)
  other arithmetic  38.4 us (12%)
  waiting for transfers between devices  36.6 us (11%)
  starting transfers between devices  30.6 us (9%)
  matrix products  29.7 us (9%)
  between operations  25.2 us (8%)
  local copies, waits for them, and re-layouts  22 us (7%)
    all_to_all x10, blocking collectives, a2a(): return lax.all_to_all(array, axes, 0, 0, tiled=True)  148 us
    all_to_all x5, waiting for transfers between devices, a2a(): return lax.all_to_all(array, axes, 0, 0, tiled=True)  36.6 us
    all_to_all x5, starting transfers between devices, a2a(): return lax.all_to_all(array, axes, 0, 0, tiled=True)  24.6 us
    dot_general x6, matrix products, apply_ham(): jnp.dot(env, field, preferred_element_type=jnp.float32).astype(jnp.bfloat16)  18.3 us
    reduce_sum x7, other arithmetic, dot_b(): return jnp.sum(first * second) * scale  17.3 us
    dot_general x6, matrix products, apply_ham(): lax.dot_general(rows, env, (((1,), (1,)), ((), ())), preferred_element_ty...  11.4 us
    reshape x6, local copies, waits for them, and re-layouts, apply_ham(): parts = [jnp.dot(env, field, preferred_element_type=jnp.float32).astype(j...  7.13 us
  transfers between devices with their start and end apart: 9, of which 5 were waited for; matrix products, arithmetic and copies ran while one was open for 9% of the time, Pallas kernels for 0%

profile of v1, /device:TPU:1, one launch (start us, length us, event | category | flops | bytes accessed | tf_op | source)
XLA Modules:
  0.0 330.3 jit_solution(7756698032270442364)
XLA Ops:
  0.7 3.2 dynamic-slice_bitcast_fusion.1
  3.9 3.2 collective-permute-start
  7.7 1.3 iota_compare_fusion
  9.0 1.3 fusion.65
  10.3 1.3 fusion.38
  16.0 6.4 %all-to-all-start = ((f32[8,24,128]{2,1,0:T(8,128)}), f32[8,24,128]{2,1,0:T(8,128)S(1)}, u32[]{:S(2)}, u32[]{:S(2)}) async-start(f32[8,24,128]{2,1,0:T(8,128)} %maximum_maximum_fusion), calls=%async_computation | async-start | bytes 196608 | tf_op jit(solution)/shard_map/all_to_all | solution.py:40
  22.4 3.1 dynamic-slice_bitcast_fusion
  26.5 3.8 %all-to-all-done = f32[8,24,128]{2,1,0:T(8,128)S(1)} async-done(((f32[8,24,128]{2,1,0:T(8,128)}), f32[8,24,128]{2,1,0:T(8,128)S(1)}, u32[]{:S(2)}, u32[]{:S(2)}) %all-to-all-start) | async-done | bytes 98336 | tf_op jit(solution)/shard_map/all_to_all | solution.py:40
  31.6 3.1 fusion.21
  34.7 1.1 copy.49
  35.9 3.1 convolution_convert_fusion.2
  39.0 1.8 copy.50
  40.8 1.0 pad_maximum_fusion.1
  41.8 18.9 %all_to_all.75 = bf16[8,2,128,128]{2,3,1,0:T(8,128)(2,1)S(1)} all-to-all(bf16[8,2,128,128]{2,3,1,0:T(8,128)(2,1)S(1)} %pad_maximum_fusion.1), channel_id=1, replica_groups=mesh['y'=4,'x'=4,'core'=2,'sec'=8] {'sec'}, dimensions={0} | all-to-all | bytes 1048576 | tf_op jit(solution)/shard_map/all_to_all | solution.py:40
  60.7 2.4 fusion.4
  63.1 1.6 fusion.20
  64.8 6.8 %all-to-all-start.2 = ((f32[16,8,1024]{2,1,0:T(8,128)}), f32[16,8,1024]{2,1,0:T(8,128)}, u32[]{:S(2)}, u32[]{:S(2)}) async-start(f32[16,8,1024]{2,1,0:T(8,128)} %fusion.20), calls=%async_computation.2 | async-start | bytes 1048576 | tf_op jit(solution)/shard_map/all_to_all | solution.py:40
  72.3 8.4 %all-to-all-done.2 = f32[16,8,1024]{2,1,0:T(8,128)} async-done(((f32[16,8,1024]{2,1,0:T(8,128)}), f32[16,8,1024]{2,1,0:T(8,128)}, u32[]{:S(2)}, u32[]{:S(2)}) %all-to-all-start.2) | async-done | bytes 524320 | tf_op jit(solution)/shard_map/all_to_all | solution.py:40
  80.7 1.1 reduce_sum.246
  81.8 1.3 multiply_reduce_fusion.12
  83.8 13.7 %all_to_all.76 = f32[16,16,128]{2,1,0:T(8,128)S(1)} all-to-all(f32[16,16,128]{2,1,0:T(8,128)S(1)} %bitcast.266), channel_id=1, replica_groups=mesh['y'=4,'x'=4,'core'=2,'sec'=8] {'core','sec'}, dimensions={0} | all-to-all | bytes 262144 | tf_op jit(solution)/shard_map/all_to_all | solution.py:40
  97.6 0.9 broadcast_in_dim.127
  98.4 4.3 %all-to-all-start.4 = ((f32[16,72,128]{2,1,0:T(8,128)}), f32[16,72,128]{2,1,0:T(8,128)}, u32[]{:S(2)}, u32[]{:S(2)}) async-start(f32[16,72,128]{2,1,0:T(8,128)} %broadcast_in_dim.127), calls=%async_computation.4 | async-start | bytes 1179648 | tf_op jit(solution)/shard_map/all_to_all | solution.py:40
  102.7 11.0 %all-to-all-done.4 = f32[16,72,128]{2,1,0:T(8,128)} async-done(((f32[16,72,128]{2,1,0:T(8,128)}), f32[16,72,128]{2,1,0:T(8,128)}, u32[]{:S(2)}, u32[]{:S(2)}) %all-to-all-start.4) | async-done | bytes 589856 | tf_op jit(solution)/shard_map/all_to_all | solution.py:40
  113.8 1.1 slice_bitcast_fusion
  114.9 0.8 copy.53
  115.7 0.9 slice_reduce_fusion.3
  116.6 2.7 multiply_reduce_fusion.4
  120.0 2.8 multiply_reduce_fusion.5
  124.1 12.9 %all_to_all.77 = f32[16,8,128]{2,1,0:T(8,128)S(1)} all-to-all(f32[16,8,128]{2,1,0:T(8,128)S(1)} %broadcast_in_dim.131), channel_id=1, replica_groups=mesh['y'=4,'x'=4,'core'=2,'sec'=8] {'core','sec'}, dimensions={0} | all-to-all | bytes 131072 | tf_op jit(solution)/shard_map/all_to_all | solution.py:40
  140.0 3.7 %convolution_convert_fusion.1 = bf16[1024,128]{1,0:T(8,128)(2,1)} fusion(bf16[1024,1024]{1,0:T(8,128)(2,1)} %collective-permute-done, f32[1024,128]{1,0:T(8,128)} %get-tuple-element.21, f32[]{:T(128)S(6)} %sqrt.22, f32[]{:T(128)} %bitcast.39, f32[1,1024,128]{2,1,0:T(8,128)S(1)} %get-tuple-element.51, f32[]{:T(128)S(6)} %sqrt.21, ...), kind=kOutput, calls=%fused_computation.30 | convolution fusion | flops 269484032 | bytes 3409036 | tf_op jit(solution)/shard_map/dot_general | solution.py:73
  143.8 1.1 copy.56
  144.9 1.8 fusion.41
  146.7 3.0 fusion.24
  149.7 1.8 copy.55
  151.5 1.0 pad_maximum_fusion.2
  152.5 18.5 %all_to_all.78 = bf16[8,2,128,128]{2,3,1,0:T(8,128)(2,1)S(1)} all-to-all(bf16[8,2,128,128]{2,3,1,0:T(8,128)(2,1)S(1)} %pad_maximum_fusion.2), channel_id=1, replica_groups=mesh['y'=4,'x'=4,'core'=2,'sec'=8] {'sec'}, dimensions={0} | all-to-all | bytes 1048576 | tf_op jit(solution)/shard_map/all_to_all | solution.py:40
  171.1 2.4 fusion.2
  173.6 0.8 fusion.19
  174.4 12.6 %all_to_all.79 = f32[16,8,1024]{2,1,0:T(8,128)} all-to-all(f32[16,8,1024]{2,1,0:T(8,128)S(1)} %fusion.19), channel_id=1, replica_groups=mesh['y'=4,'x'=4,'core'=2,'sec'=8] {'y','x'}, dimensions={0} | all-to-all | bytes 1048576 | tf_op jit(solution)/shard_map/all_to_all | solution.py:40
  187.0 1.1 reduce_sum.254
  188.1 2.4 multiply_reduce_fusion.11
  192.5 13.1 %all_to_all.80 = f32[16,16,128]{2,1,0:T(8,128)S(1)} all-to-all(f32[16,16,128]{2,1,0:T(8,128)S(1)} %bitcast.267), channel_id=1, replica_groups=mesh['y'=4,'x'=4,'core'=2,'sec'=8] {'core','sec'}, dimensions={0} | all-to-all | bytes 262144 | tf_op jit(solution)/shard_map/all_to_all | solution.py:40
  205.7 13.6 %all_to_all.81 = f32[16,72,128]{2,1,0:T(8,128)S(1)} all-to-all(f32[16,72,128]{2,1,0:T(8,128)S(1)} %broadcast_in_dim.137), channel_id=1, replica_groups=mesh['y'=4,'x'=4,'core'=2,'sec'=8] {'y','x'}, dimensions={0} | all-to-all | bytes 1179648 | tf_op jit(solution)/shard_map/all_to_all | solution.py:40
  224.6 3.7 %multiply_reduce_fusion.1 = (f32[]{:T(128)}, f32[8,16,8,128]{3,2,1,0:T(8,128)}) fusion(f32[8,16,8,128]{3,2,1,0:T(8,128)S(1)} %bitcast.251, f32[]{:T(128)S(6)} %sqrt.22, f32[8,16,8,128]{3,2,1,0:T(8,128)} %get-tuple-element.20, f32[]{:T(128)} %bitcast.39, f32[]{:T(128)S(6)} %div.41, f32[]{:T(128)S(6)} %sqrt.21, f32[]{:T(128)S(6)} %add.173, f32[]{:T(128)S(6)} %div.40, ...), kind=kLoop, calls=%fused_computation.64 | loop fusion | flops 2621439 | bytes 3150468 | tf_op jit(solution)/shard_map/reduce_sum | solution.py:90
  229.0 1.2 fusion.30
  230.4 2.4 multiply_reduce_fusion.2
  234.1 13.0 %all_to_all.82 = f32[16,8,128]{2,1,0:T(8,128)S(1)} all-to-all(f32[16,8,128]{2,1,0:T(8,128)S(1)} %broadcast_in_dim.141), channel_id=1, replica_groups=mesh['y'=4,'x'=4,'core'=2,'sec'=8] {'core','sec'}, dimensions={0} | all-to-all | bytes 131072 | tf_op jit(solution)/shard_map/all_to_all | solution.py:40
  250.3 2.8 multiply_convert_fusion
  253.2 0.8 subtract_multiply_fusion
  254.0 2.3 convolution_convert_fusion
  256.5 3.0 fusion.27
  259.5 1.1 copy.61
  260.7 18.5 %all_to_all.83 = bf16[8,2,128,128]{2,3,1,0:T(8,128)(2,1)S(1)} all-to-all(bf16[8,2,128,128]{2,3,1,0:T(8,128)(2,1)S(1)} %pad_maximum_fusion.3), channel_id=1, replica_groups=mesh['y'=4,'x'=4,'core'=2,'sec'=8] {'sec'}, dimensions={0} | all-to-all | bytes 1048576 | tf_op jit(solution)/shard_map/all_to_all | solution.py:40
  279.2 2.4 fusion
  281.8 1.6 fusion.18
  283.4 3.6 %all-to-all-start.12 = ((f32[16,8,1024]{2,1,0:T(8,128)}), f32[16,8,1024]{2,1,0:T(8,128)S(1)}, u32[]{:S(2)}, u32[]{:S(2)}) async-start(f32[16,8,1024]{2,1,0:T(8,128)} %fusion.18), calls=%async_computation.12 | async-start | bytes 1048576 | tf_op jit(solution)/shard_map/all_to_all | solution.py:40
  287.0 2.4 collective-permute-start.2
  289.5 6.8 %all-to-all-done.12 = f32[16,8,1024]{2,1,0:T(8,128)S(1)} async-done(((f32[16,8,1024]{2,1,0:T(8,128)}), f32[16,8,1024]{2,1,0:T(8,128)S(1)}, u32[]{:S(2)}, u32[]{:S(2)}) %all-to-all-start.12) | async-done | bytes 524320 | tf_op jit(solution)/shard_map/all_to_all | solution.py:40
  296.4 1.9 multiply_reduce_fusion.8
  300.2 12.9 %all_to_all.84 = f32[16,8,128]{2,1,0:T(8,128)S(1)} all-to-all(f32[16,8,128]{2,1,0:T(8,128)S(1)} %broadcast_in_dim.145), channel_id=1, replica_groups=mesh['y'=4,'x'=4,'core'=2,'sec'=8] {'core','sec'}, dimensions={0} | all-to-all | bytes 131072 | tf_op jit(solution)/shard_map/all_to_all | solution.py:40
  313.8 3.5 %all-to-all-start.14 = ((f32[16,8,128]{2,1,0:T(8,128)}), f32[16,8,128]{2,1,0:T(8,128)S(1)}, u32[]{:S(2)}, u32[]{:S(2)}) async-start(f32[16,8,128]{2,1,0:T(8,128)} %broadcast_in_dim.146), calls=%async_computation.14 | async-start | bytes 131072 | tf_op jit(solution)/shard_map/all_to_all | solution.py:40
  317.3 6.5 %all-to-all-done.14 = f32[16,8,128]{2,1,0:T(8,128)S(1)} async-done(((f32[16,8,128]{2,1,0:T(8,128)}), f32[16,8,128]{2,1,0:T(8,128)S(1)}, u32[]{:S(2)}, u32[]{:S(2)}) %all-to-all-start.14) | async-done | bytes 65568 | tf_op jit(solution)/shard_map/all_to_all | solution.py:40
  328.2 1.0 pad_maximum_fusion
  (139 shorter events, 11.0 us)
Async XLA Ops:
  0.6 6.5 %copy-start.33 = (s32[2,2]{1,0:T(2,128)S(1)}, s32[2,2]{1,0:T(2,128)}, u32[]{:S(2)}) copy-start(s32[2,2]{1,0:T(2,128)} %param.7) | copy-start | bytes 52
  0.6 9.6 %copy-start.8 = (f32[2,1024,128]{2,1,0:T(8,128)S(1)}, f32[2,1024,128]{2,1,0:T(8,128)}, u32[]{:S(2)}) copy-start(f32[2,1024,128]{2,1,0:T(8,128)} %param.5) | copy-start | bytes 3145732
  0.7 14.3 %copy-start.11 = (f32[2,1024,128]{2,1,0:T(8,128)S(1)}, f32[2,1024,128]{2,1,0:T(8,128)}, u32[]{:S(2)}) copy-start(f32[2,1024,128]{2,1,0:T(8,128)} %param.6) | copy-start | bytes 3145732
  3.9 32.0 %collective-permute-start = (bf16[1024,1024]{1,0:T(8,128)(2,1)}, bf16[1024,1024]{1,0:T(8,128)(2,1)}, u32[]{:S(2)}, u32[]{:S(2)}) collective-permute-start(bf16[1024,1024]{1,0:T(8,128)(2,1)} %dynamic-slice_bitcast_fusion.1), channel_id=1, source_target_pairs={{0,8},{8,0},{1,9},{9,1},{2,10},{10,2},{3,11},{11,3},{4,12},{12,4},... | collective-permute-start | bytes 6291464 | tf_op jit(solution)/shard_map/ppermute | solution.py:34
  14.2 21.6 %copy-start.13 = (pred[128]{0:T(512)(128)(4,1)}, pred[128]{0:T(512)(128)(4,1)S(1)}, u32[]{:S(2)}) copy-start(pred[128]{0:T(512)(128)(4,1)S(1)} %fusion.67) | copy-start | bytes 388
  16.0 14.3 %all-to-all-start = ((f32[8,24,128]{2,1,0:T(8,128)}), f32[8,24,128]{2,1,0:T(8,128)S(1)}, u32[]{:S(2)}, u32[]{:S(2)}) async-start(f32[8,24,128]{2,1,0:T(8,128)} %maximum_maximum_fusion), calls=%async_computation | async-start | bytes 196608 | tf_op jit(solution)/shard_map/all_to_all | solution.py:40
  25.5 37.6 %collective-permute-start.1 = (bf16[1024,1024]{1,0:T(8,128)(2,1)}, bf16[1024,1024]{1,0:T(8,128)(2,1)S(1)}, u32[]{:S(2)}, u32[]{:S(2)}) collective-permute-start(bf16[1024,1024]{1,0:T(8,128)(2,1)} %dynamic-slice_bitcast_fusion), channel_id=1, source_target_pairs={{0,8},{8,0},{1,9},{9,1},{2,10},{10,2},{3,11},{11,3},{4,12},{12,4},... | collective-permute-start | bytes 6291464 | tf_op jit(solution)/shard_map/ppermute | solution.py:35
  26.5 12.5 %copy-start.18 = (pred[1024]{0:T(1024)(128)(4,1)}, pred[1024]{0:T(1024)(128)(4,1)S(1)}, u32[]{:S(2)}) copy-start(pred[1024]{0:T(1024)(128)(4,1)S(1)} %iota_compare_fusion.2) | copy-start | bytes 3076
  64.8 15.9 %all-to-all-start.2 = ((f32[16,8,1024]{2,1,0:T(8,128)}), f32[16,8,1024]{2,1,0:T(8,128)}, u32[]{:S(2)}, u32[]{:S(2)}) async-start(f32[16,8,1024]{2,1,0:T(8,128)} %fusion.20), calls=%async_computation.2 | async-start | bytes 1048576 | tf_op jit(solution)/shard_map/all_to_all | solution.py:40
  71.6 43.2 %copy-start.27 = (s32[8]{0:T(128)}, s32[8]{0:T(128)S(1)}, u32[]{:S(2)}) copy-start(s32[8]{0:T(128)S(1)} %iota_multiply_fusion) | copy-start | bytes 100
  72.3 42.6 %copy-start.30 = (pred[8]{0:T(512)(128)(4,1)}, pred[8]{0:T(512)(128)(4,1)S(1)}, u32[]{:S(2)}) copy-start(pred[8]{0:T(512)(128)(4,1)S(1)} %add_compare_fusion.2) | copy-start | bytes 28
  97.5 19.1 %copy-start.14 = (pred[128]{0:T(512)(128)(4,1)S(1)}, pred[128]{0:T(512)(128)(4,1)}, u32[]{:S(2)}) copy-start(pred[128]{0:T(512)(128)(4,1)} %copy-done.13) | copy-start | bytes 388
  98.4 15.4 %all-to-all-start.4 = ((f32[16,72,128]{2,1,0:T(8,128)}), f32[16,72,128]{2,1,0:T(8,128)}, u32[]{:S(2)}, u32[]{:S(2)}) async-start(f32[16,72,128]{2,1,0:T(8,128)} %broadcast_in_dim.127), calls=%async_computation.4 | async-start | bytes 1179648 | tf_op jit(solution)/shard_map/all_to_all | solution.py:40
  102.7 21.4 %copy-start.21 = (pred[128]{0:T(512)(128)(4,1)}, pred[128]{0:T(512)(128)(4,1)S(1)}, u32[]{:S(2)}) copy-start(pred[128]{0:T(512)(128)(4,1)S(1)} %get-tuple-element.56) | copy-start | bytes 388
  102.7 21.4 %copy-start.24 = (pred[128]{0:T(512)(128)(4,1)}, pred[128]{0:T(512)(128)(4,1)S(1)}, u32[]{:S(2)}) copy-start(pred[128]{0:T(512)(128)(4,1)S(1)} %get-tuple-element.57) | copy-start | bytes 388
  102.7 17.3 %copy-start.19 = (pred[1024]{0:T(1024)(128)(4,1)S(1)}, pred[1024]{0:T(1024)(128)(4,1)}, u32[]{:S(2)}) copy-start(pred[1024]{0:T(1024)(128)(4,1)} %copy-done.18) | copy-start | bytes 3076
  116.6 6.2 %copy-start.16 = (f32[128]{0:T(128)}, f32[128]{0:T(128)S(1)}, u32[]{:S(2)}) copy-start(f32[128]{0:T(128)S(1)} %slice_reduce_fusion.3) | copy-start | bytes 1540
  173.5 14.6 %copy-start.17 = (f32[128]{0:T(128)S(1)}, f32[128]{0:T(128)}, u32[]{:S(2)}) copy-start(f32[128]{0:T(128)} %copy-done.16) | copy-start | bytes 1540
  173.5 14.6 %copy-start.28 = (s32[8]{0:T(128)S(1)}, s32[8]{0:T(128)}, u32[]{:S(2)}) copy-start(s32[8]{0:T(128)} %copy-done.27) | copy-start | bytes 100
  173.5 14.6 %copy-start.31 = (pred[8]{0:T(512)(128)(4,1)S(1)}, pred[8]{0:T(512)(128)(4,1)}, u32[]{:S(2)}) copy-start(pred[8]{0:T(512)(128)(4,1)} %copy-done.30) | copy-start | bytes 28
  173.5 18.9 %copy-start.22 = (pred[128]{0:T(512)(128)(4,1)S(1)}, pred[128]{0:T(512)(128)(4,1)}, u32[]{:S(2)}) copy-start(pred[128]{0:T(512)(128)(4,1)} %copy-done.21) | copy-start | bytes 388
  173.5 18.9 %copy-start.25 = (pred[128]{0:T(512)(128)(4,1)S(1)}, pred[128]{0:T(512)(128)(4,1)}, u32[]{:S(2)}) copy-start(pred[128]{0:T(512)(128)(4,1)} %copy-done.24) | copy-start | bytes 388
  174.4 50.2 %copy-start.15 = (pred[128]{0:T(512)(128)(4,1)S(1)}, pred[128]{0:T(512)(128)(4,1)}, u32[]{:S(2)}) copy-start(pred[128]{0:T(512)(128)(4,1)} %copy-done.13) | copy-start | bytes 388
  190.5 37.8 %copy-start.9 = (f32[8,8,128]{2,1,0:T(8,128)}, f32[8,8,128]{2,1,0:T(8,128)S(1)}, u32[]{:S(2)}) copy-start(f32[8,8,128]{2,1,0:T(8,128)S(1)} %get-tuple-element.17) | copy-start | bytes 98308
  219.3 0.8 copy-start.7
  224.6 5.6 %copy-start.20 = (pred[1024]{0:T(1024)(128)(4,1)S(1)}, pred[1024]{0:T(1024)(128)(4,1)}, u32[]{:S(2)}) copy-start(pred[1024]{0:T(1024)(128)(4,1)} %copy-done.18) | copy-start | bytes 3076
  229.0 1.3 copy-start
  229.0 1.4 copy-start.6
  230.4 2.4 copy-start.4
  250.3 2.8 copy-start.1
  250.3 2.8 copy-start.2
  250.3 2.8 copy-start.5
  281.7 5.3 %copy-start.3 = (f32[1024,128]{1,0:T(8,128)S(1)}, f32[1024,128]{1,0:T(8,128)}, u32[]{:S(2)}) copy-start(f32[1024,128]{1,0:T(8,128)} %get-tuple-element.16) | copy-start | bytes 1572868
  281.7 14.7 %copy-start.10 = (f32[8,8,128]{2,1,0:T(8,128)S(1)}, f32[8,8,128]{2,1,0:T(8,128)}, u32[]{:S(2)}) copy-start(f32[8,8,128]{2,1,0:T(8,128)} %copy-done.9) | copy-start | bytes 98308
  281.7 14.7 %copy-start.12 = (f32[8,8,128]{2,1,0:T(8,128)S(1)}, f32[8,8,128]{2,1,0:T(8,128)}, u32[]{:S(2)}) copy-start(f32[8,8,128]{2,1,0:T(8,128)} %get-tuple-element.18) | copy-start | bytes 98308
  281.7 14.7 %copy-start.29 = (s32[8]{0:T(128)S(1)}, s32[8]{0:T(128)}, u32[]{:S(2)}) copy-start(s32[8]{0:T(128)} %copy-done.27) | copy-start | bytes 100
  281.7 14.7 %copy-start.32 = (pred[8]{0:T(512)(128)(4,1)S(1)}, pred[8]{0:T(512)(128)(4,1)}, u32[]{:S(2)}) copy-start(pred[8]{0:T(512)(128)(4,1)} %copy-done.30) | copy-start | bytes 28
  281.7 18.5 %copy-start.23 = (pred[128]{0:T(512)(128)(4,1)S(1)}, pred[128]{0:T(512)(128)(4,1)}, u32[]{:S(2)}) copy-start(pred[128]{0:T(512)(128)(4,1)} %copy-done.21) | copy-start | bytes 388
  281.7 18.5 %copy-start.26 = (pred[128]{0:T(512)(128)(4,1)S(1)}, pred[128]{0:T(512)(128)(4,1)}, u32[]{:S(2)}) copy-start(pred[128]{0:T(512)(128)(4,1)} %copy-done.24) | copy-start | bytes 388
  283.4 12.9 %all-to-all-start.12 = ((f32[16,8,1024]{2,1,0:T(8,128)}), f32[16,8,1024]{2,1,0:T(8,128)S(1)}, u32[]{:S(2)}, u32[]{:S(2)}) async-start(f32[16,8,1024]{2,1,0:T(8,128)} %fusion.18), calls=%async_computation.12 | async-start | bytes 1048576 | tf_op jit(solution)/shard_map/all_to_all | solution.py:40
  287.0 41.0 %collective-permute-start.2 = (f32[1024,128]{1,0:T(8,128)S(1)}, f32[1024,128]{1,0:T(8,128)S(1)}, u32[]{:S(2)}, u32[]{:S(2)}) collective-permute-start(f32[1024,128]{1,0:T(8,128)S(1)} %copy-done.3), channel_id=1, source_target_pairs={{0,8},{8,0},{1,9},{9,1},{2,10},{10,2},{3,11},{11,3},{4,12},{12,4},... | collective-permute-start | bytes 1572872 | tf_op jit(solution)/shard_map/ppermute | solution.py:130
  289.4 38.6 %collective-permute-start.3 = (f32[1024,128]{1,0:T(8,128)S(1)}, f32[1024,128]{1,0:T(8,128)S(1)}, u32[]{:S(2)}, u32[]{:S(2)}) collective-permute-start(f32[1024,128]{1,0:T(8,128)S(1)} %subtract_multiply_fusion), channel_id=1, source_target_pairs={{0,8},{8,0},{1,9},{9,1},{2,10},{10,2},{3,11},{11,3},{4,12},{12,4},... | collective-permute-start | bytes 1572872 | tf_op jit(solution)/shard_map/ppermute | solution.py:131
  313.8 10.0 %all-to-all-start.14 = ((f32[16,8,128]{2,1,0:T(8,128)}), f32[16,8,128]{2,1,0:T(8,128)S(1)}, u32[]{:S(2)}, u32[]{:S(2)}) async-start(f32[16,8,128]{2,1,0:T(8,128)} %broadcast_in_dim.146), calls=%async_computation.14 | async-start | bytes 131072 | tf_op jit(solution)/shard_map/all_to_all | solution.py:40

commit v2 on v0

v2 whole, which is shorter than its diff:
```python
import functools

import jax
import jax.numpy as jnp
from jax import lax
from jax.experimental import pallas as pl
from jax.experimental.pallas import tpu as pltpu
from jax.sharding import Mesh, PartitionSpec as P

ITERS = 2
XY = ("y", "x")
CZ = ("core", "sec")
LANES = 128
PIECE = 256
F32 = jnp.float32
BF16 = jnp.bfloat16
SMEM = pl.BlockSpec(memory_space=pltpu.SMEM)
ANY = pl.BlockSpec(memory_space=pl.ANY)
VMEM = pl.BlockSpec(memory_space=pltpu.VMEM)


def call(kernel, outs, ins, scratch=(), flops=0):
    moved = sum(int(a.size) * a.dtype.itemsize for a, _ in ins)
    return pl.pallas_call(
        kernel,
        out_shape=[jax.ShapeDtypeStruct(s, d) for s, d in outs],
        in_specs=[s for _, s in ins],
        out_specs=[VMEM] * len(outs),
        scratch_shapes=list(scratch),
        compiler_params=pltpu.CompilerParams(vmem_limit_bytes=24 * 2**20),
        cost_estimate=pl.CostEstimate(flops=flops, bytes_accessed=moved, transcendentals=0),
    )(*[a for a, _ in ins])


def fold(product):
    parts = [product[:, k : k + LANES] for k in range(0, product.shape[1], LANES)]
    return jnp.sum(functools.reduce(lambda a, b: a + b, parts), axis=0, keepdims=True)


def tile_of(rows):
    return jnp.concatenate(rows + [jnp.zeros((8 - len(rows), LANES), F32)], axis=0)


def scalars(tile, count, scale):
    sums = jnp.sum(tile, axis=1, keepdims=True) * scale
    return [sums[k : k + 1] for k in range(count)]


def make(n_y, n_x, n_z):
    n_xy = n_y * n_x

    def per_device(psi, diag, block_dims, left_env, right_env):
        sectors, size, cols = psi.shape
        sub = cols // n_xy
        shard_rows = n_z * sub
        scale = 1.0 / (size * size)
        core = lax.axis_index("core")
        swap = [(0, 1), (1, 0)]
        ids = jnp.stack([core, lax.axis_index("sec"), lax.axis_index(XY)]).astype(jnp.int32)
        share, shard = (size, cols), (sub, size)

        def a2a(array, axes):
            return lax.all_to_all(array, axes, 0, 0, tiled=True)

        def share_mask(dims_ref, ids_ref, sector):
            row = lax.broadcasted_iota(jnp.int32, share, 0)
            col = lax.broadcasted_iota(jnp.int32, share, 1) + ids_ref[1] * cols
            return (row < dims_ref[sector, 0]) & (col < dims_ref[sector, 1])

        def start_kernel(ids_ref, dims_ref, psi_ref, diag_ref, out_ref):
            total = jnp.zeros((1, LANES), F32)
            for s in range(sectors):
                own = psi_ref[s]
                total = total + fold(jnp.where(share_mask(dims_ref, ids_ref, s), own * own, 0.0))
            c, first = ids_ref[0], pl.multiple_of(ids_ref[2] * sub, sub)
            dims = (dims_ref[c, 0], dims_ref[c, 1])
            col = lax.broadcasted_iota(jnp.int32, (sub, cols), 1) + ids_ref[1] * cols
            row = lax.broadcasted_iota(jnp.int32, (sub, cols), 0) + first
            for k in range(n_z):
                rows = pl.ds(k * cols + first, sub)
                keep = (row + k * cols < dims[0]) & (col < dims[1])
                out_ref[k, :sub] = jnp.where(keep, psi_ref[c, rows], 0.0)
                out_ref[k, sub : 2 * sub] = diag_ref[c, rows]
                out_ref[k, 2 * sub :] = tile_of([total])

        def left_matmul(ids_ref, env_ref, got_ref, field, left_ref, buf, sems, copies):
            for k, copy in enumerate(copies):
                copy.wait()
                w, i = k % 2, k // 2
                rows = jnp.dot(buf[w, pl.ds(i * PIECE, PIECE)], field, preferred_element_type=F32)
                per = PIECE // cols
                left_ref[i * per : (i + 1) * per, w] = rows.astype(BF16).reshape(per, cols, cols)

        def env_copies(ids_ref, env_ref, got_ref, buf, sems):
            copies = []
            for i in range(size // PIECE):
                rows = pl.ds(i * PIECE, PIECE)
                for w, source in enumerate((env_ref.at[0, ids_ref[0]], got_ref)):
                    copy = pltpu.make_async_copy(source.at[rows], buf.at[w, rows], sems.at[w, i])
                    copy.start()
                    copies.append(copy)
            return copies

        def first_kernel(ids_ref, dims_ref, got_ref, psi_ref, env_ref, env2_ref, u_a_ref, u_b_ref, diag_b_ref, left_ref, buf, sems):
            copies = env_copies(ids_ref, env_ref, env2_ref, buf, sems)
            got = got_ref[...]
            (norm,) = scalars(jnp.sum(got[:, 2 * sub :], axis=0), 1, scale)
            inverse = 1.0 / jnp.sqrt(norm)
            u_a = jnp.where(share_mask(dims_ref, ids_ref, ids_ref[0]), psi_ref[ids_ref[0]], 0.0) * inverse
            u_a_ref[...] = u_a
            for k in range(n_z):
                lanes = slice(k * cols, (k + 1) * cols)
                u_b_ref[:, lanes] = got[k, :sub] * inverse
                diag_b_ref[:, lanes] = got[k, sub : 2 * sub]
            left_matmul(ids_ref, env_ref, env2_ref, u_a.astype(BF16), left_ref, buf, sems, copies)

        def fresh_kernel(ids_ref, got_ref, corr_a_ref, u_a_ref, corr_b_ref, u_b_ref, env_ref, env2_ref, v_a_ref, v_b_ref, left_ref, buf, sems):
            copies = env_copies(ids_ref, env_ref, env2_ref, buf, sems)
            project, size_corr, size_u = scalars(jnp.sum(got_ref[...], axis=0), 3, scale)
            inverse = 1.0 / jnp.sqrt(size_corr - project * project * (2.0 - size_u))
            v_a = (corr_a_ref[...] - project * u_a_ref[...]) * inverse
            v_a_ref[...] = v_a
            v_b_ref[...] = (corr_b_ref[...] - project * u_b_ref[...]) * inverse
            left_matmul(ids_ref, env_ref, env2_ref, v_a.astype(BF16), left_ref, buf, sems, copies)

        def right_kernel(ids_ref, moved_ref, env_ref, got_ref, out_ref, buf, sems):
            copies = env_copies(ids_ref, env_ref, got_ref, buf, sems)
            fields = [
                jnp.concatenate([moved_ref[k, w] for k in range(n_z)], axis=1) for w in range(2)
            ]
            for i in range(size // PIECE):
                rows = pl.ds(i * PIECE, PIECE)
                total = None
                for w in range(2):
                    copies[2 * i + w].wait()
                    part = lax.dot_general(
                        fields[w], buf[w, rows], (((1,), (1,)), ((), ())), preferred_element_type=F32
                    )
                    total = part if total is None else total + part
                out_ref[:, :, rows] = total.reshape(n_xy, sub, PIECE)

        def image_of(ids_ref, dims_ref, got_ref):
            c = ids_ref[0]
            image = jnp.sum(got_ref[...], axis=0)
            row = lax.broadcasted_iota(jnp.int32, shard, 0) + (ids_ref[1] * cols + ids_ref[2] * sub)
            col = lax.broadcasted_iota(jnp.int32, shard, 1)
            return jnp.where((row < dims_ref[c, 0]) & (col < dims_ref[c, 1]), image, 0.0)

        def dots_tile(image, u_b_ref, more):
            rows = [fold(u_b_ref[...] * image)]
            if more:
                rows += [fold(more[0][...] * more[1][...]), fold(more[0][...] * image)]
            return tile_of(rows)

        def image_kernel(ids_ref, dims_ref, got_ref, u_b_ref, *refs):
            *more, image_ref, out_ref = refs
            image = image_of(ids_ref, dims_ref, got_ref)
            image_ref[...] = image
            tile = dots_tile(image, u_b_ref, more)
            for k in range(n_z):
                for c in range(2):
                    out_ref[c * n_z + k, :sub] = image[:, k * cols : (k + 1) * cols]
                    out_ref[c * n_z + k, sub:] = tile

        def last_image_kernel(ids_ref, dims_ref, got_ref, u_b_ref, v_b_ref, hu_b_ref, out_ref):
            image = image_of(ids_ref, dims_ref, got_ref)
            tile = dots_tile(image, u_b_ref, (v_b_ref, hu_b_ref))
            out_ref[...] = jnp.broadcast_to(tile[None], out_ref.shape)

        def spread_kernel(ids_ref, got_ref, out_ref):
            first = ids_ref[0] * n_z
            tile = jnp.sum(got_ref[:, sub:], axis=0)
            for k in range(n_z):
                rows = got_ref[first + k, :sub]
                for j in range(n_xy):
                    out_ref[j, k * sub : (k + 1) * sub] = rows
            for j in range(n_xy):
                out_ref[j, shard_rows:] = tile

        def sums_kernel(got_ref, out_ref):
            tile = jnp.sum(got_ref[...], axis=0)
            out_ref[...] = jnp.broadcast_to(tile[None], out_ref.shape)

        def projected(theta, tile):
            one, two, corner = scalars(tile, 3, scale)
            cross = 0.5 * (one + two)
            half = 0.5 * (theta - corner)
            lowest = 0.5 * (theta + corner) - jnp.sqrt(half * half + cross * cross)
            x, y = corner - lowest, -cross
            length = jnp.sqrt(x * x + y * y)
            x, y = x / length, y / length
            theta = x * x * theta + 2.0 * x * y * cross + y * y * corner
            return x, y, theta, lowest

        def corr_out(theta, hu_a, u_a, diag_a, hu_b, u_b, diag_b, corr_a_ref, corr_b_ref, theta_ref, out_ref):
            corr_a = (hu_a - theta * u_a) / (1.0 + jnp.abs(diag_a - theta))
            corr_a_ref[...] = corr_a
            corr_b_ref[...] = (hu_b - theta * u_b) / (1.0 + jnp.abs(diag_b - theta))
            theta_ref[...] = jnp.broadcast_to(theta, theta_ref.shape)
            tile = tile_of([fold(u_a * corr_a), fold(corr_a * corr_a), fold(u_a * u_a)])
            out_ref[...] = jnp.broadcast_to(tile[None], out_ref.shape)

        def share_of(got_ref):
            got = got_ref[:, :shard_rows].reshape(n_xy, n_z, sub, cols)
            return jnp.transpose(got, (1, 0, 2, 3)).reshape(share)

        def begin_kernel(ids_ref, got_ref, u_a_ref, u_b_ref, hu_b_ref, diag_ref, diag_b_ref, hu_a_ref, corr_a_ref, corr_b_ref, theta_ref, out_ref):
            (theta,) = scalars(jnp.sum(got_ref[:, shard_rows:], axis=0), 1, scale)
            hu_a = share_of(got_ref)
            hu_a_ref[...] = hu_a
            corr_out(theta, hu_a, u_a_ref[...], diag_ref[ids_ref[0]], hu_b_ref[...], u_b_ref[...], diag_b_ref[...], corr_a_ref, corr_b_ref, theta_ref, out_ref)

        def update_kernel(ids_ref, got_ref, old_theta_ref, u_a_ref, v_a_ref, hu_a_ref, u_b_ref, v_b_ref, hu_b_ref, hv_b_ref, diag_ref, diag_b_ref, u_a_out, hu_a_out, u_b_out, hu_b_out, corr_a_ref, corr_b_ref, theta_ref, out_ref):
            tile = jnp.sum(got_ref[:, shard_rows:], axis=0)
            x, y, theta, _ = projected(old_theta_ref[0:1, 0:1], tile)
            u_a = x * u_a_ref[...] + y * v_a_ref[...]
            hu_a = x * hu_a_ref[...] + y * share_of(got_ref)
            u_b = x * u_b_ref[...] + y * v_b_ref[...]
            hu_b = x * hu_b_ref[...] + y * hv_b_ref[...]
            u_a_out[...], hu_a_out[...] = u_a, hu_a
            u_b_out[...], hu_b_out[...] = u_b, hu_b
            corr_out(theta, hu_a, u_a, diag_ref[ids_ref[0]], hu_b, u_b, diag_b_ref[...], corr_a_ref, corr_b_ref, theta_ref, out_ref)

        def last_kernel(ids_ref, got_ref, theta_ref, u_a_ref, v_a_ref, u_far_ref, v_far_ref, out_ref, energy_ref):
            tile = jnp.sum(got_ref[...], axis=0)
            x, y, _, lowest = projected(theta_ref[0:1, 0:1], tile)
            c = ids_ref[0]
            out_ref[c] = x * u_a_ref[...] + y * v_a_ref[...]
            out_ref[1 - c] = x * u_far_ref[...] + y * v_far_ref[...]
            energy_ref[...] = jnp.broadcast_to(lowest, energy_ref.shape)

        def v(*arrays):
            return [(a, VMEM) for a in arrays]

        i_ids, i_dims = (ids, SMEM), (block_dims, SMEM)
        env_scratch = [pltpu.VMEM((2, size, size), BF16), pltpu.SemaphoreType.DMA((2, size // PIECE))]
        left_out = ((n_z, 2, cols, cols), BF16)
        small = ((2 * n_z, 8, cols), F32)
        tile_out = ((8, cols), F32)
        work = 4 * size * size * cols

        (first,) = call(start_kernel, [((n_z, 2 * sub + 8, cols), F32)], [i_ids, i_dims] + v(psi, diag))
        first, left_env, right_env = lax.optimization_barrier((first, left_env, right_env))
        other = lax.dynamic_index_in_dim(left_env[0], 1 - core, 0, keepdims=False)
        left_got = lax.ppermute(other, "core", swap)
        other = lax.dynamic_index_in_dim(right_env[0], 1 - core, 0, keepdims=False)
        right_got = lax.ppermute(other, "core", swap)
        first = a2a(first, "sec")
        i_lefts = [(left_env, ANY), (left_got, ANY)]
        i_rights = [(right_env, ANY), (right_got, ANY)]

        def apply_right(left):
            moved = a2a(left, "sec")
            (partial,) = call(right_kernel, [((n_xy, sub, size), F32)], [i_ids] + v(moved) + i_rights, env_scratch, work)
            return a2a(partial, XY)

        def gather(payload):
            payload = a2a(payload, CZ)
            (payload,) = call(spread_kernel, [((n_xy, shard_rows + 8, cols), F32)], [i_ids] + v(payload))
            return a2a(payload, XY)

        payload_out = ((2 * n_z, sub + 8, cols), F32)
        u_a, u_b, diag_b, left = call(
            first_kernel, [(share, F32), (shard, F32), (shard, F32), left_out],
            [i_ids, i_dims] + v(first, psi) + i_lefts, env_scratch, work,
        )
        got = apply_right(left)
        hu_b, payload = call(image_kernel, [(shard, F32), payload_out], [i_ids, i_dims] + v(got, u_b))
        got = gather(payload)
        hu_a, corr_a, corr_b, theta, sums = call(
            begin_kernel, [(share, F32), (share, F32), (shard, F32), tile_out, small],
            [i_ids] + v(got, u_a, u_b, hu_b, diag, diag_b),
        )
        for step in range(ITERS):
            sums = a2a(sums, CZ)
            v_a, v_b, left = call(
                fresh_kernel, [(share, F32), (shard, F32), left_out],
                [i_ids] + v(sums, corr_a, u_a, corr_b, u_b) + i_lefts, env_scratch, work,
            )
            got = apply_right(left)
            if step == ITERS - 1:
                break
            hv_b, payload = call(
                image_kernel, [(shard, F32), payload_out], [i_ids, i_dims] + v(got, u_b, v_b, hu_b)
            )
            got = gather(payload)
            u_a, hu_a, u_b, hu_b, corr_a, corr_b, theta, sums = call(
                update_kernel,
                [(share, F32), (share, F32), (shard, F32), (shard, F32), (share, F32), (shard, F32), tile_out, small],
                [i_ids] + v(got, theta, u_a, v_a, hu_a, u_b, v_b, hu_b, hv_b, diag, diag_b),
            )
        u_far = lax.ppermute(u_a, "core", swap)
        v_far = lax.ppermute(v_a, "core", swap)
        (sums,) = call(last_image_kernel, [small], [i_ids, i_dims] + v(got, u_b, v_b, hu_b))
        sums = a2a(sums, CZ)
        (sums,) = call(sums_kernel, [((n_xy, 8, cols), F32)], v(sums))
        sums = a2a(sums, XY)
        out, energy = call(
            last_kernel, [(psi.shape, F32), tile_out], [i_ids] + v(sums, theta, u_a, v_a, u_far, v_far)
        )
        return out, energy[0, 0]

    return per_device


def solution(mesh):
    n_z = mesh.shape["sec"]
    n_y = n_x = int(round((mesh.shape["term"] // 2) ** 0.5))
    fine = Mesh(mesh.devices.reshape(n_y, n_x, 2, n_z), ("y", "x", "core", "sec"))
    term = ("y", "x", "core")
    in_specs = (
        P(None, None, "sec"),
        P(None, None, "sec"),
        P(),
        P(term, None, None, None),
        P(term, None, None, None),
    )
    out_specs = (P(None, None, "sec"), P())
    return jax.shard_map(
        make(n_y, n_x, n_z), mesh=fine, in_specs=in_specs, out_specs=out_specs, check_vma=False
    )
```

time: 746 us -> 265 us (0.36)
  waiting for transfers between devices: 369 us -> 29.7 us
  blocking collectives: 262 us -> 172 us
  between operations: 36.5 us -> 0.86 us
  Pallas kernels: 0 us -> 32.1 us
  other arithmetic: 28.7 us -> 0.08 us
  matrix products: 22.1 us -> 0 us
  starting transfers between devices: 0.12 us -> 17.3 us
  local copies, waits for them, and re-layouts: 22.2 us -> 12.1 us
    psum x3 -> x0, waiting for transfers between devices: 369 us -> none  [apply_ham(): summed = lax.psum(partial_sum, 'term')]
    psum x9 -> x0, blocking collectives: 113 us -> none  [the longest x2 24.3 us: per_device(): orth_sum = lax.psum(local_dot(orth, orth), 'sec')]
    pallas_call x0 -> x16, Pallas kernels: none -> 32.1 us  [call(): pl.pallas_call(kernel, out_shape=[jax.ShapeDtypeStruct(s, d) for s, d in...]
    all_to_all x0 -> x3, waiting for transfers between devices: none -> 29.7 us  [a2a(): return lax.all_to_all(array, axes, 0, 0, tiled=True)]
    all_to_all x6 -> x12, blocking collectives: 149 us -> 172 us  [a2a(): return lax.all_to_all(array, axes, 0, 0, tiled=True)]
    reduce_sum x9 -> x0, other arithmetic: 23.1 us -> none  [local_dot(): return jnp.sum(first * second) * scale]
    dot_general x6 -> x0, matrix products: 22.1 us -> none  [the longest x3 14.3 us: apply_ham(): jnp.einsum('wsic,wsjc->sij', moved, right_env, preferred_element_type=jnp...]
    all_to_all x0 -> x3, starting transfers between devices: none -> 10.7 us  [a2a(): return lax.all_to_all(array, axes, 0, 0, tiled=True)]
  transfers between devices with their start and end apart: 3 -> 7, of which waited for: 3 -> 3; matrix products, arithmetic and copies ran while one was open for 0% -> 1% of each run, Pallas kernels for 0% -> 2%
where the time goes in v2:
time: 265 us; the launch traced here: 264 us
  blocking collectives  172 us (65%)
  Pallas kernels  32.1 us (12%)
  waiting for transfers between devices  29.7 us (11%)
  starting transfers between devices  17.3 us (7%)
  local copies, waits for them, and re-layouts  12.1 us (5%)
    all_to_all x12, blocking collectives, a2a(): return lax.all_to_all(array, axes, 0, 0, tiled=True)  172 us
    pallas_call x16, Pallas kernels, call(): pl.pallas_call(kernel, out_shape=[jax.ShapeDtypeStruct(s, d) for s, d in...  32.1 us
    all_to_all x3, waiting for transfers between devices, a2a(): return lax.all_to_all(array, axes, 0, 0, tiled=True)  29.7 us
    all_to_all x3, starting transfers between devices, a2a(): return lax.all_to_all(array, axes, 0, 0, tiled=True)  10.7 us
    unnamed x32, local copies, waits for them, and re-layouts  8.15 us
  transfers between devices with their start and end apart: 7, of which 3 were waited for; matrix products, arithmetic and copies ran while one was open for 1% of the time, Pallas kernels for 2%

profile of v2, /device:TPU:1, one launch (start us, length us, event | category | flops | bytes accessed | tf_op | source)
XLA Modules:
  0.0 264.0 jit_solution(12625170113796161661)
XLA Ops:
  0.6 0.1 pad_add_fusion.ids_ref
  0.7 1.2 copy-done.7
  1.9 1.2 copy-done.9
  3.2 0.7 copy-done.14
  3.8 0.9 shard_map.68
  4.7 1.9 dynamic-slice_bitcast_fusion.1
  6.6 0.0 copy-start
  6.7 0.0 copy-start.15
  6.7 3.3 %collective-permute-start = (bf16[1024,1024]{1,0:T(8,128)(2,1)S(1)}, bf16[1024,1024]{1,0:T(8,128)(2,1)S(1)}, u32[]{:S(2)}, u32[]{:S(2)}) collective-permute-start(bf16[1024,1024]{1,0:T(8,128)(2,1)S(1)} %dynamic-slice_bitcast_fusion.1), channel_id=1, source_target_pairs={{0,8},{8,0},{1,9},{9,1},{2,10},{10,2},{3,11},{11,3},{4,12},{12,4},... | collective-permute-start | bytes 6291464 | tf_op jit(solution)/shard_map/ppermute | solution.py:245
  10.0 0.0 copy-done.2
  10.0 1.5 dynamic-slice_bitcast_fusion
  11.5 0.8 collective-permute-start.1
  12.3 14.1 %all_to_all.75.got_ref = f32[8,24,128]{2,1,0:T(8,128)S(1)} all-to-all(f32[8,24,128]{2,1,0:T(8,128)S(1)} %shard_map.68), channel_id=1, replica_groups=mesh['y'=4,'x'=4,'core'=2,'sec'=8] {'sec'}, dimensions={0} | all-to-all | bytes 196608 | tf_op jit(solution)/shard_map/all_to_all | solution.py:63
  26.4 0.0 collective-permute-done.env2_ref
  26.4 0.0 copy-done
  26.4 0.0 copy-done.15
  26.4 0.0 copy-start.10
  26.4 1.2 copy-done.10
  27.6 3.4 %shard_map.69 = (f32[1024,128]{1,0:T(8,128)S(1)}, f32[8,1024]{1,0:T(8,128)S(1)}, f32[8,1024]{1,0:T(8,128)S(1)}, bf16[8,2,128,128]{3,2,1,0:T(8,128)(2,1)S(1)}) custom-call(s32[3]{0:T(128)S(1)} %pad_add_fusion.ids_ref, s32[2,2]{1,0:T(2,128)S(1)} %copy-done.15, f32[8,24,128]{2,1,0:T(8,128)S(1)} %all_to_all.75.got_ref, f32[2,1024,128]{2,1,0:T(8,128)S(1)} %copy-done.10, ...), custom_call_target="tpu_custom_call" | custom-call | flops 536870912 | bytes 7438364 | tf_op jit(solution)/shard_map/pallas_call | solution.py:24
  31.0 0.0 copy-done.5
  31.0 0.0 copy-start.13
  31.1 0.8 copy-done.13
  31.8 3.5 %all-to-all-start.1 = ((bf16[8,2,128,128]{3,2,1,0:T(8,128)(2,1)}), bf16[8,2,128,128]{3,2,1,0:T(8,128)(2,1)S(1)}, u32[]{:S(2)}, u32[]{:S(2)}) async-start(bf16[8,2,128,128]{3,2,1,0:T(8,128)(2,1)} %copy-done.13), calls=%async_computation.1 | async-start | bytes 1048576 | tf_op jit(solution)/shard_map/all_to_all | solution.py:63
  35.3 0.0 collective-permute-done.1.got_ref
  35.3 16.4 %all-to-all-done.1.moved_ref = bf16[8,2,128,128]{3,2,1,0:T(8,128)(2,1)S(1)} async-done(((bf16[8,2,128,128]{3,2,1,0:T(8,128)(2,1)}), bf16[8,2,128,128]{3,2,1,0:T(8,128)(2,1)S(1)}, u32[]{:S(2)}, u32[]{:S(2)}) %all-to-all-start.1) | async-done | bytes 524320 | tf_op jit(solution)/shard_map/all_to_all | solution.py:63
  51.7 2.2 copy-done.3
  53.9 3.9 %shard_map.70 = f32[16,8,1024]{2,1,0:T(8,128)S(1)} custom-call(s32[3]{0:T(128)S(1)} %pad_add_fusion.ids_ref, bf16[8,2,128,128]{3,2,1,0:T(8,128)(2,1)S(1)} %all-to-all-done.1.moved_ref, bf16[1,2,1024,1024]{3,2,1,0:T(8,128)(2,1)S(1)} %copy-done.3, bf16[1024,1024]{1,0:T(8,128)(2,1)S(1)} %collective-permute-done.1.got_ref), custom_call_target="tpu_custom_call" | custom-call | flops 536870912 | bytes 6815756 | tf_op jit(solution)/shard_map/pallas_call | solution.py:24
  57.8 0.0 copy-start.8
  57.9 16.1 %all_to_all.76.got_ref = f32[16,8,1024]{2,1,0:T(8,128)S(1)} all-to-all(f32[16,8,1024]{2,1,0:T(8,128)S(1)} %shard_map.70), channel_id=1, replica_groups=mesh['y'=4,'x'=4,'core'=2,'sec'=8] {'y','x'}, dimensions={0} | all-to-all | bytes 1048576 | tf_op jit(solution)/shard_map/all_to_all | solution.py:63
  74.0 0.6 shard_map.71
  74.6 12.9 %all_to_all.77.got_ref = f32[16,16,128]{2,1,0:T(8,128)S(1)} all-to-all(f32[16,16,128]{2,1,0:T(8,128)S(1)} %get-tuple-element.38), channel_id=1, replica_groups=mesh['y'=4,'x'=4,'core'=2,'sec'=8] {'core','sec'}, dimensions={0} | all-to-all | bytes 262144 | tf_op jit(solution)/shard_map/all_to_all | solution.py:63
  87.5 0.6 shard_map.72
  88.1 13.8 %all_to_all.78.got_ref = f32[16,72,128]{2,1,0:T(8,128)S(1)} all-to-all(f32[16,72,128]{2,1,0:T(8,128)S(1)} %shard_map.72), channel_id=1, replica_groups=mesh['y'=4,'x'=4,'core'=2,'sec'=8] {'y','x'}, dimensions={0} | all-to-all | bytes 1179648 | tf_op jit(solution)/shard_map/all_to_all | solution.py:63
  101.9 0.0 copy-done.8
  101.9 1.0 shard_map.73
  102.9 12.9 %all_to_all.79.got_ref = f32[16,8,128]{2,1,0:T(8,128)S(1)} all-to-all(f32[16,8,128]{2,1,0:T(8,128)S(1)} %get-tuple-element.42), channel_id=1, replica_groups=mesh['y'=4,'x'=4,'core'=2,'sec'=8] {'core','sec'}, dimensions={0} | all-to-all | bytes 131072 | tf_op jit(solution)/shard_map/all_to_all | solution.py:63
  115.8 3.5 %shard_map.74 = (f32[1024,128]{1,0:T(8,128)S(1)}, f32[8,1024]{1,0:T(8,128)S(1)}, bf16[8,2,128,128]{3,2,1,0:T(8,128)(2,1)S(1)}) custom-call(s32[3]{0:T(128)S(1)} %pad_add_fusion.ids_ref, f32[16,8,128]{2,1,0:T(8,128)S(1)} %all_to_all.79.got_ref, f32[1024,128]{1,0:T(8,128)S(1)} %get-tuple-element.43.corr_a_ref, f32[1024,128]{1,0:T(8,128)S(1)} %get-tuple-element.39.u_a_ref, ...), custom_call_target="tpu_custom_call" | custom-call | flops 536870912 | bytes 7471116 | tf_op jit(solution)/shard_map/pallas_call | solution.py:24
  119.3 18.5 %all_to_all.80.moved_ref = bf16[8,2,128,128]{3,2,1,0:T(8,128)(2,1)S(1)} all-to-all(bf16[8,2,128,128]{3,2,1,0:T(8,128)(2,1)S(1)} %get-tuple-element.45), channel_id=1, replica_groups=mesh['y'=4,'x'=4,'core'=2,'sec'=8] {'sec'}, dimensions={0} | all-to-all | bytes 1048576 | tf_op jit(solution)/shard_map/all_to_all | solution.py:63
  137.8 3.9 %shard_map.75 = f32[16,8,1024]{2,1,0:T(8,128)S(1)} custom-call(s32[3]{0:T(128)S(1)} %pad_add_fusion.ids_ref, bf16[8,2,128,128]{3,2,1,0:T(8,128)(2,1)S(1)} %all_to_all.80.moved_ref, bf16[1,2,1024,1024]{3,2,1,0:T(8,128)(2,1)S(1)} %copy-done.4, bf16[1024,1024]{1,0:T(8,128)(2,1)S(1)} %collective-permute-done.1.got_ref), custom_call_target="tpu_custom_call" | custom-call | flops 536870912 | bytes 6815756 | tf_op jit(solution)/shard_map/pallas_call | solution.py:24
  141.8 12.1 %all_to_all.81.got_ref = f32[16,8,1024]{2,1,0:T(8,128)S(1)} all-to-all(f32[16,8,1024]{2,1,0:T(8,128)S(1)} %shard_map.75), channel_id=1, replica_groups=mesh['y'=4,'x'=4,'core'=2,'sec'=8] {'y','x'}, dimensions={0} | all-to-all | bytes 1048576 | tf_op jit(solution)/shard_map/all_to_all | solution.py:63
  153.9 0.6 shard_map.76
  154.5 13.2 %all_to_all.82.got_ref = f32[16,16,128]{2,1,0:T(8,128)S(1)} all-to-all(f32[16,16,128]{2,1,0:T(8,128)S(1)} %get-tuple-element.47), channel_id=1, replica_groups=mesh['y'=4,'x'=4,'core'=2,'sec'=8] {'core','sec'}, dimensions={0} | all-to-all | bytes 262144 | tf_op jit(solution)/shard_map/all_to_all | solution.py:63
  167.7 0.6 shard_map.77
  168.3 13.8 %all_to_all.83.got_ref = f32[16,72,128]{2,1,0:T(8,128)S(1)} all-to-all(f32[16,72,128]{2,1,0:T(8,128)S(1)} %shard_map.77), channel_id=1, replica_groups=mesh['y'=4,'x'=4,'core'=2,'sec'=8] {'y','x'}, dimensions={0} | all-to-all | bytes 1179648 | tf_op jit(solution)/shard_map/all_to_all | solution.py:63
  182.1 1.8 shard_map.78
  183.9 12.9 %all_to_all.84.got_ref = f32[16,8,128]{2,1,0:T(8,128)S(1)} all-to-all(f32[16,8,128]{2,1,0:T(8,128)S(1)} %get-tuple-element.52), channel_id=1, replica_groups=mesh['y'=4,'x'=4,'core'=2,'sec'=8] {'core','sec'}, dimensions={0} | all-to-all | bytes 131072 | tf_op jit(solution)/shard_map/all_to_all | solution.py:63
  196.8 3.4 %shard_map.79 = (f32[1024,128]{1,0:T(8,128)S(1)}, f32[8,1024]{1,0:T(8,128)S(1)}, bf16[8,2,128,128]{3,2,1,0:T(8,128)(2,1)S(1)}) custom-call(s32[3]{0:T(128)S(1)} %pad_add_fusion.ids_ref, f32[16,8,128]{2,1,0:T(8,128)S(1)} %all_to_all.84.got_ref, f32[1024,128]{1,0:T(8,128)S(1)} %get-tuple-element.53.corr_a_ref, f32[1024,128]{1,0:T(8,128)S(1)} %get-tuple-element.54.u_a_ref, ...), custom_call_target="tpu_custom_call" | custom-call | flops 536870912 | bytes 7471116 | tf_op jit(solution)/shard_map/pallas_call | solution.py:24
  200.3 0.8 copy-done.11
  201.1 18.5 %all_to_all.85.moved_ref = bf16[8,2,128,128]{3,2,1,0:T(8,128)(2,1)S(1)} all-to-all(bf16[8,2,128,128]{3,2,1,0:T(8,128)(2,1)S(1)} %get-tuple-element.57), channel_id=1, replica_groups=mesh['y'=4,'x'=4,'core'=2,'sec'=8] {'sec'}, dimensions={0} | all-to-all | bytes 1048576 | tf_op jit(solution)/shard_map/all_to_all | solution.py:63
  219.6 4.7 %shard_map.80 = f32[16,8,1024]{2,1,0:T(8,128)} custom-call(s32[3]{0:T(128)S(1)} %pad_add_fusion.ids_ref, bf16[8,2,128,128]{3,2,1,0:T(8,128)(2,1)S(1)} %all_to_all.85.moved_ref, bf16[1,2,1024,1024]{3,2,1,0:T(8,128)(2,1)S(1)} %copy-done.4, bf16[1024,1024]{1,0:T(8,128)(2,1)S(1)} %collective-permute-done.1.got_ref), custom_call_target="tpu_custom_call" | custom-call | flops 536870912 | bytes 6815756 | tf_op jit(solution)/shard_map/pallas_call | solution.py:24
  224.4 0.0 copy-start.12
  224.4 3.7 %all-to-all-start.12 = ((f32[16,8,1024]{2,1,0:T(8,128)}), f32[16,8,1024]{2,1,0:T(8,128)S(1)}, u32[]{:S(2)}, u32[]{:S(2)}) async-start(f32[16,8,1024]{2,1,0:T(8,128)} %shard_map.80), calls=%async_computation.12 | async-start | bytes 1048576 | tf_op jit(solution)/shard_map/all_to_all | solution.py:63
  228.1 2.4 collective-permute-start.2
  230.5 0.1 collective-permute-start.3
  230.6 6.8 %all-to-all-done.12.got_ref = f32[16,8,1024]{2,1,0:T(8,128)S(1)} async-done(((f32[16,8,1024]{2,1,0:T(8,128)}), f32[16,8,1024]{2,1,0:T(8,128)S(1)}, u32[]{:S(2)}, u32[]{:S(2)}) %all-to-all-start.12) | async-done | bytes 524320 | tf_op jit(solution)/shard_map/all_to_all | solution.py:63
  237.4 0.6 shard_map.81
  238.0 12.9 %all_to_all.86.got_ref = f32[16,8,128]{2,1,0:T(8,128)S(1)} all-to-all(f32[16,8,128]{2,1,0:T(8,128)S(1)} %shard_map.81), channel_id=1, replica_groups=mesh['y'=4,'x'=4,'core'=2,'sec'=8] {'core','sec'}, dimensions={0} | all-to-all | bytes 131072 | tf_op jit(solution)/shard_map/all_to_all | solution.py:63
  250.9 0.6 shard_map.82
  251.6 3.5 %all-to-all-start.14 = ((f32[16,8,128]{2,1,0:T(8,128)}), f32[16,8,128]{2,1,0:T(8,128)S(1)}, u32[]{:S(2)}, u32[]{:S(2)}) async-start(f32[16,8,128]{2,1,0:T(8,128)} %shard_map.82), calls=%async_computation.14 | async-start | bytes 131072 | tf_op jit(solution)/shard_map/all_to_all | solution.py:63
  255.1 0.0 collective-permute-done.2.u_far_ref
  255.1 0.0 collective-permute-done.3.v_far_ref
  255.1 6.5 %all-to-all-done.14.got_ref = f32[16,8,128]{2,1,0:T(8,128)S(1)} async-done(((f32[16,8,128]{2,1,0:T(8,128)}), f32[16,8,128]{2,1,0:T(8,128)S(1)}, u32[]{:S(2)}, u32[]{:S(2)}) %all-to-all-start.14) | async-done | bytes 65568 | tf_op jit(solution)/shard_map/all_to_all | solution.py:63
  261.6 1.9 shard_map.83
  263.5 0.5 slice.3
  (14 shorter events, 0.0 us)
Async XLA Ops:
  0.7 1.2 copy-start.7
  1.9 1.2 copy-start.9
  3.2 0.7 copy-start.14
  4.7 5.3 %copy-start.2 = (bf16[1,2,1024,1024]{3,2,1,0:T(8,128)(2,1)S(1)}, bf16[1,2,1024,1024]{3,2,1,0:T(8,128)(2,1)}, u32[]{:S(2)}) copy-start(bf16[1,2,1024,1024]{3,2,1,0:T(8,128)(2,1)} %env_ref.5) | copy-start | bytes 12582916
  6.6 19.8 %copy-start = (bf16[1,2,1024,1024]{3,2,1,0:T(8,128)(2,1)S(1)}, bf16[1,2,1024,1024]{3,2,1,0:T(8,128)(2,1)}, u32[]{:S(2)}) copy-start(bf16[1,2,1024,1024]{3,2,1,0:T(8,128)(2,1)} %env_ref.4) | copy-start | bytes 12582916
  6.7 19.7 %copy-start.15 = (s32[2,2]{1,0:T(2,128)S(1)}, s32[2,2]{1,0:T(2,128)}, u32[]{:S(2)}) copy-start(s32[2,2]{1,0:T(2,128)} %dims_ref.9) | copy-start | bytes 52
  6.7 19.7 %collective-permute-start = (bf16[1024,1024]{1,0:T(8,128)(2,1)S(1)}, bf16[1024,1024]{1,0:T(8,128)(2,1)S(1)}, u32[]{:S(2)}, u32[]{:S(2)}) collective-permute-start(bf16[1024,1024]{1,0:T(8,128)(2,1)S(1)} %dynamic-slice_bitcast_fusion.1), channel_id=1, source_target_pairs={{0,8},{8,0},{1,9},{9,1},{2,10},{10,2},{3,11},{11,3},{4,12},{12,4},... | collective-permute-start | bytes 6291464 | tf_op jit(solution)/shard_map/ppermute | solution.py:245
  11.5 23.8 %collective-permute-start.1 = (bf16[1024,1024]{1,0:T(8,128)(2,1)}, bf16[1024,1024]{1,0:T(8,128)(2,1)S(1)}, u32[]{:S(2)}, u32[]{:S(2)}) collective-permute-start(bf16[1024,1024]{1,0:T(8,128)(2,1)} %dynamic-slice_bitcast_fusion), channel_id=1, source_target_pairs={{0,8},{8,0},{1,9},{9,1},{2,10},{10,2},{3,11},{11,3},{4,12},{12,4},... | collective-permute-start | bytes 6291464 | tf_op jit(solution)/shard_map/ppermute | solution.py:247
  26.4 1.2 copy-start.10
  27.6 3.4 %copy-start.5 = (bf16[1024,1024]{1,0:T(8,128)(2,1)}, bf16[1024,1024]{1,0:T(8,128)(2,1)S(1)}, u32[]{:S(2)}) copy-start(bf16[1024,1024]{1,0:T(8,128)(2,1)S(1)} %collective-permute-done.env2_ref) | copy-start | bytes 6291460
  31.0 0.8 copy-start.13
  31.8 19.9 %all-to-all-start.1 = ((bf16[8,2,128,128]{3,2,1,0:T(8,128)(2,1)}), bf16[8,2,128,128]{3,2,1,0:T(8,128)(2,1)S(1)}, u32[]{:S(2)}, u32[]{:S(2)}) async-start(bf16[8,2,128,128]{3,2,1,0:T(8,128)(2,1)} %copy-done.13), calls=%async_computation.1 | async-start | bytes 1048576 | tf_op jit(solution)/shard_map/all_to_all | solution.py:63
  51.7 2.2 copy-start.3
  53.9 61.9 %copy-start.6 = (bf16[1024,1024]{1,0:T(8,128)(2,1)S(1)}, bf16[1024,1024]{1,0:T(8,128)(2,1)}, u32[]{:S(2)}) copy-start(bf16[1024,1024]{1,0:T(8,128)(2,1)} %copy-done.5) | copy-start | bytes 6291460
  57.8 44.0 %copy-start.8 = (f32[2,1024,128]{2,1,0:T(8,128)S(1)}, f32[2,1024,128]{2,1,0:T(8,128)}, u32[]{:S(2)}) copy-start(f32[2,1024,128]{2,1,0:T(8,128)} %diag_ref.5) | copy-start | bytes 3145732
  87.5 28.3 %copy-start.1 = (bf16[1,2,1024,1024]{3,2,1,0:T(8,128)(2,1)S(1)}, bf16[1,2,1024,1024]{3,2,1,0:T(8,128)(2,1)}, u32[]{:S(2)}) copy-start(bf16[1,2,1024,1024]{3,2,1,0:T(8,128)(2,1)} %env_ref.4) | copy-start | bytes 12582916
  115.8 22.0 %copy-start.4 = (bf16[1,2,1024,1024]{3,2,1,0:T(8,128)(2,1)S(1)}, bf16[1,2,1024,1024]{3,2,1,0:T(8,128)(2,1)}, u32[]{:S(2)}) copy-start(bf16[1,2,1024,1024]{3,2,1,0:T(8,128)(2,1)} %env_ref.5) | copy-start | bytes 12582916
  200.3 0.8 copy-start.11
  224.4 37.3 %copy-start.12 = (f32[1024,128]{1,0:T(8,128)S(1)}, f32[1024,128]{1,0:T(8,128)}, u32[]{:S(2)}) copy-start(f32[1024,128]{1,0:T(8,128)} %copy-done.11) | copy-start | bytes 1572868
  224.4 13.1 %all-to-all-start.12 = ((f32[16,8,1024]{2,1,0:T(8,128)}), f32[16,8,1024]{2,1,0:T(8,128)S(1)}, u32[]{:S(2)}, u32[]{:S(2)}) async-start(f32[16,8,1024]{2,1,0:T(8,128)} %shard_map.80), calls=%async_computation.12 | async-start | bytes 1048576 | tf_op jit(solution)/shard_map/all_to_all | solution.py:63
  228.1 27.0 %collective-permute-start.2 = (f32[1024,128]{1,0:T(8,128)S(1)}, f32[1024,128]{1,0:T(8,128)S(1)}, u32[]{:S(2)}, u32[]{:S(2)}) collective-permute-start(f32[1024,128]{1,0:T(8,128)S(1)} %get-tuple-element.54.u_a_ref), channel_id=1, source_target_pairs={{0,8},{8,0},{1,9},{9,1},{2,10},{10,2},{3,11},{11,3},{4,12},{12,4},... | collective-permute-start | bytes 1572872 | tf_op jit(solution)/shard_map/ppermute | solution.py:292
  230.5 24.6 %collective-permute-start.3 = (f32[1024,128]{1,0:T(8,128)}, f32[1024,128]{1,0:T(8,128)S(1)}, u32[]{:S(2)}, u32[]{:S(2)}) collective-permute-start(f32[1024,128]{1,0:T(8,128)} %copy-done.11), channel_id=1, source_target_pairs={{0,8},{8,0},{1,9},{9,1},{2,10},{10,2},{3,11},{11,3},{4,12},{12,4},... | collective-permute-start | bytes 1572872 | tf_op jit(solution)/shard_map/ppermute | solution.py:293
  251.6 10.0 %all-to-all-start.14 = ((f32[16,8,128]{2,1,0:T(8,128)}), f32[16,8,128]{2,1,0:T(8,128)S(1)}, u32[]{:S(2)}, u32[]{:S(2)}) async-start(f32[16,8,128]{2,1,0:T(8,128)} %shard_map.82), calls=%async_computation.14 | async-start | bytes 131072 | tf_op jit(solution)/shard_map/all_to_all | solution.py:63

commit v3 on v2

v3 whole, which is shorter than its diff:
```python
import functools

import jax
import jax.numpy as jnp
from jax import lax
from jax.experimental import pallas as pl
from jax.experimental.pallas import tpu as pltpu
from jax.sharding import Mesh, PartitionSpec as P

ITERS = 2
XY = ("y", "x")
CZ = ("core", "sec")
ALL = ("y", "x", "core", "sec")
LANES = 128
PIECE = 256
F32 = jnp.float32
BF16 = jnp.bfloat16
SMEM = pl.BlockSpec(memory_space=pltpu.SMEM)
HBM = pl.BlockSpec(memory_space=pltpu.HBM)
VMEM = pl.BlockSpec(memory_space=pltpu.VMEM)


def call(kernel, outs, ins, scratch=(), flops=0):
    moved = sum(int(a.size) * a.dtype.itemsize for a, _ in ins)
    return pl.pallas_call(
        kernel,
        out_shape=[jax.ShapeDtypeStruct(s, d) for s, d in outs],
        in_specs=[s for _, s in ins],
        out_specs=[VMEM] * len(outs),
        scratch_shapes=list(scratch),
        compiler_params=pltpu.CompilerParams(vmem_limit_bytes=24 * 2**20),
        cost_estimate=pl.CostEstimate(flops=flops, bytes_accessed=moved, transcendentals=0),
    )(*[a for a, _ in ins])


def fold(product):
    parts = [product[:, k : k + LANES] for k in range(0, product.shape[1], LANES)]
    return jnp.sum(functools.reduce(lambda a, b: a + b, parts), axis=0, keepdims=True)


def tile_of(rows):
    return jnp.concatenate(rows + [jnp.zeros((8 - len(rows), LANES), F32)], axis=0)


def make(n_y, n_x, n_z):
    n_xy = n_y * n_x

    def per_device(psi, diag, block_dims, left_env, right_env):
        sectors, size, cols = psi.shape
        sub = cols // n_xy
        shard_rows = n_z * sub
        scale = 1.0 / (size * size)
        core = lax.axis_index("core")
        swap = [(0, 1), (1, 0)]
        meta = jnp.stack(
            [core, lax.axis_index("sec"), lax.axis_index(XY)]
            + [block_dims[s, k] for s in range(sectors) for k in range(2)]
        ).astype(jnp.int32)
        share, shard = (size, cols), (sub, size)

        def a2a(array, axes):
            return lax.all_to_all(array, axes, 0, 0, tiled=True)

        def dims_of(meta_ref, sector):
            return meta_ref[3 + 2 * sector], meta_ref[4 + 2 * sector]

        def share_mask(meta_ref, sector):
            row = lax.broadcasted_iota(jnp.int32, share, 0)
            col = lax.broadcasted_iota(jnp.int32, share, 1) + meta_ref[1] * cols
            rows, columns = dims_of(meta_ref, sector)
            return (row < rows) & (col < columns)

        def start_kernel(meta_ref, psi_ref, diag_ref, out_ref, psi_a_ref, buf, sems):
            core, q = meta_ref[0], meta_ref[2]
            copies = [
                pltpu.make_async_copy(psi_ref.at[s], buf.at[s], sems.at[s]) for s in range(sectors)
            ]
            copies.append(
                pltpu.make_async_copy(diag_ref.at[core, :, q], out_ref.at[:, pl.ds(sub, sub)], sems.at[sectors])
            )
            for copy in copies:
                copy.start()
            total = jnp.zeros((1, LANES), F32)
            for s in range(sectors):
                copies[s].wait()
                own = jnp.where(share_mask(meta_ref, s), buf[s], 0.0)
                total = total + fold(own * own)

                @pl.when(core == s)
                def _():
                    psi_a_ref[...] = own

            first = pl.multiple_of(q * sub, sub)
            for k in range(n_z):
                out_ref[k, :sub] = psi_a_ref[pl.ds(k * cols + first, sub)]
                out_ref[k, 2 * sub :] = tile_of([total])
            copies[sectors].wait()

        def left_matmul(meta_ref, env_ref, got_ref, field, left_ref):
            core, per = meta_ref[0], PIECE // cols
            for i in range(size // PIECE):
                rows = pl.ds(i * PIECE, PIECE)
                for w in range(2):
                    env = env_ref[0, core, rows] if w == 0 else got_ref[rows]
                    part = jnp.dot(env, field, preferred_element_type=F32)
                    left_ref[i * per : (i + 1) * per, w] = part.astype(BF16).reshape(per, cols, cols)

        def first_kernel(meta_ref, got_ref, psi_a_ref, env_ref, env2_ref, u_a_ref, u_b_ref, diag_b_ref, left_ref):
            got = got_ref[...]
            norm = jnp.sum(jnp.sum(got[:, 2 * sub :], axis=0), axis=(0, 1), keepdims=True) * scale
            inverse = 1.0 / jnp.sqrt(norm)
            u_a = psi_a_ref[...] * inverse
            u_a_ref[...] = u_a
            for k in range(n_z):
                lanes = slice(k * cols, (k + 1) * cols)
                u_b_ref[:, lanes] = got[k, :sub] * inverse
                diag_b_ref[:, lanes] = got[k, sub : 2 * sub]
            left_matmul(meta_ref, env_ref, env2_ref, u_a.astype(BF16), left_ref)

        def right_kernel(meta_ref, moved_ref, env_ref, got_ref, out_ref):
            core = meta_ref[0]
            fields = [
                jnp.concatenate([moved_ref[k, w] for k in range(n_z)], axis=1) for w in range(2)
            ]
            for i in range(size // PIECE):
                rows = pl.ds(i * PIECE, PIECE)
                total = None
                for w in range(2):
                    env = env_ref[0, core, rows] if w == 0 else got_ref[rows]
                    part = lax.dot_general(
                        fields[w], env, (((1,), (1,)), ((), ())), preferred_element_type=F32
                    )
                    total = part if total is None else total + part
                out_ref[:, :, rows] = total.reshape(n_xy, sub, PIECE).astype(out_ref.dtype)

        def image_of(meta_ref, got_ref):
            image = jnp.sum(got_ref[...].astype(F32), axis=0)
            row = lax.broadcasted_iota(jnp.int32, shard, 0) + (meta_ref[1] * cols + meta_ref[2] * sub)
            col = lax.broadcasted_iota(jnp.int32, shard, 1)
            rows, columns = dims_of(meta_ref, meta_ref[0])
            return jnp.where((row < rows) & (col < columns), image, 0.0)

        def dots_tile(image, u_b_ref, more):
            u = u_b_ref[...]
            if not more:
                return tile_of([fold(u * image)])
            corr, hu = more[0][...], more[1][...]
            pairs = [(u, image), (corr, hu), (corr, image), (u, corr), (corr, corr), (u, u)]
            return tile_of([fold(a * b) for a, b in pairs])

        def image_kernel(meta_ref, got_ref, u_b_ref, *refs):
            *more, image_ref, out_ref = refs
            image = image_of(meta_ref, got_ref)
            image_ref[...] = image
            tile = dots_tile(image, u_b_ref, more)
            for k in range(n_z):
                for c in range(2):
                    out_ref[c * n_z + k, :sub] = image[:, k * cols : (k + 1) * cols]
                    out_ref[c * n_z + k, sub:] = tile

        def last_image_kernel(meta_ref, got_ref, u_b_ref, corr_b_ref, hu_b_ref, out_ref):
            image = image_of(meta_ref, got_ref)
            tile = dots_tile(image, u_b_ref, (corr_b_ref, hu_b_ref))
            sums = jnp.sum(tile, axis=1, keepdims=True)
            row = lax.broadcasted_iota(jnp.int32, tile.shape, 0)
            lane = lax.broadcasted_iota(jnp.int32, tile.shape, 1)
            line = jnp.sum(jnp.where(row == lane, sums, 0.0), axis=0, keepdims=True)
            out_ref[...] = jnp.broadcast_to(line, out_ref.shape)

        def spread_kernel(meta_ref, got_ref, out_ref):
            first = meta_ref[0] * n_z
            tile = jnp.sum(got_ref[:, sub:], axis=0)
            for k in range(n_z):
                rows = got_ref[first + k, :sub]
                for j in range(n_xy):
                    out_ref[j, k * sub : (k + 1) * sub] = rows
            for j in range(n_xy):
                out_ref[j, shard_rows:] = tile

        def projected(theta, sums):
            u_image, corr_hu, corr_image, project, size_corr, size_u = sums
            inverse = 1.0 / jnp.sqrt(size_corr - project * project * (2.0 - size_u))
            cross = 0.5 * ((u_image - project * theta) + (corr_hu - project * theta)) * inverse
            corner = corr_image - project * (corr_hu + u_image) + project * project * theta
            corner = corner * inverse * inverse
            half = 0.5 * (theta - corner)
            lowest = 0.5 * (theta + corner) - jnp.sqrt(half * half + cross * cross)
            x, y = corner - lowest, -cross
            length = jnp.sqrt(x * x + y * y)
            x, y = x / length, y / length
            theta = x * x * theta + 2.0 * x * y * cross + y * y * corner
            return x - y * project * inverse, y * inverse, theta, lowest

        def sums_of(got_ref, count):
            tile = jnp.sum(got_ref[:, shard_rows:], axis=0)
            sums = jnp.sum(tile, axis=1, keepdims=True) * scale
            return [sums[k : k + 1] for k in range(count)]

        def correction(theta, image, vector, diagonal):
            return (image - theta * vector) / (1.0 + jnp.abs(diagonal - theta))

        def share_of(got_ref):
            got = got_ref[:, :shard_rows].reshape(n_xy, n_z, sub, cols)
            return jnp.transpose(got, (1, 0, 2, 3)).reshape(share)

        def begin_kernel(meta_ref, got_ref, u_a_ref, u_b_ref, hu_b_ref, diag_ref, diag_b_ref, env_ref, env2_ref, hu_a_ref, corr_a_ref, corr_b_ref, theta_ref, left_ref):
            (theta,) = sums_of(got_ref, 1)
            theta_ref[...] = jnp.broadcast_to(theta, theta_ref.shape)
            hu_a = share_of(got_ref)
            hu_a_ref[...] = hu_a
            corr_a = correction(theta, hu_a, u_a_ref[...], diag_ref[meta_ref[0]])
            corr_a_ref[...] = corr_a
            corr_b_ref[...] = correction(theta, hu_b_ref[...], u_b_ref[...], diag_b_ref[...])
            left_matmul(meta_ref, env_ref, env2_ref, corr_a.astype(BF16), left_ref)

        def update_kernel(meta_ref, got_ref, old_theta_ref, u_a_ref, corr_a_ref, hu_a_ref, u_b_ref, corr_b_ref, hu_b_ref, hc_b_ref, diag_ref, diag_b_ref, env_ref, env2_ref, u_a_out, corr_a_out, hu_a_out, u_b_out, corr_b_out, hu_b_out, theta_ref, left_ref):
            one, two, theta, _ = projected(old_theta_ref[0:1, 0:1], sums_of(got_ref, 6))
            theta_ref[...] = jnp.broadcast_to(theta, theta_ref.shape)
            u_a = one * u_a_ref[...] + two * corr_a_ref[...]
            hu_a = one * hu_a_ref[...] + two * share_of(got_ref)
            corr_a = correction(theta, hu_a, u_a, diag_ref[meta_ref[0]])
            u_a_out[...], hu_a_out[...], corr_a_out[...] = u_a, hu_a, corr_a
            u_b = one * u_b_ref[...] + two * corr_b_ref[...]
            hu_b = one * hu_b_ref[...] + two * hc_b_ref[...]
            u_b_out[...], hu_b_out[...] = u_b, hu_b
            corr_b_out[...] = correction(theta, hu_b, u_b, diag_b_ref[...])
            left_matmul(meta_ref, env_ref, env2_ref, corr_a.astype(BF16), left_ref)

        def last_kernel(meta_ref, got_ref, theta_ref, u_a_ref, corr_a_ref, u_far_ref, corr_far_ref, out_ref, energy_ref):
            line = jnp.sum(got_ref[...], axis=0, keepdims=True) * scale
            sums = [line[:, k : k + 1] for k in range(6)]
            one, two, _, lowest = projected(theta_ref[0:1, 0:1], sums)
            c = meta_ref[0]
            out_ref[c] = one * u_a_ref[...] + two * corr_a_ref[...]
            out_ref[1 - c] = one * u_far_ref[...] + two * corr_far_ref[...]
            energy_ref[...] = lowest

        def v(*arrays):
            return [(a, VMEM) for a in arrays]

        i_meta = [(meta, SMEM)]
        left_out = ((n_z, 2, cols, cols), BF16)
        tile_out, a_out, b_out = ((8, cols), F32), (share, F32), (shard, F32)
        work = 4 * size * size * cols

        first, psi_a = call(
            start_kernel,
            [((n_z, 2 * sub + 8, cols), F32), a_out],
            i_meta + [(psi, HBM), (diag.reshape(sectors, n_z, n_xy, sub, cols), HBM)],
            [pltpu.VMEM(psi.shape, F32), pltpu.SemaphoreType.DMA((sectors + 1,))],
        )

        def swapped(env):
            other = lax.dynamic_index_in_dim(env[0], 1 - core, 0, keepdims=False)
            return lax.ppermute(other, "core", swap)

        first, left_env = lax.optimization_barrier((first, left_env))
        lefts = v(left_env, swapped(left_env))
        first = a2a(first, "sec")
        u_a, u_b, diag_b, left = call(
            first_kernel, [a_out, b_out, b_out, left_out], i_meta + v(first, psi_a) + lefts, (), work
        )
        left, right_env = lax.optimization_barrier((left, right_env))
        rights = v(right_env, swapped(right_env))

        def apply_right(left, kind):
            moved = a2a(left, "sec")
            (partial,) = call(
                right_kernel, [((n_xy, sub, size), kind)], i_meta + v(moved) + rights, (), work
            )
            return a2a(partial, XY)

        def gather(payload):
            payload = a2a(payload, CZ)
            (payload,) = call(spread_kernel, [((n_xy, shard_rows + 8, cols), F32)], i_meta + v(payload))
            return a2a(payload, XY)

        payload_out = ((2 * n_z, sub + 8, cols), F32)
        got = apply_right(left, F32)
        hu_b, payload = call(image_kernel, [b_out, payload_out], i_meta + v(got, u_b))
        got = gather(payload)
        hu_a, corr_a, corr_b, theta, left = call(
            begin_kernel,
            [a_out, a_out, b_out, tile_out, left_out],
            i_meta + v(got, u_a, u_b, hu_b, diag, diag_b) + lefts, (), work,
        )
        for _ in range(ITERS - 1):
            got = apply_right(left, F32)
            hc_b, payload = call(
                image_kernel, [b_out, payload_out], i_meta + v(got, u_b, corr_b, hu_b)
            )
            got = gather(payload)
            u_a, corr_a, hu_a, u_b, corr_b, hu_b, theta, left = call(
                update_kernel,
                [a_out, a_out, a_out, b_out, b_out, b_out, tile_out, left_out],
                i_meta + v(got, theta, u_a, corr_a, hu_a, u_b, corr_b, hu_b, hc_b, diag, diag_b) + lefts,
                (), work,
            )
        u_far = lax.ppermute(u_a, "core", swap)
        corr_far = lax.ppermute(corr_a, "core", swap)
        got = apply_right(left, BF16)
        (sums,) = call(
            last_image_kernel, [((2 * n_z * n_xy, cols), F32)], i_meta + v(got, u_b, corr_b, hu_b)
        )
        sums = a2a(sums, ALL)
        out, energy = call(
            last_kernel, [(psi.shape, F32), ((1, 1), F32)],
            i_meta + v(sums, theta, u_a, corr_a, u_far, corr_far),
        )
        return out, energy.reshape(())

    return per_device


def solution(mesh):
    n_z = mesh.shape["sec"]
    n_y = n_x = int(round((mesh.shape["term"] // 2) ** 0.5))
    fine = Mesh(mesh.devices.reshape(n_y, n_x, 2, n_z), ("y", "x", "core", "sec"))
    term = ("y", "x", "core")
    in_specs = (
        P(None, None, "sec"),
        P(None, None, "sec"),
        P(),
        P(term, None, None, None),
        P(term, None, None, None),
    )
    out_specs = (P(None, None, "sec"), P())
    return jax.shard_map(
        make(n_y, n_x, n_z), mesh=fine, in_specs=in_specs, out_specs=out_specs, check_vma=False
    )
```

time: 265 us -> 230 us (0.87)
  blocking collectives: 172 us -> 148 us
  Pallas kernels: 32.1 us -> 20.7 us
  waiting for transfers between devices: 29.7 us -> 26.1 us
  starting transfers between devices: 17.3 us -> 20 us
    all_to_all x12 -> x10, blocking collectives: 172 us -> 148 us  [a2a(): return lax.all_to_all(array, axes, 0, 0, tiled=True)]
    pallas_call x16 -> x13, Pallas kernels: 32.1 us -> 20.7 us  [call(): pl.pallas_call(kernel, out_shape=[jax.ShapeDtypeStruct(s, d) for s, d in...]
    all_to_all x3 -> x2, waiting for transfers between devices: 29.7 us -> 26.1 us  [a2a(): return lax.all_to_all(array, axes, 0, 0, tiled=True)]
    another operation x0 -> x1, local copies, waits for them, and re-layouts: none -> 2.7 us  [per_device(): jnp.stack([core, lax.axis_index('sec'), lax.axis_index(XY)] + [block_dims...]
    all_to_all x3 -> x2, starting transfers between devices: 10.7 us -> 12.6 us  [a2a(): return lax.all_to_all(array, axes, 0, 0, tiled=True)]
    unnamed x32 -> x18, local copies, waits for them, and re-layouts: 8.15 us -> 7.55 us
  transfers between devices with their start and end apart: 7 -> 6, of which waited for: 3 -> 2; matrix products, arithmetic and copies ran while one was open for 1% -> 0% of each run, Pallas kernels for 2% -> 1%
where the time goes in v3:
time: 230 us; the launch traced here: 229 us
  blocking collectives  148 us (64%)
  waiting for transfers between devices  26.1 us (11%)
  Pallas kernels  20.7 us (9%)
  starting transfers between devices  20 us (9%)
  local copies, waits for them, and re-layouts  13.8 us (6%)
    all_to_all x10, blocking collectives, a2a(): return lax.all_to_all(array, axes, 0, 0, tiled=True)  148 us
    all_to_all x2, waiting for transfers between devices, a2a(): return lax.all_to_all(array, axes, 0, 0, tiled=True)  26.1 us
    pallas_call x13, Pallas kernels, call(): pl.pallas_call(kernel, out_shape=[jax.ShapeDtypeStruct(s, d) for s, d in...  20.7 us
    all_to_all x2, starting transfers between devices, a2a(): return lax.all_to_all(array, axes, 0, 0, tiled=True)  12.6 us
    unnamed x18, local copies, waits for them, and re-layouts  7.55 us
    ppermute x2, starting transfers between devices, swapped(): return lax.ppermute(other, 'core', swap)  4.93 us
  transfers between devices with their start and end apart: 6, of which 2 were waited for; matrix products, arithmetic and copies ran while one was open for 0% of the time, Pallas kernels for 1%

profile of v3, /device:TPU:1, one launch (start us, length us, event | category | flops | bytes accessed | tf_op | source)
XLA Modules:
  0.0 229.0 jit_solution(12465027903228631229)
XLA Ops:
  0.6 1.5 fusion
  2.1 2.7 %stack.15.meta_ref = s32[7]{0:T(128)S(1)} concatenate(s32[1]{0:T(128)} %bitcast, s32[1]{0:T(128)} %bitcast.1, s32[1]{0:T(128)} %bitcast.2, s32[1]{0:T(128)} %bitcast.3, s32[1]{0:T(128)} %bitcast.4, s32[1]{0:T(128)} %bitcast.5, s32[1]{0:T(128)} %bitcast.6), dimensions={0} | concatenate | bytes 56 | tf_op jit(solution)/shard_map/stack | solution.py:55
  4.8 0.0 copy-start.3
  4.8 1.2 copy-done.3
  6.1 0.0 copy-start.5
  6.1 1.2 copy-done.5
  7.3 1.1 shard_map.68
  8.4 0.0 copy-start
  8.4 1.9 dynamic-slice_bitcast_fusion.1
  10.3 3.3 %collective-permute-start = (bf16[1024,1024]{1,0:T(8,128)(2,1)S(1)}, bf16[1024,1024]{1,0:T(8,128)(2,1)S(1)}, u32[]{:S(2)}, u32[]{:S(2)}) collective-permute-start(bf16[1024,1024]{1,0:T(8,128)(2,1)S(1)} %dynamic-slice_bitcast_fusion.1), channel_id=1, source_target_pairs={{0,8},{8,0},{1,9},{9,1},{2,10},{10,2},{3,11},{11,3},{4,12},{12,4},... | collective-permute-start | bytes 6291464 | tf_op jit(solution)/shard_map/ppermute | solution.py:255
  13.7 14.0 %all_to_all.66.got_ref = f32[8,24,128]{2,1,0:T(8,128)S(1)} all-to-all(f32[8,24,128]{2,1,0:T(8,128)S(1)} %get-tuple-element.31), channel_id=1, replica_groups=mesh['y'=4,'x'=4,'core'=2,'sec'=8] {'sec'}, dimensions={0} | all-to-all | bytes 196608 | tf_op jit(solution)/shard_map/all_to_all | solution.py:62
  27.7 0.0 collective-permute-done.env2_ref
  27.7 0.0 copy-done
  27.7 0.0 copy-start.1
  27.7 1.9 shard_map.69
  29.7 0.3 copy-done.1
  29.9 0.2 dynamic-slice_bitcast_fusion
  30.1 1.6 collective-permute-start.1
  31.7 20.4 %all_to_all.67.moved_ref = bf16[8,2,128,128]{3,2,1,0:T(8,128)(2,1)S(1)} all-to-all(bf16[8,2,128,128]{3,2,1,0:T(8,128)(2,1)S(1)} %get-tuple-element.35), channel_id=1, replica_groups=mesh['y'=4,'x'=4,'core'=2,'sec'=8] {'sec'}, dimensions={0} | all-to-all | bytes 1048576 | tf_op jit(solution)/shard_map/all_to_all | solution.py:62
  52.1 0.0 collective-permute-done.1.got_ref
  52.1 2.0 shard_map.70
  54.1 0.0 copy-start.4
  54.1 17.3 %all_to_all.68.got_ref = f32[16,8,1024]{2,1,0:T(8,128)S(1)} all-to-all(f32[16,8,1024]{2,1,0:T(8,128)S(1)} %shard_map.70), channel_id=1, replica_groups=mesh['y'=4,'x'=4,'core'=2,'sec'=8] {'y','x'}, dimensions={0} | all-to-all | bytes 1048576 | tf_op jit(solution)/shard_map/all_to_all | solution.py:62
  71.5 0.6 shard_map.71
  72.1 11.7 %all_to_all.69.got_ref = f32[16,16,128]{2,1,0:T(8,128)S(1)} all-to-all(f32[16,16,128]{2,1,0:T(8,128)S(1)} %get-tuple-element.38), channel_id=1, replica_groups=mesh['y'=4,'x'=4,'core'=2,'sec'=8] {'core','sec'}, dimensions={0} | all-to-all | bytes 262144 | tf_op jit(solution)/shard_map/all_to_all | solution.py:62
  83.7 0.6 shard_map.72
  84.3 13.7 %all_to_all.70.got_ref = f32[16,72,128]{2,1,0:T(8,128)S(1)} all-to-all(f32[16,72,128]{2,1,0:T(8,128)S(1)} %shard_map.72), channel_id=1, replica_groups=mesh['y'=4,'x'=4,'core'=2,'sec'=8] {'y','x'}, dimensions={0} | all-to-all | bytes 1179648 | tf_op jit(solution)/shard_map/all_to_all | solution.py:62
  98.0 0.0 copy-done.4
  98.0 2.0 shard_map.73
  100.0 18.1 %all_to_all.71.moved_ref = bf16[8,2,128,128]{3,2,1,0:T(8,128)(2,1)S(1)} all-to-all(bf16[8,2,128,128]{3,2,1,0:T(8,128)(2,1)S(1)} %get-tuple-element.42), channel_id=1, replica_groups=mesh['y'=4,'x'=4,'core'=2,'sec'=8] {'sec'}, dimensions={0} | all-to-all | bytes 1048576 | tf_op jit(solution)/shard_map/all_to_all | solution.py:62
  118.0 2.0 shard_map.74
  120.1 12.7 %all_to_all.72.got_ref = f32[16,8,1024]{2,1,0:T(8,128)S(1)} all-to-all(f32[16,8,1024]{2,1,0:T(8,128)S(1)} %shard_map.74), channel_id=1, replica_groups=mesh['y'=4,'x'=4,'core'=2,'sec'=8] {'y','x'}, dimensions={0} | all-to-all | bytes 1048576 | tf_op jit(solution)/shard_map/all_to_all | solution.py:62
  132.8 0.6 shard_map.75
  133.4 14.7 %all_to_all.73.got_ref = f32[16,16,128]{2,1,0:T(8,128)S(1)} all-to-all(f32[16,16,128]{2,1,0:T(8,128)S(1)} %get-tuple-element.44), channel_id=1, replica_groups=mesh['y'=4,'x'=4,'core'=2,'sec'=8] {'core','sec'}, dimensions={0} | all-to-all | bytes 262144 | tf_op jit(solution)/shard_map/all_to_all | solution.py:62
  148.1 0.6 shard_map.76
  148.7 13.7 %all_to_all.74.got_ref = f32[16,72,128]{2,1,0:T(8,128)S(1)} all-to-all(f32[16,72,128]{2,1,0:T(8,128)S(1)} %shard_map.76), channel_id=1, replica_groups=mesh['y'=4,'x'=4,'core'=2,'sec'=8] {'y','x'}, dimensions={0} | all-to-all | bytes 1179648 | tf_op jit(solution)/shard_map/all_to_all | solution.py:62
  162.4 2.8 %shard_map.77 = (f32[1024,128]{1,0:T(8,128)S(1)}, f32[1024,128]{1,0:T(8,128)S(1)}, f32[1024,128]{1,0:T(8,128)}, f32[8,1024]{1,0:T(8,128)S(1)}, f32[8,1024]{1,0:T...) custom-call(s32[7]{0:T(128)S(1)} %stack.15.meta_ref, ...), custom_call_target="tpu_custom_call" | custom-call | flops 536870912 | bytes 9670684 | tf_op jit(solution)/shard_map/pallas_call | solution.py:25
  165.2 0.0 copy-start.6
  165.2 0.8 copy-done.6
  166.0 0.0 copy-start.8
  166.0 0.8 copy-done.8
  166.8 3.8 %all-to-all-start.9 = ((bf16[8,2,128,128]{3,2,1,0:T(8,128)(2,1)}), bf16[8,2,128,128]{3,2,1,0:T(8,128)(2,1)S(1)}, u32[]{:S(2)}, u32[]{:S(2)}) async-start(bf16[8,2,128,128]{3,2,1,0:T(8,128)(2,1)} %copy-done.8), calls=%async_computation.9 | async-start | bytes 1048576 | tf_op jit(solution)/shard_map/all_to_all | solution.py:62
  170.6 2.2 collective-permute-start.2
  172.8 0.3 collective-permute-start.3
  173.1 13.0 %all-to-all-done.9.moved_ref = bf16[8,2,128,128]{3,2,1,0:T(8,128)(2,1)S(1)} async-done(((bf16[8,2,128,128]{3,2,1,0:T(8,128)(2,1)}), bf16[8,2,128,128]{3,2,1,0:T(8,128)(2,1)S(1)}, u32[]{:S(2)}, u32[]{:S(2)}) %all-to-all-start.9) | async-done | bytes 524320 | tf_op jit(solution)/shard_map/all_to_all | solution.py:62
  186.1 0.0 copy-start.2
  186.1 2.2 copy-done.2
  188.3 2.0 shard_map.78
  190.3 11.3 %all_to_all.75.got_ref = bf16[16,8,1024]{2,1,0:T(8,128)(2,1)S(1)} all-to-all(bf16[16,8,1024]{2,1,0:T(8,128)(2,1)S(1)} %shard_map.78), channel_id=1, replica_groups=mesh['y'=4,'x'=4,'core'=2,'sec'=8] {'y','x'}, dimensions={0} | all-to-all | bytes 524288 | tf_op jit(solution)/shard_map/all_to_all | solution.py:62
  201.6 1.4 shard_map.79
  203.0 8.8 %all-to-all-start.11 = ((f32[256,1,128]{2,1,0:T(1,128)}), f32[256,1,128]{2,1,0:T(1,128)S(1)}, u32[]{:S(2)}, u32[]{:S(2)}) async-start(f32[256,1,128]{2,1,0:T(1,128)} %bitcast.11), calls=%async_computation.11 | async-start | bytes 262144 | tf_op jit(solution)/shard_map/all_to_all | solution.py:62
  211.8 0.0 collective-permute-done.2.u_far_ref
  211.9 0.0 collective-permute-done.3.corr_far_ref
  211.9 13.1 %all-to-all-done.11 = f32[256,1,128]{2,1,0:T(1,128)S(1)} async-done(((f32[256,1,128]{2,1,0:T(1,128)}), f32[256,1,128]{2,1,0:T(1,128)S(1)}, u32[]{:S(2)}, u32[]{:S(2)}) %all-to-all-start.11) | async-done | bytes 131104 | tf_op jit(solution)/shard_map/all_to_all | solution.py:62
  224.9 0.0 copy-start.7
  225.0 1.0 copy-done.7
  226.0 3.1 %shard_map.80 = (f32[2,1024,128]{2,1,0:T(8,128)}, f32[1,1]{1,0:T(1,128)}) custom-call(s32[7]{0:T(128)S(1)} %stack.15.meta_ref, f32[256,128]{1,0:T(8,128)S(1)} %bitcast.18, f32[8,128]{1,0:T(8,128)S(1)} %get-tuple-element.53.theta_ref, f32[1024,128]{1,0:T(8,128)S(1)} %get-tuple-element.54.u_a_ref, f32[1024,128]{1,0:T(8,128)S(1)} %copy-done.7, ...), custom_call_target="tpu_custom_call" | custom-call | bytes 2232348 | tf_op jit(solution)/shard_map/pallas_call | solution.py:25
Async XLA Ops:
  4.8 1.2 copy-start.3
  6.1 1.2 copy-start.5
  8.4 19.3 %copy-start = (bf16[1,2,1024,1024]{3,2,1,0:T(8,128)(2,1)S(1)}, bf16[1,2,1024,1024]{3,2,1,0:T(8,128)(2,1)}, u32[]{:S(2)}) copy-start(bf16[1,2,1024,1024]{3,2,1,0:T(8,128)(2,1)} %env_ref.4) | copy-start | bytes 12582916
  10.3 17.4 %collective-permute-start = (bf16[1024,1024]{1,0:T(8,128)(2,1)S(1)}, bf16[1024,1024]{1,0:T(8,128)(2,1)S(1)}, u32[]{:S(2)}, u32[]{:S(2)}) collective-permute-start(bf16[1024,1024]{1,0:T(8,128)(2,1)S(1)} %dynamic-slice_bitcast_fusion.1), channel_id=1, source_target_pairs={{0,8},{8,0},{1,9},{9,1},{2,10},{10,2},{3,11},{11,3},{4,12},{12,4},... | collective-permute-start | bytes 6291464 | tf_op jit(solution)/shard_map/ppermute | solution.py:255
  27.7 2.2 copy-start.1
  30.1 22.0 %collective-permute-start.1 = (bf16[1024,1024]{1,0:T(8,128)(2,1)S(1)}, bf16[1024,1024]{1,0:T(8,128)(2,1)S(1)}, u32[]{:S(2)}, u32[]{:S(2)}) collective-permute-start(bf16[1024,1024]{1,0:T(8,128)(2,1)S(1)} %dynamic-slice_bitcast_fusion), channel_id=1, source_target_pairs={{0,8},{8,0},{1,9},{9,1},{2,10},{10,2},{3,11},{11,3},{4,12},{12,4},... | collective-permute-start | bytes 6291464 | tf_op jit(solution)/shard_map/ppermute | solution.py:255
  54.1 43.9 %copy-start.4 = (f32[2,1024,128]{2,1,0:T(8,128)S(1)}, f32[2,1024,128]{2,1,0:T(8,128)}, u32[]{:S(2)}) copy-start(f32[2,1024,128]{2,1,0:T(8,128)} %diag_ref.3) | copy-start | bytes 3145732
  165.2 0.8 copy-start.6
  166.0 0.8 copy-start.8
  166.8 19.2 %all-to-all-start.9 = ((bf16[8,2,128,128]{3,2,1,0:T(8,128)(2,1)}), bf16[8,2,128,128]{3,2,1,0:T(8,128)(2,1)S(1)}, u32[]{:S(2)}, u32[]{:S(2)}) async-start(bf16[8,2,128,128]{3,2,1,0:T(8,128)(2,1)} %copy-done.8), calls=%async_computation.9 | async-start | bytes 1048576 | tf_op jit(solution)/shard_map/all_to_all | solution.py:62
  170.6 41.3 %collective-permute-start.2 = (f32[1024,128]{1,0:T(8,128)S(1)}, f32[1024,128]{1,0:T(8,128)}, u32[]{:S(2)}, u32[]{:S(2)}) collective-permute-start(f32[1024,128]{1,0:T(8,128)S(1)} %get-tuple-element.54.u_a_ref), channel_id=1, source_target_pairs={{0,8},{8,0},{1,9},{9,1},{2,10},{10,2},{3,11},{11,3},{4,12},{12,4},... | collective-permute-start | bytes 1572872 | tf_op jit(solution)/shard_map/ppermute | solution.py:299
  172.8 39.1 %collective-permute-start.3 = (f32[1024,128]{1,0:T(8,128)}, f32[1024,128]{1,0:T(8,128)}, u32[]{:S(2)}, u32[]{:S(2)}) collective-permute-start(f32[1024,128]{1,0:T(8,128)} %copy-done.6), channel_id=1, source_target_pairs={{0,8},{8,0},{1,9},{9,1},{2,10},{10,2},{3,11},{11,3},{4,12},{12,4},... | collective-permute-start | bytes 1572872 | tf_op jit(solution)/shard_map/ppermute | solution.py:300
  186.1 2.2 copy-start.2
  203.0 21.9 %all-to-all-start.11 = ((f32[256,1,128]{2,1,0:T(1,128)}), f32[256,1,128]{2,1,0:T(1,128)S(1)}, u32[]{:S(2)}, u32[]{:S(2)}) async-start(f32[256,1,128]{2,1,0:T(1,128)} %bitcast.11), calls=%async_computation.11 | async-start | bytes 262144 | tf_op jit(solution)/shard_map/all_to_all | solution.py:62
  224.9 1.0 copy-start.7

commit v4 on v3

--- a/solution.py
+++ b/solution.py
@@ -13,10 +13,11 @@
 ALL = ("y", "x", "core", "sec")
 LANES = 128
 PIECE = 256
+LIMIT = 24
+START = 4 * 10**9
 F32 = jnp.float32
 BF16 = jnp.bfloat16
 SMEM = pl.BlockSpec(memory_space=pltpu.SMEM)
-HBM = pl.BlockSpec(memory_space=pltpu.HBM)
 VMEM = pl.BlockSpec(memory_space=pltpu.VMEM)
 
 
@@ -28,7 +29,7 @@
         in_specs=[s for _, s in ins],
         out_specs=[VMEM] * len(outs),
         scratch_shapes=list(scratch),
-        compiler_params=pltpu.CompilerParams(vmem_limit_bytes=24 * 2**20),
+        compiler_params=pltpu.CompilerParams(vmem_limit_bytes=LIMIT * 2**20),
         cost_estimate=pl.CostEstimate(flops=flops, bytes_accessed=moved, transcendentals=0),
     )(*[a for a, _ in ins])
 
@@ -52,52 +53,49 @@
         scale = 1.0 / (size * size)
         core = lax.axis_index("core")
         swap = [(0, 1), (1, 0)]
-        meta = jnp.stack(
-            [core, lax.axis_index("sec"), lax.axis_index(XY)]
-            + [block_dims[s, k] for s in range(sectors) for k in range(2)]
-        ).astype(jnp.int32)
+        row = lax.broadcasted_iota(jnp.int32, (sectors + 2, 2), 0) - sectors
+        col = lax.broadcasted_iota(jnp.int32, (sectors + 2, 2), 1)
+        meta = jnp.where(
+            row < 0,
+            jnp.pad(block_dims, ((0, 2), (0, 0))),
+            jnp.where(row > 0, lax.axis_index(XY), jnp.where(col == 0, core, lax.axis_index("sec"))),
+        )
         share, shard = (size, cols), (sub, size)
 
         def a2a(array, axes):
             return lax.all_to_all(array, axes, 0, 0, tiled=True)
 
         def dims_of(meta_ref, sector):
-            return meta_ref[3 + 2 * sector], meta_ref[4 + 2 * sector]
+            return meta_ref[sector, 0], meta_ref[sector, 1]
+
+        def place(meta_ref):
+            return meta_ref[sectors, 0], meta_ref[sectors, 1], meta_ref[sectors + 1, 0]
 
         def share_mask(meta_ref, sector):
             row = lax.broadcasted_iota(jnp.int32, share, 0)
-            col = lax.broadcasted_iota(jnp.int32, share, 1) + meta_ref[1] * cols
+            col = lax.broadcasted_iota(jnp.int32, share, 1) + place(meta_ref)[1] * cols
             rows, columns = dims_of(meta_ref, sector)
             return (row < rows) & (col < columns)
 
-        def start_kernel(meta_ref, psi_ref, diag_ref, out_ref, psi_a_ref, buf, sems):
-            core, q = meta_ref[0], meta_ref[2]
-            copies = [
-                pltpu.make_async_copy(psi_ref.at[s], buf.at[s], sems.at[s]) for s in range(sectors)
-            ]
-            copies.append(
-                pltpu.make_async_copy(diag_ref.at[core, :, q], out_ref.at[:, pl.ds(sub, sub)], sems.at[sectors])
-            )
-            for copy in copies:
-                copy.start()
+        def own_rows(meta_ref, k):
+            return pl.ds(pl.multiple_of(k * cols + place(meta_ref)[2] * sub, sub), sub)
+
+        def start_kernel(meta_ref, psi_ref, out_ref, psi_a_ref):
             total = jnp.zeros((1, LANES), F32)
             for s in range(sectors):
-                copies[s].wait()
-                own = jnp.where(share_mask(meta_ref, s), buf[s], 0.0)
+                own = jnp.where(share_mask(meta_ref, s), psi_ref[s], 0.0)
                 total = total + fold(own * own)
 
-                @pl.when(core == s)
+                @pl.when(place(meta_ref)[0] == s)
                 def _():
                     psi_a_ref[...] = own
 
-            first = pl.multiple_of(q * sub, sub)
-            for k in range(n_z):
-                out_ref[k, :sub] = psi_a_ref[pl.ds(k * cols + first, sub)]
-                out_ref[k, 2 * sub :] = tile_of([total])
-            copies[sectors].wait()
+            for k in range(n_z):
+                out_ref[k, :sub] = psi_a_ref[own_rows(meta_ref, k)]
+                out_ref[k, sub:] = tile_of([total])
 
         def left_matmul(meta_ref, env_ref, got_ref, field, left_ref):
-            core, per = meta_ref[0], PIECE // cols
+            core, per = place(meta_ref)[0], PIECE // cols
             for i in range(size // PIECE):
                 rows = pl.ds(i * PIECE, PIECE)
                 for w in range(2):
@@ -105,20 +103,19 @@
                     part = jnp.dot(env, field, preferred_element_type=F32)
                     left_ref[i * per : (i + 1) * per, w] = part.astype(BF16).reshape(per, cols, cols)
 
-        def first_kernel(meta_ref, got_ref, psi_a_ref, env_ref, env2_ref, u_a_ref, u_b_ref, diag_b_ref, left_ref):
+        def first_kernel(meta_ref, got_ref, psi_a_ref, env_ref, env2_ref, u_a_ref, u_b_ref, left_ref):
             got = got_ref[...]
-            norm = jnp.sum(jnp.sum(got[:, 2 * sub :], axis=0), axis=(0, 1), keepdims=True) * scale
+            norm = jnp.sum(jnp.sum(got[:, sub:], axis=0), axis=(0, 1), keepdims=True) * scale
             inverse = 1.0 / jnp.sqrt(norm)
             u_a = psi_a_ref[...] * inverse
             u_a_ref[...] = u_a
             for k in range(n_z):
                 lanes = slice(k * cols, (k + 1) * cols)
                 u_b_ref[:, lanes] = got[k, :sub] * inverse
-                diag_b_ref[:, lanes] = got[k, sub : 2 * sub]
             left_matmul(meta_ref, env_ref, env2_ref, u_a.astype(BF16), left_ref)
 
-        def right_kernel(meta_ref, moved_ref, env_ref, got_ref, out_ref):
-            core = meta_ref[0]
+        def right_pieces(meta_ref, moved_ref, env_ref, got_ref):
+            core = place(meta_ref)[0]
             fields = [
                 jnp.concatenate([moved_ref[k, w] for k in range(n_z)], axis=1) for w in range(2)
             ]
@@ -131,13 +128,18 @@
                         fields[w], env, (((1,), (1,)), ((), ())), preferred_element_type=F32
                     )
                     total = part if total is None else total + part
+                yield rows, total
+
+        def right_kernel(meta_ref, moved_ref, env_ref, got_ref, out_ref):
+            for rows, total in right_pieces(meta_ref, moved_ref, env_ref, got_ref):
                 out_ref[:, :, rows] = total.reshape(n_xy, sub, PIECE).astype(out_ref.dtype)
 
         def image_of(meta_ref, got_ref):
+            core, z, q = place(meta_ref)
             image = jnp.sum(got_ref[...].astype(F32), axis=0)
-            row = lax.broadcasted_iota(jnp.int32, shard, 0) + (meta_ref[1] * cols + meta_ref[2] * sub)
+            row = lax.broadcasted_iota(jnp.int32, shard, 0) + (z * cols + q * sub)
             col = lax.broadcasted_iota(jnp.int32, shard, 1)
-            rows, columns = dims_of(meta_ref, meta_ref[0])
+            rows, columns = dims_of(meta_ref, core)
             return jnp.where((row < rows) & (col < columns), image, 0.0)
 
         def dots_tile(image, u_b_ref, more):
@@ -148,15 +150,24 @@
             pairs = [(u, image), (corr, hu), (corr, image), (u, corr), (corr, corr), (u, u)]
             return tile_of([fold(a * b) for a, b in pairs])
 
-        def image_kernel(meta_ref, got_ref, u_b_ref, *refs):
-            *more, image_ref, out_ref = refs
+        def put_image(meta_ref, got_ref, u_b_ref, more, image_ref, out_ref):
             image = image_of(meta_ref, got_ref)
             image_ref[...] = image
             tile = dots_tile(image, u_b_ref, more)
             for k in range(n_z):
                 for c in range(2):
                     out_ref[c * n_z + k, :sub] = image[:, k * cols : (k + 1) * cols]
-                    out_ref[c * n_z + k, sub:] = tile
+                    out_ref[c * n_z + k, sub : sub + 8] = tile
+
+        def first_image_kernel(meta_ref, got_ref, u_b_ref, diag_ref, image_ref, out_ref):
+            put_image(meta_ref, got_ref, u_b_ref, (), image_ref, out_ref)
+            core = place(meta_ref)[0]
+            for k in range(n_z):
+                out_ref[core * n_z + k, sub + 8 :] = diag_ref[core, own_rows(meta_ref, k)]
+                out_ref[(1 - core) * n_z + k, sub + 8 :] = jnp.zeros((sub, cols), F32)
+
+        def image_kernel(meta_ref, got_ref, u_b_ref, corr_b_ref, hu_b_ref, image_ref, out_ref):
+            put_image(meta_ref, got_ref, u_b_ref, (corr_b_ref, hu_b_ref), image_ref, out_ref)
 
         def last_image_kernel(meta_ref, got_ref, u_b_ref, corr_b_ref, hu_b_ref, out_ref):
             image = image_of(meta_ref, got_ref)
@@ -167,13 +178,15 @@
             line = jnp.sum(jnp.where(row == lane, sums, 0.0), axis=0, keepdims=True)
             out_ref[...] = jnp.broadcast_to(line, out_ref.shape)
 
-        def spread_kernel(meta_ref, got_ref, out_ref):
-            first = meta_ref[0] * n_z
-            tile = jnp.sum(got_ref[:, sub:], axis=0)
+        def spread_kernel(meta_ref, got_ref, out_ref, *diag_b_ref):
+            first = place(meta_ref)[0] * n_z
+            tile = jnp.sum(got_ref[:, sub : sub + 8], axis=0)
             for k in range(n_z):
                 rows = got_ref[first + k, :sub]
                 for j in range(n_xy):
                     out_ref[j, k * sub : (k + 1) * sub] = rows
+                for ref in diag_b_ref:
+                    ref[:, k * cols : (k + 1) * cols] = got_ref[first + k, sub + 8 :]
             for j in range(n_xy):
                 out_ref[j, shard_rows:] = tile
 
@@ -208,7 +221,7 @@
             theta_ref[...] = jnp.broadcast_to(theta, theta_ref.shape)
             hu_a = share_of(got_ref)
             hu_a_ref[...] = hu_a
-            corr_a = correction(theta, hu_a, u_a_ref[...], diag_ref[meta_ref[0]])
+            corr_a = correction(theta, hu_a, u_a_ref[...], diag_ref[place(meta_ref)[0]])
             corr_a_ref[...] = corr_a
             corr_b_ref[...] = correction(theta, hu_b_ref[...], u_b_ref[...], diag_b_ref[...])
             left_matmul(meta_ref, env_ref, env2_ref, corr_a.astype(BF16), left_ref)
@@ -218,7 +231,7 @@
             theta_ref[...] = jnp.broadcast_to(theta, theta_ref.shape)
             u_a = one * u_a_ref[...] + two * corr_a_ref[...]
             hu_a = one * hu_a_ref[...] + two * share_of(got_ref)
-            corr_a = correction(theta, hu_a, u_a, diag_ref[meta_ref[0]])
+            corr_a = correction(theta, hu_a, u_a, diag_ref[place(meta_ref)[0]])
             u_a_out[...], hu_a_out[...], corr_a_out[...] = u_a, hu_a, corr_a
             u_b = one * u_b_ref[...] + two * corr_b_ref[...]
             hu_b = one * hu_b_ref[...] + two * hc_b_ref[...]
@@ -230,7 +243,7 @@
             line = jnp.sum(got_ref[...], axis=0, keepdims=True) * scale
             sums = [line[:, k : k + 1] for k in range(6)]
             one, two, _, lowest = projected(theta_ref[0:1, 0:1], sums)
-            c = meta_ref[0]
+            c = place(meta_ref)[0]
             out_ref[c] = one * u_a_ref[...] + two * corr_a_ref[...]
             out_ref[1 - c] = one * u_far_ref[...] + two * corr_far_ref[...]
             energy_ref[...] = lowest
@@ -244,61 +257,67 @@
         work = 4 * size * size * cols
 
         first, psi_a = call(
-            start_kernel,
-            [((n_z, 2 * sub + 8, cols), F32), a_out],
-            i_meta + [(psi, HBM), (diag.reshape(sectors, n_z, n_xy, sub, cols), HBM)],
-            [pltpu.VMEM(psi.shape, F32), pltpu.SemaphoreType.DMA((sectors + 1,))],
-        )
-
-        def swapped(env):
-            other = lax.dynamic_index_in_dim(env[0], 1 - core, 0, keepdims=False)
-            return lax.ppermute(other, "core", swap)
-
-        first, left_env = lax.optimization_barrier((first, left_env))
-        lefts = v(left_env, swapped(left_env))
+            start_kernel, [((n_z, sub + 8, cols), F32), a_out], i_meta + v(psi), (), START
+        )
+
+        def swapped(env, other):
+            give = lax.dynamic_slice(
+                env, (0, other, 0, 0), (1, 1, size, size), allow_negative_indices=False
+            )
+            return lax.ppermute(give.reshape(size, size), "core", swap)
+
+        first, left_env, other = lax.optimization_barrier((first, left_env, 1 - core))
+        lefts = v(left_env, swapped(left_env, other))
         first = a2a(first, "sec")
-        u_a, u_b, diag_b, left = call(
-            first_kernel, [a_out, b_out, b_out, left_out], i_meta + v(first, psi_a) + lefts, (), work
+        u_a, u_b, left = call(
+            first_kernel, [a_out, b_out, left_out], i_meta + v(first, psi_a) + lefts, (), work
         )
         left, right_env = lax.optimization_barrier((left, right_env))
-        rights = v(right_env, swapped(right_env))
-
-        def apply_right(left, kind):
+        rights = v(right_env, swapped(right_env, other))
+
+        def apply_right(left, kind=F32):
             moved = a2a(left, "sec")
             (partial,) = call(
                 right_kernel, [((n_xy, sub, size), kind)], i_meta + v(moved) + rights, (), work
             )
             return a2a(partial, XY)
 
-        def gather(payload):
+        def gather(payload, *more):
             payload = a2a(payload, CZ)
-            (payload,) = call(spread_kernel, [((n_xy, shard_rows + 8, cols), F32)], i_meta + v(payload))
-            return a2a(payload, XY)
+            payload, *more = call(
+                spread_kernel, [((n_xy, shard_rows + 8, cols), F32), *more], i_meta + v(payload)
+            )
+            return [a2a(payload, XY), *more]
 
         payload_out = ((2 * n_z, sub + 8, cols), F32)
-        got = apply_right(left, F32)
-        hu_b, payload = call(image_kernel, [b_out, payload_out], i_meta + v(got, u_b))
-        got = gather(payload)
+        got = apply_right(left)
+        hu_b, payload = call(
+            first_image_kernel,
+            [b_out, ((2 * n_z, 2 * sub + 8, cols), F32)],
+            i_meta + v(got, u_b, diag),
+        )
+        got, diag_b = gather(payload, b_out)
         hu_a, corr_a, corr_b, theta, left = call(
             begin_kernel,
             [a_out, a_out, b_out, tile_out, left_out],
             i_meta + v(got, u_a, u_b, hu_b, diag, diag_b) + lefts, (), work,
         )
         for _ in range(ITERS - 1):
-            got = apply_right(left, F32)
+            got = apply_right(left)
             hc_b, payload = call(
                 image_kernel, [b_out, payload_out], i_meta + v(got, u_b, corr_b, hu_b)
             )
-            got = gather(payload)
+            (got,) = gather(payload)
             u_a, corr_a, hu_a, u_b, corr_b, hu_b, theta, left = call(
                 update_kernel,
                 [a_out, a_out, a_out, b_out, b_out, b_out, tile_out, left_out],
                 i_meta + v(got, theta, u_a, corr_a, hu_a, u_b, corr_b, hu_b, hc_b, diag, diag_b) + lefts,
                 (), work,
             )
-        u_far = lax.ppermute(u_a, "core", swap)
-        corr_far = lax.ppermute(corr_a, "core", swap)
         got = apply_right(left, BF16)
+        got, u_send, corr_send = lax.optimization_barrier((got, u_a, corr_a))
+        u_far = lax.ppermute(u_send, "core", swap)
+        corr_far = lax.ppermute(corr_send, "core", swap)
         (sums,) = call(
             last_image_kernel, [((2 * n_z * n_xy, cols), F32)], i_meta + v(got, u_b, corr_b, hu_b)
         )

time: 230 us -> 220 us (0.957)
  blocking collectives: 148 us -> 185 us
  waiting for transfers between devices: 26.1 us -> 0.01 us
  local copies, waits for them, and re-layouts: 13.8 us -> 2.94 us
  starting transfers between devices: 20 us -> 10.1 us
    all_to_all x10 -> x12, blocking collectives: 148 us -> 185 us  [a2a(): return lax.all_to_all(array, axes, 0, 0, tiled=True)]
    all_to_all x2 -> x0, waiting for transfers between devices: 26.1 us -> none  [a2a(): return lax.all_to_all(array, axes, 0, 0, tiled=True)]
    all_to_all x2 -> x0, starting transfers between devices: 12.6 us -> none  [a2a(): return lax.all_to_all(array, axes, 0, 0, tiled=True)]
    unnamed x18 -> x8, local copies, waits for them, and re-layouts: 7.55 us -> 2.6 us
    another operation x1 -> x0, local copies, waits for them, and re-layouts: 2.7 us -> none  [per_device(): jnp.stack([core, lax.axis_index('sec'), lax.axis_index(XY)] + [block_dims...]
    ppermute x4, starting transfers between devices: 7.4 us -> 10.1 us  [the longest x1 5.09 us: per_device(): u_far = lax.ppermute(u_send, 'core', swap)]
  transfers between devices with their start and end apart: 6 -> 4, of which waited for: 2 -> 0; matrix products, arithmetic and copies ran while one was open for 0% -> 0% of each run, Pallas kernels for 1% -> 0%
where the time goes in v4:
time: 220 us; the launch traced here: 219 us
  blocking collectives  185 us (84%)
  Pallas kernels  19.7 us (9%)
  starting transfers between devices  10.1 us (5%)
  local copies, waits for them, and re-layouts  2.94 us (1%)
    all_to_all x12, blocking collectives, a2a(): return lax.all_to_all(array, axes, 0, 0, tiled=True)  185 us
    pallas_call x13, Pallas kernels, call(): pl.pallas_call(kernel, out_shape=[jax.ShapeDtypeStruct(s, d) for s, d in...  19.7 us
    ppermute x1, starting transfers between devices, per_device(): u_far = lax.ppermute(u_send, 'core', swap)  5.09 us
    ppermute x2, starting transfers between devices, swapped(): return lax.ppermute(give.reshape(size, size), 'core', swap)  4.96 us
  transfers between devices with their start and end apart: 4, of which 0 were waited for; matrix products, arithmetic and copies ran while one was open for 0% of the time, Pallas kernels for 0%

profile of v4, /device:TPU:1, one launch (start us, length us, event | category | flops | bytes accessed | tf_op | source)
XLA Modules:
  0.0 219.3 jit_solution(1894057241653534520)
XLA Ops:
  0.7 0.8 select_select_fusion.meta_ref
  1.4 0.0 copy-start.3
  1.4 1.2 copy-done.3
  2.7 0.0 copy-start
  2.7 1.0 shard_map.68
  3.7 1.2 copy-done
  4.8 0.2 dynamic-slice_bitcast_fusion.1
  5.0 3.3 %collective-permute-start = (bf16[1024,1024]{1,0:T(8,128)(2,1)S(1)}, bf16[1024,1024]{1,0:T(8,128)(2,1)S(1)}, u32[]{:S(2)}, u32[]{:S(2)}) collective-permute-start(bf16[1024,1024]{1,0:T(8,128)(2,1)S(1)} %dynamic-slice_bitcast_fusion.1), channel_id=1, source_target_pairs={{0,8},{8,0},{1,9},{9,1},{2,10},{10,2},{3,11},{11,3},{4,12},{12,4},... | collective-permute-start | bytes 6291464 | tf_op jit(solution)/shard_map/ppermute | solution.py:267
  8.3 13.4 %all_to_all.66.got_ref = f32[8,16,128]{2,1,0:T(8,128)S(1)} all-to-all(f32[8,16,128]{2,1,0:T(8,128)S(1)} %get-tuple-element.36), channel_id=1, replica_groups=mesh['y'=4,'x'=4,'core'=2,'sec'=8] {'sec'}, dimensions={0} | all-to-all | bytes 131072 | tf_op jit(solution)/shard_map/all_to_all | solution.py:66
  21.7 0.0 collective-permute-done.env2_ref
  21.7 0.0 copy-start.1
  21.7 2.0 shard_map.69
  23.7 0.2 copy-done.1
  23.9 0.2 dynamic-slice_bitcast_fusion
  24.1 1.6 collective-permute-start.1
  25.7 20.4 %all_to_all.67.moved_ref = bf16[8,2,128,128]{3,2,1,0:T(8,128)(2,1)S(1)} all-to-all(bf16[8,2,128,128]{3,2,1,0:T(8,128)(2,1)S(1)} %get-tuple-element.41), channel_id=1, replica_groups=mesh['y'=4,'x'=4,'core'=2,'sec'=8] {'sec'}, dimensions={0} | all-to-all | bytes 1048576 | tf_op jit(solution)/shard_map/all_to_all | solution.py:66
  46.1 0.0 copy-start.2
  46.1 0.0 collective-permute-done.1.got_ref
  46.1 2.1 shard_map.70
  48.2 17.2 %all_to_all.68.got_ref = f32[16,8,1024]{2,1,0:T(8,128)S(1)} all-to-all(f32[16,8,1024]{2,1,0:T(8,128)S(1)} %shard_map.70), channel_id=1, replica_groups=mesh['y'=4,'x'=4,'core'=2,'sec'=8] {'y','x'}, dimensions={0} | all-to-all | bytes 1048576 | tf_op jit(solution)/shard_map/all_to_all | solution.py:66
  65.4 0.0 copy-done.2
  65.4 0.6 shard_map.71
  66.0 12.6 %all_to_all.69.got_ref = f32[16,24,128]{2,1,0:T(8,128)S(1)} all-to-all(f32[16,24,128]{2,1,0:T(8,128)S(1)} %get-tuple-element.44), channel_id=1, replica_groups=mesh['y'=4,'x'=4,'core'=2,'sec'=8] {'core','sec'}, dimensions={0} | all-to-all | bytes 393216 | tf_op jit(solution)/shard_map/all_to_all | solution.py:66
  78.6 0.6 shard_map.72
  79.2 13.9 %all_to_all.70.got_ref = f32[16,72,128]{2,1,0:T(8,128)S(1)} all-to-all(f32[16,72,128]{2,1,0:T(8,128)S(1)} %get-tuple-element.45), channel_id=1, replica_groups=mesh['y'=4,'x'=4,'core'=2,'sec'=8] {'y','x'}, dimensions={0} | all-to-all | bytes 1179648 | tf_op jit(solution)/shard_map/all_to_all | solution.py:66
  93.1 2.0 shard_map.73
  95.1 21.1 %all_to_all.71.moved_ref = bf16[8,2,128,128]{3,2,1,0:T(8,128)(2,1)S(1)} all-to-all(bf16[8,2,128,128]{3,2,1,0:T(8,128)(2,1)S(1)} %get-tuple-element.49), channel_id=1, replica_groups=mesh['y'=4,'x'=4,'core'=2,'sec'=8] {'sec'}, dimensions={0} | all-to-all | bytes 1048576 | tf_op jit(solution)/shard_map/all_to_all | solution.py:66
  116.2 2.1 shard_map.74
  118.3 11.7 %all_to_all.72.got_ref = f32[16,8,1024]{2,1,0:T(8,128)S(1)} all-to-all(f32[16,8,1024]{2,1,0:T(8,128)S(1)} %shard_map.74), channel_id=1, replica_groups=mesh['y'=4,'x'=4,'core'=2,'sec'=8] {'y','x'}, dimensions={0} | all-to-all | bytes 1048576 | tf_op jit(solution)/shard_map/all_to_all | solution.py:66
  129.9 0.6 shard_map.75
  130.6 13.7 %all_to_all.73.got_ref = f32[16,16,128]{2,1,0:T(8,128)S(1)} all-to-all(f32[16,16,128]{2,1,0:T(8,128)S(1)} %get-tuple-element.51), channel_id=1, replica_groups=mesh['y'=4,'x'=4,'core'=2,'sec'=8] {'core','sec'}, dimensions={0} | all-to-all | bytes 262144 | tf_op jit(solution)/shard_map/all_to_all | solution.py:66
  144.2 0.6 shard_map.76
  144.9 13.7 %all_to_all.74.got_ref = f32[16,72,128]{2,1,0:T(8,128)S(1)} all-to-all(f32[16,72,128]{2,1,0:T(8,128)S(1)} %shard_map.76), channel_id=1, replica_groups=mesh['y'=4,'x'=4,'core'=2,'sec'=8] {'y','x'}, dimensions={0} | all-to-all | bytes 1179648 | tf_op jit(solution)/shard_map/all_to_all | solution.py:66
  158.6 2.9 %shard_map.77 = (f32[1024,128]{1,0:T(8,128)S(1)}, f32[1024,128]{1,0:T(8,128)S(1)}, f32[1024,128]{1,0:T(8,128)}, f32[8,1024]{1,0:T(8,128)S(1)}, f32[8,1024]{1,0:T...) custom-call(s32[4,2]{1,0:T(4,128)S(1)} %select_select_fusion.meta_ref, ...), custom_call_target="tpu_custom_call" | custom-call | flops 536870912 | bytes 9670688 | tf_op jit(solution)/shard_map/pallas_call | solution.py:26
  161.5 18.0 %all_to_all.75.moved_ref = bf16[8,2,128,128]{3,2,1,0:T(8,128)(2,1)S(1)} all-to-all(bf16[8,2,128,128]{3,2,1,0:T(8,128)(2,1)S(1)} %get-tuple-element.56), channel_id=1, replica_groups=mesh['y'=4,'x'=4,'core'=2,'sec'=8] {'sec'}, dimensions={0} | all-to-all | bytes 1048576 | tf_op jit(solution)/shard_map/all_to_all | solution.py:66
  179.5 2.1 shard_map.78
  181.6 11.1 %all_to_all.76.got_ref = bf16[16,8,1024]{2,1,0:T(8,128)(2,1)S(1)} all-to-all(bf16[16,8,1024]{2,1,0:T(8,128)(2,1)S(1)} %shard_map.78), channel_id=1, replica_groups=mesh['y'=4,'x'=4,'core'=2,'sec'=8] {'y','x'}, dimensions={0} | all-to-all | bytes 524288 | tf_op jit(solution)/shard_map/all_to_all | solution.py:66
  192.7 5.1 %collective-permute-start.2 = (f32[1024,128]{1,0:T(8,128)S(1)}, f32[1024,128]{1,0:T(8,128)S(1)}, u32[]{:S(2)}, u32[]{:S(2)}) collective-permute-start(f32[1024,128]{1,0:T(8,128)S(1)} %get-tuple-element.64.u_a_ref), channel_id=1, source_target_pairs={{0,8},{8,0},{1,9},{9,1},{2,10},{10,2},{3,11},{11,3},{4,12},{12,4},... | collective-permute-start | bytes 1572872 | tf_op jit(solution)/shard_map/ppermute | solution.py:319
  197.8 0.0 collective-permute-start.3
  197.8 0.7 shard_map.79
  198.5 18.4 %all_to_all.77 = f32[256,1,128]{2,1,0:T(1,128)S(1)} all-to-all(f32[256,1,128]{2,1,0:T(1,128)S(1)} %bitcast.10), channel_id=1, replica_groups=mesh['y'=4,'x'=4,'core'=2,'sec'=8] {'y','x','core','sec'}, dimensions={0} | all-to-all | bytes 262144 | tf_op jit(solution)/shard_map/all_to_all | solution.py:66
  216.9 0.0 collective-permute-done.2.u_far_ref
  216.9 0.0 collective-permute-done.3.corr_far_ref
  216.9 2.4 %shard_map.80 = (f32[2,1024,128]{2,1,0:T(8,128)}, f32[1,1]{1,0:T(1,128)}) custom-call(s32[4,2]{1,0:T(4,128)S(1)} %select_select_fusion.meta_ref, f32[256,128]{1,0:T(8,128)S(1)} %bitcast.9, f32[8,128]{1,0:T(8,128)S(1)} %get-tuple-element.63.theta_ref, f32[1024,128]{1,0:T(8,128)S(1)} %get-tuple-element.64.u_a_ref, ...), custom_call_target="tpu_custom_call" | custom-call | bytes 2232352 | tf_op jit(solution)/shard_map/pallas_call | solution.py:26
  (2 shorter events, 0.0 us)
Async XLA Ops:
  1.4 1.2 copy-start.3
  2.7 2.2 copy-start
  5.0 16.7 %collective-permute-start = (bf16[1024,1024]{1,0:T(8,128)(2,1)S(1)}, bf16[1024,1024]{1,0:T(8,128)(2,1)S(1)}, u32[]{:S(2)}, u32[]{:S(2)}) collective-permute-start(bf16[1024,1024]{1,0:T(8,128)(2,1)S(1)} %dynamic-slice_bitcast_fusion.1), channel_id=1, source_target_pairs={{0,8},{8,0},{1,9},{9,1},{2,10},{10,2},{3,11},{11,3},{4,12},{12,4},... | collective-permute-start | bytes 6291464 | tf_op jit(solution)/shard_map/ppermute | solution.py:267
  21.7 2.2 copy-start.1
  24.1 22.0 %collective-permute-start.1 = (bf16[1024,1024]{1,0:T(8,128)(2,1)S(1)}, bf16[1024,1024]{1,0:T(8,128)(2,1)S(1)}, u32[]{:S(2)}, u32[]{:S(2)}) collective-permute-start(bf16[1024,1024]{1,0:T(8,128)(2,1)S(1)} %dynamic-slice_bitcast_fusion), channel_id=1, source_target_pairs={{0,8},{8,0},{1,9},{9,1},{2,10},{10,2},{3,11},{11,3},{4,12},{12,4},... | collective-permute-start | bytes 6291464 | tf_op jit(solution)/shard_map/ppermute | solution.py:267
  46.1 19.2 %copy-start.2 = (f32[2,1024,128]{2,1,0:T(8,128)S(1)}, f32[2,1024,128]{2,1,0:T(8,128)}, u32[]{:S(2)}) copy-start(f32[2,1024,128]{2,1,0:T(8,128)} %diag_ref.5) | copy-start | bytes 3145732
  192.7 24.2 %collective-permute-start.2 = (f32[1024,128]{1,0:T(8,128)S(1)}, f32[1024,128]{1,0:T(8,128)S(1)}, u32[]{:S(2)}, u32[]{:S(2)}) collective-permute-start(f32[1024,128]{1,0:T(8,128)S(1)} %get-tuple-element.64.u_a_ref), channel_id=1, source_target_pairs={{0,8},{8,0},{1,9},{9,1},{2,10},{10,2},{3,11},{11,3},{4,12},{12,4},... | collective-permute-start | bytes 1572872 | tf_op jit(solution)/shard_map/ppermute | solution.py:319
  197.8 19.1 %collective-permute-start.3 = (f32[1024,128]{1,0:T(8,128)S(1)}, f32[1024,128]{1,0:T(8,128)S(1)}, u32[]{:S(2)}, u32[]{:S(2)}) collective-permute-start(f32[1024,128]{1,0:T(8,128)S(1)} %get-tuple-element.65.corr_a_ref), channel_id=1, source_target_pairs={{0,8},{8,0},{1,9},{9,1},{2,10},{10,2},{3,11},{11,3},{4,12},{12,4},... | collective-permute-start | bytes 1572872 | tf_op jit(solution)/shard_map/ppermute | solution.py:320

commit v5 on v4

--- a/solution.py
+++ b/solution.py
@@ -39,8 +39,16 @@
     return jnp.sum(functools.reduce(lambda a, b: a + b, parts), axis=0, keepdims=True)
 
 
-def tile_of(rows):
-    return jnp.concatenate(rows + [jnp.zeros((8 - len(rows), LANES), F32)], axis=0)
+def line_of(rows):
+    tile = jnp.concatenate(rows + [jnp.zeros((8 - len(rows), LANES), F32)], axis=0)
+    sums = jnp.sum(tile, axis=1, keepdims=True)
+    row = lax.broadcasted_iota(jnp.int32, tile.shape, 0)
+    lane = lax.broadcasted_iota(jnp.int32, tile.shape, 1)
+    return jnp.sum(jnp.where(row == lane, sums, 0.0), axis=0, keepdims=True)
+
+
+def add_rows(ref, start, step, count):
+    return functools.reduce(lambda a, b: a + b, [ref[pl.ds(start + step * k, 1)] for k in range(count)])
 
 
 def make(n_y, n_x, n_z):
@@ -50,6 +58,7 @@
         sectors, size, cols = psi.shape
         sub = cols // n_xy
         shard_rows = n_z * sub
+        one, two = sub + 1, 2 * sub + 1
         scale = 1.0 / (size * size)
         core = lax.axis_index("core")
         swap = [(0, 1), (1, 0)]
@@ -65,6 +74,10 @@
         def a2a(array, axes):
             return lax.all_to_all(array, axes, 0, 0, tiled=True)
 
+        def a2a_rows(array, parts, axes):
+            blocks = array.reshape(parts, array.shape[0] // parts, 1, cols)
+            return a2a(blocks, axes).reshape(array.shape)
+
         def dims_of(meta_ref, sector):
             return meta_ref[sector, 0], meta_ref[sector, 1]
 
@@ -91,8 +104,8 @@
                     psi_a_ref[...] = own
 
             for k in range(n_z):
-                out_ref[k, :sub] = psi_a_ref[own_rows(meta_ref, k)]
-                out_ref[k, sub:] = tile_of([total])
+                out_ref[pl.ds(k * one, sub)] = psi_a_ref[own_rows(meta_ref, k)]
+                out_ref[pl.ds(k * one + sub, 1)] = total
 
         def left_matmul(meta_ref, env_ref, got_ref, field, left_ref):
             core, per = place(meta_ref)[0], PIECE // cols
@@ -104,14 +117,13 @@
                     left_ref[i * per : (i + 1) * per, w] = part.astype(BF16).reshape(per, cols, cols)
 
         def first_kernel(meta_ref, got_ref, psi_a_ref, env_ref, env2_ref, u_a_ref, u_b_ref, left_ref):
-            got = got_ref[...]
-            norm = jnp.sum(jnp.sum(got[:, sub:], axis=0), axis=(0, 1), keepdims=True) * scale
+            norm = jnp.sum(add_rows(got_ref, sub, one, n_z), axis=1, keepdims=True) * scale
             inverse = 1.0 / jnp.sqrt(norm)
             u_a = psi_a_ref[...] * inverse
             u_a_ref[...] = u_a
             for k in range(n_z):
                 lanes = slice(k * cols, (k + 1) * cols)
-                u_b_ref[:, lanes] = got[k, :sub] * inverse
+                u_b_ref[:, lanes] = got_ref[pl.ds(k * one, sub)] * inverse
             left_matmul(meta_ref, env_ref, env2_ref, u_a.astype(BF16), left_ref)
 
         def right_pieces(meta_ref, moved_ref, env_ref, got_ref):
@@ -142,53 +154,58 @@
             rows, columns = dims_of(meta_ref, core)
             return jnp.where((row < rows) & (col < columns), image, 0.0)
 
-        def dots_tile(image, u_b_ref, more):
+        def dots_line(image, u_b_ref, more):
             u = u_b_ref[...]
             if not more:
-                return tile_of([fold(u * image)])
+                return line_of([fold(u * image)])
             corr, hu = more[0][...], more[1][...]
             pairs = [(u, image), (corr, hu), (corr, image), (u, corr), (corr, corr), (u, u)]
-            return tile_of([fold(a * b) for a, b in pairs])
-
-        def put_image(meta_ref, got_ref, u_b_ref, more, image_ref, out_ref):
+            return line_of([fold(a * b) for a, b in pairs])
+
+        def put_image(meta_ref, got_ref, u_b_ref, more, image_ref, out_ref, step):
             image = image_of(meta_ref, got_ref)
             image_ref[...] = image
-            tile = dots_tile(image, u_b_ref, more)
+            line = dots_line(image, u_b_ref, more)
             for k in range(n_z):
                 for c in range(2):
-                    out_ref[c * n_z + k, :sub] = image[:, k * cols : (k + 1) * cols]
-                    out_ref[c * n_z + k, sub : sub + 8] = tile
+                    first = (c * n_z + k) * step
+                    out_ref[pl.ds(first, sub)] = image[:, k * cols : (k + 1) * cols]
+                    out_ref[pl.ds(first + sub, 1)] = line
 
         def first_image_kernel(meta_ref, got_ref, u_b_ref, diag_ref, image_ref, out_ref):
-            put_image(meta_ref, got_ref, u_b_ref, (), image_ref, out_ref)
+            put_image(meta_ref, got_ref, u_b_ref, (), image_ref, out_ref, two)
             core = place(meta_ref)[0]
             for k in range(n_z):
-                out_ref[core * n_z + k, sub + 8 :] = diag_ref[core, own_rows(meta_ref, k)]
-                out_ref[(1 - core) * n_z + k, sub + 8 :] = jnp.zeros((sub, cols), F32)
+                rows = diag_ref[core, own_rows(meta_ref, k)]
+                for c in range(2):
+                    out_ref[pl.ds((c * n_z + k) * two + one, sub)] = rows
 
         def image_kernel(meta_ref, got_ref, u_b_ref, corr_b_ref, hu_b_ref, image_ref, out_ref):
-            put_image(meta_ref, got_ref, u_b_ref, (corr_b_ref, hu_b_ref), image_ref, out_ref)
+            put_image(meta_ref, got_ref, u_b_ref, (corr_b_ref, hu_b_ref), image_ref, out_ref, one)
 
         def last_image_kernel(meta_ref, got_ref, u_b_ref, corr_b_ref, hu_b_ref, out_ref):
             image = image_of(meta_ref, got_ref)
-            tile = dots_tile(image, u_b_ref, (corr_b_ref, hu_b_ref))
-            sums = jnp.sum(tile, axis=1, keepdims=True)
-            row = lax.broadcasted_iota(jnp.int32, tile.shape, 0)
-            lane = lax.broadcasted_iota(jnp.int32, tile.shape, 1)
-            line = jnp.sum(jnp.where(row == lane, sums, 0.0), axis=0, keepdims=True)
+            line = dots_line(image, u_b_ref, (corr_b_ref, hu_b_ref))
             out_ref[...] = jnp.broadcast_to(line, out_ref.shape)
 
         def spread_kernel(meta_ref, got_ref, out_ref, *diag_b_ref):
-            first = place(meta_ref)[0] * n_z
-            tile = jnp.sum(got_ref[:, sub : sub + 8], axis=0)
-            for k in range(n_z):
-                rows = got_ref[first + k, :sub]
+            core = place(meta_ref)[0]
+            step = two if diag_b_ref else one
+            full = shard_rows + 1
+
+            def mine(k, start):
+                rows = [got_ref[pl.ds((c * n_z + k) * step + start, sub)] for c in range(2)]
+                return jnp.where(core == 0, rows[0], rows[1])
+
+            line = add_rows(got_ref, sub, step, 2 * n_z)
+            for k in range(n_z):
+                rows = mine(k, 0)
                 for j in range(n_xy):
-                    out_ref[j, k * sub : (k + 1) * sub] = rows
+                    out_ref[pl.ds(j * full + k * sub, sub)] = rows
                 for ref in diag_b_ref:
-                    ref[:, k * cols : (k + 1) * cols] = got_ref[first + k, sub + 8 :]
+                    ref[:, k * cols : (k + 1) * cols] = mine(k, one)
             for j in range(n_xy):
-                out_ref[j, shard_rows:] = tile
+                out_ref[pl.ds(j * full + shard_rows, 1)] = line
 
         def projected(theta, sums):
             u_image, corr_hu, corr_image, project, size_corr, size_u = sums
@@ -205,16 +222,18 @@
             return x - y * project * inverse, y * inverse, theta, lowest
 
         def sums_of(got_ref, count):
-            tile = jnp.sum(got_ref[:, shard_rows:], axis=0)
-            sums = jnp.sum(tile, axis=1, keepdims=True) * scale
-            return [sums[k : k + 1] for k in range(count)]
+            line = add_rows(got_ref, shard_rows, shard_rows + 1, n_xy) * scale
+            return [line[:, k : k + 1] for k in range(count)]
 
         def correction(theta, image, vector, diagonal):
             return (image - theta * vector) / (1.0 + jnp.abs(diagonal - theta))
 
         def share_of(got_ref):
-            got = got_ref[:, :shard_rows].reshape(n_xy, n_z, sub, cols)
-            return jnp.transpose(got, (1, 0, 2, 3)).reshape(share)
+            parts = [
+                got_ref[pl.ds(j * (shard_rows + 1), shard_rows)].reshape(n_z, 1, sub, cols)
+                for j in range(n_xy)
+            ]
+            return jnp.concatenate(parts, axis=1).reshape(share)
 
         def begin_kernel(meta_ref, got_ref, u_a_ref, u_b_ref, hu_b_ref, diag_ref, diag_b_ref, env_ref, env2_ref, hu_a_ref, corr_a_ref, corr_b_ref, theta_ref, left_ref):
             (theta,) = sums_of(got_ref, 1)
@@ -227,14 +246,14 @@
             left_matmul(meta_ref, env_ref, env2_ref, corr_a.astype(BF16), left_ref)
 
         def update_kernel(meta_ref, got_ref, old_theta_ref, u_a_ref, corr_a_ref, hu_a_ref, u_b_ref, corr_b_ref, hu_b_ref, hc_b_ref, diag_ref, diag_b_ref, env_ref, env2_ref, u_a_out, corr_a_out, hu_a_out, u_b_out, corr_b_out, hu_b_out, theta_ref, left_ref):
-            one, two, theta, _ = projected(old_theta_ref[0:1, 0:1], sums_of(got_ref, 6))
+            old, new, theta, _ = projected(old_theta_ref[0:1, 0:1], sums_of(got_ref, 6))
             theta_ref[...] = jnp.broadcast_to(theta, theta_ref.shape)
-            u_a = one * u_a_ref[...] + two * corr_a_ref[...]
-            hu_a = one * hu_a_ref[...] + two * share_of(got_ref)
+            u_a = old * u_a_ref[...] + new * corr_a_ref[...]
+            hu_a = old * hu_a_ref[...] + new * share_of(got_ref)
             corr_a = correction(theta, hu_a, u_a, diag_ref[place(meta_ref)[0]])
             u_a_out[...], hu_a_out[...], corr_a_out[...] = u_a, hu_a, corr_a
-            u_b = one * u_b_ref[...] + two * corr_b_ref[...]
-            hu_b = one * hu_b_ref[...] + two * hc_b_ref[...]
+            u_b = old * u_b_ref[...] + new * corr_b_ref[...]
+            hu_b = old * hu_b_ref[...] + new * hc_b_ref[...]
             u_b_out[...], hu_b_out[...] = u_b, hu_b
             corr_b_out[...] = correction(theta, hu_b, u_b, diag_b_ref[...])
             left_matmul(meta_ref, env_ref, env2_ref, corr_a.astype(BF16), left_ref)
@@ -242,10 +261,10 @@
         def last_kernel(meta_ref, got_ref, theta_ref, u_a_ref, corr_a_ref, u_far_ref, corr_far_ref, out_ref, energy_ref):
             line = jnp.sum(got_ref[...], axis=0, keepdims=True) * scale
             sums = [line[:, k : k + 1] for k in range(6)]
-            one, two, _, lowest = projected(theta_ref[0:1, 0:1], sums)
+            old, new, _, lowest = projected(theta_ref[0:1, 0:1], sums)
             c = place(meta_ref)[0]
-            out_ref[c] = one * u_a_ref[...] + two * corr_a_ref[...]
-            out_ref[1 - c] = one * u_far_ref[...] + two * corr_far_ref[...]
+            out_ref[c] = old * u_a_ref[...] + new * corr_a_ref[...]
+            out_ref[1 - c] = old * u_far_ref[...] + new * corr_far_ref[...]
             energy_ref[...] = lowest
 
         def v(*arrays):
@@ -257,7 +276,7 @@
         work = 4 * size * size * cols
 
         first, psi_a = call(
-            start_kernel, [((n_z, sub + 8, cols), F32), a_out], i_meta + v(psi), (), START
+            start_kernel, [((n_z * one, cols), F32), a_out], i_meta + v(psi), (), START
         )
 
         def swapped(env, other):
@@ -268,7 +287,7 @@
 
         first, left_env, other = lax.optimization_barrier((first, left_env, 1 - core))
         lefts = v(left_env, swapped(left_env, other))
-        first = a2a(first, "sec")
+        first = a2a_rows(first, n_z, "sec")
         u_a, u_b, left = call(
             first_kernel, [a_out, b_out, left_out], i_meta + v(first, psi_a) + lefts, (), work
         )
@@ -283,17 +302,17 @@
             return a2a(partial, XY)
 
         def gather(payload, *more):
-            payload = a2a(payload, CZ)
+            payload = a2a_rows(payload, 2 * n_z, CZ)
             payload, *more = call(
-                spread_kernel, [((n_xy, shard_rows + 8, cols), F32), *more], i_meta + v(payload)
-            )
-            return [a2a(payload, XY), *more]
-
-        payload_out = ((2 * n_z, sub + 8, cols), F32)
+                spread_kernel, [((n_xy * (shard_rows + 1), cols), F32), *more], i_meta + v(payload)
+            )
+            return [a2a_rows(payload, n_xy, XY), *more]
+
+        payload_out = ((2 * n_z * one, cols), F32)
         got = apply_right(left)
         hu_b, payload = call(
             first_image_kernel,
-            [b_out, ((2 * n_z, 2 * sub + 8, cols), F32)],
+            [b_out, ((2 * n_z * two, cols), F32)],
             i_meta + v(got, u_b, diag),
         )
         got, diag_b = gather(payload, b_out)

time: 220 us -> 216 us (0.982)
  blocking collectives: 185 us -> 181 us
    all_to_all x12, blocking collectives: 185 us -> 181 us  [a2a(): return lax.all_to_all(array, axes, 0, 0, tiled=True)]
where the time goes in v5:
time: 216 us
  blocking collectives  181 us (84%)
  Pallas kernels  20.3 us (9%)
  starting transfers between devices  9.7 us (4%)
  local copies, waits for them, and re-layouts  2.99 us (1%)
    all_to_all x12, blocking collectives, a2a(): return lax.all_to_all(array, axes, 0, 0, tiled=True)  181 us
    pallas_call x13, Pallas kernels, call(): pl.pallas_call(kernel, out_shape=[jax.ShapeDtypeStruct(s, d) for s, d in...  20.3 us
    ppermute x2, starting transfers between devices, swapped(): return lax.ppermute(give.reshape(size, size), 'core', swap)  4.87 us
    ppermute x1, starting transfers between devices, per_device(): u_far = lax.ppermute(u_send, 'core', swap)  4.82 us
  transfers between devices with their start and end apart: 4, of which 0 were waited for; matrix products, arithmetic and copies ran while one was open for 0% of the time, Pallas kernels for 0%

profile of v5, /device:TPU:1, one launch (start us, length us, event | category | flops | bytes accessed | tf_op | source)
XLA Modules:
  0.0 215.6 jit_solution(14351219867102287441)
XLA Ops:
  0.7 0.8 select_select_fusion.meta_ref
  1.4 0.0 copy-start.3
  1.4 1.2 copy-done.3
  2.7 0.0 copy-start
  2.7 1.0 shard_map.68
  3.7 1.2 copy-done
  4.8 0.2 dynamic-slice_bitcast_fusion.1
  5.0 3.3 %collective-permute-start = (bf16[1024,1024]{1,0:T(8,128)(2,1)S(1)}, bf16[1024,1024]{1,0:T(8,128)(2,1)S(1)}, u32[]{:S(2)}, u32[]{:S(2)}) collective-permute-start(bf16[1024,1024]{1,0:T(8,128)(2,1)S(1)} %dynamic-slice_bitcast_fusion.1), channel_id=1, source_target_pairs={{0,8},{8,0},{1,9},{9,1},{2,10},{10,2},{3,11},{11,3},{4,12},{12,4},... | collective-permute-start | bytes 6291464 | tf_op jit(solution)/shard_map/ppermute | solution.py:286
  8.3 13.2 %all_to_all.66 = f32[8,9,1,128]{3,2,1,0:T(1,128)S(1)} all-to-all(f32[8,9,1,128]{3,2,1,0:T(1,128)S(1)} %bitcast.30), channel_id=1, replica_groups=mesh['y'=4,'x'=4,'core'=2,'sec'=8] {'sec'}, dimensions={0} | all-to-all | bytes 73728 | tf_op jit(solution)/shard_map/all_to_all | solution.py:75
  21.5 0.0 collective-permute-done.env2_ref
  21.5 0.0 copy-start.1
  21.5 1.9 shard_map.69
  23.4 0.3 copy-done.1
  23.7 0.2 dynamic-slice_bitcast_fusion
  23.9 1.5 collective-permute-start.1
  25.4 20.4 %all_to_all.67.moved_ref = bf16[8,2,128,128]{3,2,1,0:T(8,128)(2,1)S(1)} all-to-all(bf16[8,2,128,128]{3,2,1,0:T(8,128)(2,1)S(1)} %get-tuple-element.41), channel_id=1, replica_groups=mesh['y'=4,'x'=4,'core'=2,'sec'=8] {'sec'}, dimensions={0} | all-to-all | bytes 1048576 | tf_op jit(solution)/shard_map/all_to_all | solution.py:75
  45.8 0.0 copy-start.2
  45.8 0.0 collective-permute-done.1.got_ref
  45.8 2.1 shard_map.70
  47.9 17.2 %all_to_all.68.got_ref = f32[16,8,1024]{2,1,0:T(8,128)S(1)} all-to-all(f32[16,8,1024]{2,1,0:T(8,128)S(1)} %shard_map.70), channel_id=1, replica_groups=mesh['y'=4,'x'=4,'core'=2,'sec'=8] {'y','x'}, dimensions={0} | all-to-all | bytes 1048576 | tf_op jit(solution)/shard_map/all_to_all | solution.py:75
  65.1 0.0 copy-done.2
  65.1 0.7 shard_map.71
  65.8 11.7 %all_to_all.69 = f32[16,17,1,128]{3,2,1,0:T(1,128)S(1)} all-to-all(f32[16,17,1,128]{3,2,1,0:T(1,128)S(1)} %bitcast.28), channel_id=1, replica_groups=mesh['y'=4,'x'=4,'core'=2,'sec'=8] {'core','sec'}, dimensions={0} | all-to-all | bytes 278528 | tf_op jit(solution)/shard_map/all_to_all | solution.py:75
  77.5 0.6 shard_map.72
  78.1 13.4 %all_to_all.70 = f32[16,65,1,128]{3,2,1,0:T(1,128)S(1)} all-to-all(f32[16,65,1,128]{3,2,1,0:T(1,128)S(1)} %bitcast.23), channel_id=1, replica_groups=mesh['y'=4,'x'=4,'core'=2,'sec'=8] {'y','x'}, dimensions={0} | all-to-all | bytes 1064960 | tf_op jit(solution)/shard_map/all_to_all | solution.py:75
  91.5 2.0 shard_map.73
  93.5 18.3 %all_to_all.71.moved_ref = bf16[8,2,128,128]{3,2,1,0:T(8,128)(2,1)S(1)} all-to-all(bf16[8,2,128,128]{3,2,1,0:T(8,128)(2,1)S(1)} %get-tuple-element.49), channel_id=1, replica_groups=mesh['y'=4,'x'=4,'core'=2,'sec'=8] {'sec'}, dimensions={0} | all-to-all | bytes 1048576 | tf_op jit(solution)/shard_map/all_to_all | solution.py:75
  111.8 2.1 shard_map.74
  113.8 12.5 %all_to_all.72.got_ref = f32[16,8,1024]{2,1,0:T(8,128)S(1)} all-to-all(f32[16,8,1024]{2,1,0:T(8,128)S(1)} %shard_map.74), channel_id=1, replica_groups=mesh['y'=4,'x'=4,'core'=2,'sec'=8] {'y','x'}, dimensions={0} | all-to-all | bytes 1048576 | tf_op jit(solution)/shard_map/all_to_all | solution.py:75
  126.4 0.7 shard_map.75
  127.1 14.5 %all_to_all.73 = f32[16,9,1,128]{3,2,1,0:T(1,128)S(1)} all-to-all(f32[16,9,1,128]{3,2,1,0:T(1,128)S(1)} %bitcast.29), channel_id=1, replica_groups=mesh['y'=4,'x'=4,'core'=2,'sec'=8] {'core','sec'}, dimensions={0} | all-to-all | bytes 147456 | tf_op jit(solution)/shard_map/all_to_all | solution.py:75
  141.5 0.6 shard_map.76
  142.2 13.7 %all_to_all.74 = f32[16,65,1,128]{3,2,1,0:T(1,128)S(1)} all-to-all(f32[16,65,1,128]{3,2,1,0:T(1,128)S(1)} %bitcast.21), channel_id=1, replica_groups=mesh['y'=4,'x'=4,'core'=2,'sec'=8] {'y','x'}, dimensions={0} | all-to-all | bytes 1064960 | tf_op jit(solution)/shard_map/all_to_all | solution.py:75
  155.8 3.3 %shard_map.77 = (f32[1024,128]{1,0:T(8,128)S(1)}, f32[1024,128]{1,0:T(8,128)S(1)}, f32[1024,128]{1,0:T(8,128)}, f32[8,1024]{1,0:T(8,128)S(1)}, f32[8,1024]{1,0:T...) custom-call(s32[4,2]{1,0:T(4,128)S(1)} %select_select_fusion.meta_ref, ...), custom_call_target="tpu_custom_call" | custom-call | flops 536870912 | bytes 9613344 | tf_op jit(solution)/shard_map/pallas_call | solution.py:26
  159.2 17.0 %all_to_all.75.moved_ref = bf16[8,2,128,128]{3,2,1,0:T(8,128)(2,1)S(1)} all-to-all(bf16[8,2,128,128]{3,2,1,0:T(8,128)(2,1)S(1)} %get-tuple-element.56), channel_id=1, replica_groups=mesh['y'=4,'x'=4,'core'=2,'sec'=8] {'sec'}, dimensions={0} | all-to-all | bytes 1048576 | tf_op jit(solution)/shard_map/all_to_all | solution.py:75
  176.2 2.1 shard_map.78
  178.2 11.0 %all_to_all.76.got_ref = bf16[16,8,1024]{2,1,0:T(8,128)(2,1)S(1)} all-to-all(bf16[16,8,1024]{2,1,0:T(8,128)(2,1)S(1)} %shard_map.78), channel_id=1, replica_groups=mesh['y'=4,'x'=4,'core'=2,'sec'=8] {'y','x'}, dimensions={0} | all-to-all | bytes 524288 | tf_op jit(solution)/shard_map/all_to_all | solution.py:75
  189.3 4.8 %collective-permute-start.2 = (f32[1024,128]{1,0:T(8,128)S(1)}, f32[1024,128]{1,0:T(8,128)S(1)}, u32[]{:S(2)}, u32[]{:S(2)}) collective-permute-start(f32[1024,128]{1,0:T(8,128)S(1)} %get-tuple-element.64.u_a_ref), channel_id=1, source_target_pairs={{0,8},{8,0},{1,9},{9,1},{2,10},{10,2},{3,11},{11,3},{4,12},{12,4},... | collective-permute-start | bytes 1572872 | tf_op jit(solution)/shard_map/ppermute | solution.py:338
  194.1 0.0 collective-permute-start.3
  194.1 0.7 shard_map.79
  194.8 18.4 %all_to_all.77 = f32[256,1,128]{2,1,0:T(1,128)S(1)} all-to-all(f32[256,1,128]{2,1,0:T(1,128)S(1)} %bitcast.25), channel_id=1, replica_groups=mesh['y'=4,'x'=4,'core'=2,'sec'=8] {'y','x','core','sec'}, dimensions={0} | all-to-all | bytes 262144 | tf_op jit(solution)/shard_map/all_to_all | solution.py:75
  213.2 0.0 collective-permute-done.2.u_far_ref
  213.2 0.0 collective-permute-done.3.corr_far_ref
  213.2 2.4 %shard_map.80 = (f32[2,1024,128]{2,1,0:T(8,128)}, f32[1,1]{1,0:T(1,128)}) custom-call(s32[4,2]{1,0:T(4,128)S(1)} %select_select_fusion.meta_ref, f32[256,128]{1,0:T(8,128)S(1)} %bitcast.24, f32[8,128]{1,0:T(8,128)S(1)} %get-tuple-element.63.theta_ref, f32[1024,128]{1,0:T(8,128)S(1)} %get-tuple-element.64.u_a_ref, ...), custom_call_target="tpu_custom_call" | custom-call | bytes 2232352 | tf_op jit(solution)/shard_map/pallas_call | solution.py:26
  (2 shorter events, 0.0 us)
Async XLA Ops:
  1.4 1.2 copy-start.3
  2.7 2.2 %copy-start = (bf16[1,2,1024,1024]{3,2,1,0:T(8,128)(2,1)S(1)}, bf16[1,2,1024,1024]{3,2,1,0:T(8,128)(2,1)}, u32[]{:S(2)}) copy-start(bf16[1,2,1024,1024]{3,2,1,0:T(8,128)(2,1)} %env_ref.4) | copy-start | bytes 12582916
  5.0 16.5 %collective-permute-start = (bf16[1024,1024]{1,0:T(8,128)(2,1)S(1)}, bf16[1024,1024]{1,0:T(8,128)(2,1)S(1)}, u32[]{:S(2)}, u32[]{:S(2)}) collective-permute-start(bf16[1024,1024]{1,0:T(8,128)(2,1)S(1)} %dynamic-slice_bitcast_fusion.1), channel_id=1, source_target_pairs={{0,8},{8,0},{1,9},{9,1},{2,10},{10,2},{3,11},{11,3},{4,12},{12,4},... | collective-permute-start | bytes 6291464 | tf_op jit(solution)/shard_map/ppermute | solution.py:286
  21.5 2.2 %copy-start.1 = (bf16[1,2,1024,1024]{3,2,1,0:T(8,128)(2,1)S(1)}, bf16[1,2,1024,1024]{3,2,1,0:T(8,128)(2,1)}, u32[]{:S(2)}) copy-start(bf16[1,2,1024,1024]{3,2,1,0:T(8,128)(2,1)} %env_ref.5) | copy-start | bytes 12582916
  23.9 22.0 %collective-permute-start.1 = (bf16[1024,1024]{1,0:T(8,128)(2,1)S(1)}, bf16[1024,1024]{1,0:T(8,128)(2,1)S(1)}, u32[]{:S(2)}, u32[]{:S(2)}) collective-permute-start(bf16[1024,1024]{1,0:T(8,128)(2,1)S(1)} %dynamic-slice_bitcast_fusion), channel_id=1, source_target_pairs={{0,8},{8,0},{1,9},{9,1},{2,10},{10,2},{3,11},{11,3},{4,12},{12,4},... | collective-permute-start | bytes 6291464 | tf_op jit(solution)/shard_map/ppermute | solution.py:286
  45.8 19.3 %copy-start.2 = (f32[2,1024,128]{2,1,0:T(8,128)S(1)}, f32[2,1024,128]{2,1,0:T(8,128)}, u32[]{:S(2)}) copy-start(f32[2,1024,128]{2,1,0:T(8,128)} %diag_ref.5) | copy-start | bytes 3145732
  189.3 24.0 %collective-permute-start.2 = (f32[1024,128]{1,0:T(8,128)S(1)}, f32[1024,128]{1,0:T(8,128)S(1)}, u32[]{:S(2)}, u32[]{:S(2)}) collective-permute-start(f32[1024,128]{1,0:T(8,128)S(1)} %get-tuple-element.64.u_a_ref), channel_id=1, source_target_pairs={{0,8},{8,0},{1,9},{9,1},{2,10},{10,2},{3,11},{11,3},{4,12},{12,4},... | collective-permute-start | bytes 1572872 | tf_op jit(solution)/shard_map/ppermute | solution.py:338
  194.1 19.1 %collective-permute-start.3 = (f32[1024,128]{1,0:T(8,128)S(1)}, f32[1024,128]{1,0:T(8,128)S(1)}, u32[]{:S(2)}, u32[]{:S(2)}) collective-permute-start(f32[1024,128]{1,0:T(8,128)S(1)} %get-tuple-element.65.corr_a_ref), channel_id=1, source_target_pairs={{0,8},{8,0},{1,9},{9,1},{2,10},{10,2},{3,11},{11,3},{4,12},{12,4},... | collective-permute-start | bytes 1572872 | tf_op jit(solution)/shard_map/ppermute | solution.py:339

commit v6 on v5

--- a/solution.py
+++ b/solution.py
@@ -12,7 +12,8 @@
 CZ = ("core", "sec")
 ALL = ("y", "x", "core", "sec")
 LANES = 128
-PIECE = 256
+PIECE = 1024
+BROWS = 16
 LIMIT = 24
 START = 4 * 10**9
 F32 = jnp.float32
@@ -188,24 +189,31 @@
             line = dots_line(image, u_b_ref, (corr_b_ref, hu_b_ref))
             out_ref[...] = jnp.broadcast_to(line, out_ref.shape)
 
-        def spread_kernel(meta_ref, got_ref, out_ref, *diag_b_ref):
-            core = place(meta_ref)[0]
-            step = two if diag_b_ref else one
+        def mine(meta_ref, got_ref, k, step, start):
+            rows = [got_ref[pl.ds((c * n_z + k) * step + start, sub)] for c in range(2)]
+            return jnp.where(place(meta_ref)[0] == 0, rows[0], rows[1])
+
+        def first_spread_kernel(meta_ref, got_ref, out_ref, diag_b_ref):
             full = shard_rows + 1
-
-            def mine(k, start):
-                rows = [got_ref[pl.ds((c * n_z + k) * step + start, sub)] for c in range(2)]
-                return jnp.where(core == 0, rows[0], rows[1])
-
-            line = add_rows(got_ref, sub, step, 2 * n_z)
-            for k in range(n_z):
-                rows = mine(k, 0)
+            line = add_rows(got_ref, sub, two, 2 * n_z)
+            for k in range(n_z):
+                rows = mine(meta_ref, got_ref, k, two, 0)
                 for j in range(n_xy):
                     out_ref[pl.ds(j * full + k * sub, sub)] = rows
-                for ref in diag_b_ref:
-                    ref[:, k * cols : (k + 1) * cols] = mine(k, one)
+                diag_b_ref[:, k * cols : (k + 1) * cols] = mine(meta_ref, got_ref, k, two, one)
             for j in range(n_xy):
                 out_ref[pl.ds(j * full + shard_rows, 1)] = line
+
+        def spread_kernel(meta_ref, got_ref, out_ref):
+            line = add_rows(got_ref, sub, one, 2 * n_z)
+            pieces = []
+            for _ in range(3):
+                pieces.append(line.astype(BF16).astype(F32))
+                line = line - pieces[-1]
+            pieces.append(jnp.zeros((BROWS - 3, cols), F32))
+            rows = [mine(meta_ref, got_ref, k, one, 0) for k in range(n_z)]
+            block = jnp.concatenate(rows + pieces, axis=0).astype(BF16)
+            out_ref[...] = jnp.broadcast_to(block[None], out_ref.shape)
 
         def projected(theta, sums):
             u_image, corr_hu, corr_image, project, size_corr, size_u = sums
@@ -221,37 +229,36 @@
             theta = x * x * theta + 2.0 * x * y * cross + y * y * corner
             return x - y * project * inverse, y * inverse, theta, lowest
 
-        def sums_of(got_ref, count):
-            line = add_rows(got_ref, shard_rows, shard_rows + 1, n_xy) * scale
-            return [line[:, k : k + 1] for k in range(count)]
-
         def correction(theta, image, vector, diagonal):
             return (image - theta * vector) / (1.0 + jnp.abs(diagonal - theta))
 
-        def share_of(got_ref):
-            parts = [
-                got_ref[pl.ds(j * (shard_rows + 1), shard_rows)].reshape(n_z, 1, sub, cols)
-                for j in range(n_xy)
-            ]
+        def share_of(parts):
+            parts = [part.reshape(n_z, 1, sub, cols) for part in parts]
             return jnp.concatenate(parts, axis=1).reshape(share)
 
         def begin_kernel(meta_ref, got_ref, u_a_ref, u_b_ref, hu_b_ref, diag_ref, diag_b_ref, env_ref, env2_ref, hu_a_ref, corr_a_ref, corr_b_ref, theta_ref, left_ref):
-            (theta,) = sums_of(got_ref, 1)
+            full = shard_rows + 1
+            theta = add_rows(got_ref, shard_rows, full, n_xy)[:, :1] * scale
             theta_ref[...] = jnp.broadcast_to(theta, theta_ref.shape)
-            hu_a = share_of(got_ref)
+            hu_a = share_of([got_ref[pl.ds(j * full, shard_rows)] for j in range(n_xy)])
             hu_a_ref[...] = hu_a
             corr_a = correction(theta, hu_a, u_a_ref[...], diag_ref[place(meta_ref)[0]])
             corr_a_ref[...] = corr_a
             corr_b_ref[...] = correction(theta, hu_b_ref[...], u_b_ref[...], diag_b_ref[...])
             left_matmul(meta_ref, env_ref, env2_ref, corr_a.astype(BF16), left_ref)
 
-        def update_kernel(meta_ref, got_ref, old_theta_ref, u_a_ref, corr_a_ref, hu_a_ref, u_b_ref, corr_b_ref, hu_b_ref, hc_b_ref, diag_ref, diag_b_ref, env_ref, env2_ref, u_a_out, corr_a_out, hu_a_out, u_b_out, corr_b_out, hu_b_out, theta_ref, left_ref):
-            old, new, theta, _ = projected(old_theta_ref[0:1, 0:1], sums_of(got_ref, 6))
+        def update_kernel(meta_ref, got_ref, old_theta_ref, u_a_ref, corr_a_ref, hu_a_ref, u_b_ref, corr_b_ref, hu_b_ref, hc_b_ref, diag_ref, diag_b_ref, env_ref, env2_ref, u_a_out, corr_a_out, u_b_out, corr_b_out, hu_b_out, theta_ref, left_ref, *hu_a_out):
+            lines = jnp.sum(got_ref[:, shard_rows:].astype(F32), axis=0)
+            line = jnp.sum(lines, axis=0, keepdims=True) * scale
+            sums = [line[:, k : k + 1] for k in range(6)]
+            old, new, theta, _ = projected(old_theta_ref[0:1, 0:1], sums)
             theta_ref[...] = jnp.broadcast_to(theta, theta_ref.shape)
             u_a = old * u_a_ref[...] + new * corr_a_ref[...]
-            hu_a = old * hu_a_ref[...] + new * share_of(got_ref)
+            hu_a = old * hu_a_ref[...] + new * share_of([got_ref[j, :shard_rows].astype(F32) for j in range(n_xy)])
             corr_a = correction(theta, hu_a, u_a, diag_ref[place(meta_ref)[0]])
-            u_a_out[...], hu_a_out[...], corr_a_out[...] = u_a, hu_a, corr_a
+            u_a_out[...], corr_a_out[...] = u_a, corr_a
+            for ref in hu_a_out:
+                ref[...] = hu_a
             u_b = old * u_b_ref[...] + new * corr_b_ref[...]
             hu_b = old * hu_b_ref[...] + new * hc_b_ref[...]
             u_b_out[...], hu_b_out[...] = u_b, hu_b
@@ -263,9 +270,9 @@
             sums = [line[:, k : k + 1] for k in range(6)]
             old, new, _, lowest = projected(theta_ref[0:1, 0:1], sums)
             c = place(meta_ref)[0]
+            energy_ref[...] = lowest
             out_ref[c] = old * u_a_ref[...] + new * corr_a_ref[...]
             out_ref[1 - c] = old * u_far_ref[...] + new * corr_far_ref[...]
-            energy_ref[...] = lowest
 
         def v(*arrays):
             return [(a, VMEM) for a in arrays]
@@ -300,13 +307,6 @@
                 right_kernel, [((n_xy, sub, size), kind)], i_meta + v(moved) + rights, (), work
             )
             return a2a(partial, XY)
-
-        def gather(payload, *more):
-            payload = a2a_rows(payload, 2 * n_z, CZ)
-            payload, *more = call(
-                spread_kernel, [((n_xy * (shard_rows + 1), cols), F32), *more], i_meta + v(payload)
-            )
-            return [a2a_rows(payload, n_xy, XY), *more]
 
         payload_out = ((2 * n_z * one, cols), F32)
         got = apply_right(left)
@@ -315,24 +315,36 @@
             [b_out, ((2 * n_z * two, cols), F32)],
             i_meta + v(got, u_b, diag),
         )
-        got, diag_b = gather(payload, b_out)
+        payload, diag_b = call(
+            first_spread_kernel,
+            [((n_xy * (shard_rows + 1), cols), F32), b_out],
+            i_meta + v(a2a_rows(payload, 2 * n_z, CZ)),
+        )
+        got = a2a_rows(payload, n_xy, XY)
         hu_a, corr_a, corr_b, theta, left = call(
             begin_kernel,
             [a_out, a_out, b_out, tile_out, left_out],
             i_meta + v(got, u_a, u_b, hu_b, diag, diag_b) + lefts, (), work,
         )
-        for _ in range(ITERS - 1):
+        for step in range(ITERS - 1):
             got = apply_right(left)
             hc_b, payload = call(
                 image_kernel, [b_out, payload_out], i_meta + v(got, u_b, corr_b, hu_b)
             )
-            (got,) = gather(payload)
-            u_a, corr_a, hu_a, u_b, corr_b, hu_b, theta, left = call(
+            (payload,) = call(
+                spread_kernel,
+                [((n_xy, shard_rows + BROWS, cols), BF16)],
+                i_meta + v(a2a_rows(payload, 2 * n_z, CZ)),
+            )
+            got = a2a(payload, XY)
+            more = [a_out] * (step < ITERS - 2)
+            u_a, corr_a, u_b, corr_b, hu_b, theta, left, *more = call(
                 update_kernel,
-                [a_out, a_out, a_out, b_out, b_out, b_out, tile_out, left_out],
+                [a_out, a_out, b_out, b_out, b_out, tile_out, left_out] + more,
                 i_meta + v(got, theta, u_a, corr_a, hu_a, u_b, corr_b, hu_b, hc_b, diag, diag_b) + lefts,
                 (), work,
             )
+            (hu_a,) = more or (None,)
         got = apply_right(left, BF16)
         got, u_send, corr_send = lax.optimization_barrier((got, u_a, corr_a))
         u_far = lax.ppermute(u_send, "core", swap)

time: 216 us -> 213 us (0.986)
    all_to_all x12, blocking collectives: 181 us -> 179 us  [a2a(): return lax.all_to_all(array, axes, 0, 0, tiled=True)]
where the time goes in v6:
time: 213 us; the launch traced here: 212 us
  blocking collectives  179 us (84%)
  Pallas kernels  19.4 us (9%)
  starting transfers between devices  9.59 us (5%)
  local copies, waits for them, and re-layouts  2.99 us (1%)
    all_to_all x12, blocking collectives, a2a(): return lax.all_to_all(array, axes, 0, 0, tiled=True)  179 us
    pallas_call x13, Pallas kernels, call(): pl.pallas_call(kernel, out_shape=[jax.ShapeDtypeStruct(s, d) for s, d in...  19.4 us
    ppermute x2, starting transfers between devices, swapped(): return lax.ppermute(give.reshape(size, size), 'core', swap)  4.87 us
    ppermute x1, starting transfers between devices, per_device(): u_far = lax.ppermute(u_send, 'core', swap)  4.72 us
  transfers between devices with their start and end apart: 4, of which 0 were waited for; matrix products, arithmetic and copies ran while one was open for 0% of the time, Pallas kernels for 0%

profile of v6, /device:TPU:1, one launch (start us, length us, event | category | flops | bytes accessed | tf_op | source)
XLA Modules:
  0.0 212.2 jit_solution(18358340639252573582)
XLA Ops:
  0.7 0.8 select_select_fusion.meta_ref
  1.4 0.0 copy-start.3
  1.4 1.2 copy-done.3
  2.7 0.0 copy-start
  2.7 1.0 shard_map.68
  3.7 1.2 copy-done
  4.8 0.2 dynamic-slice_bitcast_fusion.1
  5.0 3.3 %collective-permute-start = (bf16[1024,1024]{1,0:T(8,128)(2,1)S(1)}, bf16[1024,1024]{1,0:T(8,128)(2,1)S(1)}, u32[]{:S(2)}, u32[]{:S(2)}) collective-permute-start(bf16[1024,1024]{1,0:T(8,128)(2,1)S(1)} %dynamic-slice_bitcast_fusion.1), channel_id=1, source_target_pairs={{0,8},{8,0},{1,9},{9,1},{2,10},{10,2},{3,11},{11,3},{4,12},{12,4},... | collective-permute-start | bytes 6291464 | tf_op jit(solution)/shard_map/ppermute | solution.py:293
  8.3 13.2 %all_to_all.66 = f32[8,9,1,128]{3,2,1,0:T(1,128)S(1)} all-to-all(f32[8,9,1,128]{3,2,1,0:T(1,128)S(1)} %bitcast.26), channel_id=1, replica_groups=mesh['y'=4,'x'=4,'core'=2,'sec'=8] {'sec'}, dimensions={0} | all-to-all | bytes 73728 | tf_op jit(solution)/shard_map/all_to_all | solution.py:76
  21.5 0.0 collective-permute-done.env2_ref
  21.5 0.0 copy-start.1
  21.5 1.9 shard_map.69
  23.4 0.3 copy-done.1
  23.7 0.2 dynamic-slice_bitcast_fusion
  23.9 1.5 collective-permute-start.1
  25.4 20.4 %all_to_all.67.moved_ref = bf16[8,2,128,128]{3,2,1,0:T(8,128)(2,1)S(1)} all-to-all(bf16[8,2,128,128]{3,2,1,0:T(8,128)(2,1)S(1)} %get-tuple-element.41), channel_id=1, replica_groups=mesh['y'=4,'x'=4,'core'=2,'sec'=8] {'sec'}, dimensions={0} | all-to-all | bytes 1048576 | tf_op jit(solution)/shard_map/all_to_all | solution.py:76
  45.8 0.0 copy-start.2
  45.8 0.0 collective-permute-done.1.got_ref
  45.8 2.0 shard_map.70
  47.9 17.2 %all_to_all.68.got_ref = f32[16,8,1024]{2,1,0:T(8,128)S(1)} all-to-all(f32[16,8,1024]{2,1,0:T(8,128)S(1)} %shard_map.70), channel_id=1, replica_groups=mesh['y'=4,'x'=4,'core'=2,'sec'=8] {'y','x'}, dimensions={0} | all-to-all | bytes 1048576 | tf_op jit(solution)/shard_map/all_to_all | solution.py:76
  65.1 0.0 copy-done.2
  65.1 0.7 shard_map.71
  65.8 11.7 %all_to_all.69 = f32[16,17,1,128]{3,2,1,0:T(1,128)S(1)} all-to-all(f32[16,17,1,128]{3,2,1,0:T(1,128)S(1)} %bitcast.24), channel_id=1, replica_groups=mesh['y'=4,'x'=4,'core'=2,'sec'=8] {'core','sec'}, dimensions={0} | all-to-all | bytes 278528 | tf_op jit(solution)/shard_map/all_to_all | solution.py:76
  77.4 0.6 shard_map.72
  78.1 13.4 %all_to_all.70 = f32[16,65,1,128]{3,2,1,0:T(1,128)S(1)} all-to-all(f32[16,65,1,128]{3,2,1,0:T(1,128)S(1)} %bitcast.19), channel_id=1, replica_groups=mesh['y'=4,'x'=4,'core'=2,'sec'=8] {'y','x'}, dimensions={0} | all-to-all | bytes 1064960 | tf_op jit(solution)/shard_map/all_to_all | solution.py:76
  91.5 1.9 shard_map.73
  93.4 18.3 %all_to_all.71.moved_ref = bf16[8,2,128,128]{3,2,1,0:T(8,128)(2,1)S(1)} all-to-all(bf16[8,2,128,128]{3,2,1,0:T(8,128)(2,1)S(1)} %get-tuple-element.49), channel_id=1, replica_groups=mesh['y'=4,'x'=4,'core'=2,'sec'=8] {'sec'}, dimensions={0} | all-to-all | bytes 1048576 | tf_op jit(solution)/shard_map/all_to_all | solution.py:76
  111.7 2.0 shard_map.74
  113.7 12.5 %all_to_all.72.got_ref = f32[16,8,1024]{2,1,0:T(8,128)S(1)} all-to-all(f32[16,8,1024]{2,1,0:T(8,128)S(1)} %shard_map.74), channel_id=1, replica_groups=mesh['y'=4,'x'=4,'core'=2,'sec'=8] {'y','x'}, dimensions={0} | all-to-all | bytes 1048576 | tf_op jit(solution)/shard_map/all_to_all | solution.py:76
  126.2 0.7 shard_map.75
  126.9 14.5 %all_to_all.73 = f32[16,9,1,128]{3,2,1,0:T(1,128)S(1)} all-to-all(f32[16,9,1,128]{3,2,1,0:T(1,128)S(1)} %bitcast.25), channel_id=1, replica_groups=mesh['y'=4,'x'=4,'core'=2,'sec'=8] {'core','sec'}, dimensions={0} | all-to-all | bytes 147456 | tf_op jit(solution)/shard_map/all_to_all | solution.py:76
  141.4 0.6 shard_map.76
  142.0 10.8 %all_to_all.74.got_ref = bf16[16,80,128]{2,1,0:T(8,128)(2,1)S(1)} all-to-all(bf16[16,80,128]{2,1,0:T(8,128)(2,1)S(1)} %shard_map.76), channel_id=1, replica_groups=mesh['y'=4,'x'=4,'core'=2,'sec'=8] {'y','x'}, dimensions={0} | all-to-all | bytes 655360 | tf_op jit(solution)/shard_map/all_to_all | solution.py:76
  152.8 2.6 %shard_map.77 = (f32[1024,128]{1,0:T(8,128)S(1)}, f32[1024,128]{1,0:T(8,128)S(1)}, f32[8,1024]{1,0:T(8,128)S(1)}, f32[8,1024]{1,0:T(8,128)S(1)}, f32[8,1024]{1,0...) custom-call(s32[4,2]{1,0:T(4,128)S(1)} %select_select_fusion.meta_ref, ...), custom_call_target="tpu_custom_call" | custom-call | flops 536870912 | bytes 9408544 | tf_op jit(solution)/shard_map/pallas_call | solution.py:27
  155.4 17.7 %all_to_all.75.moved_ref = bf16[8,2,128,128]{3,2,1,0:T(8,128)(2,1)S(1)} all-to-all(bf16[8,2,128,128]{3,2,1,0:T(8,128)(2,1)S(1)} %get-tuple-element.56), channel_id=1, replica_groups=mesh['y'=4,'x'=4,'core'=2,'sec'=8] {'sec'}, dimensions={0} | all-to-all | bytes 1048576 | tf_op jit(solution)/shard_map/all_to_all | solution.py:76
  173.1 2.1 shard_map.78
  175.2 10.7 %all_to_all.76.got_ref = bf16[16,8,1024]{2,1,0:T(8,128)(2,1)S(1)} all-to-all(bf16[16,8,1024]{2,1,0:T(8,128)(2,1)S(1)} %shard_map.78), channel_id=1, replica_groups=mesh['y'=4,'x'=4,'core'=2,'sec'=8] {'y','x'}, dimensions={0} | all-to-all | bytes 524288 | tf_op jit(solution)/shard_map/all_to_all | solution.py:76
  185.9 4.7 %collective-permute-start.2 = (f32[1024,128]{1,0:T(8,128)S(1)}, f32[1024,128]{1,0:T(8,128)S(1)}, u32[]{:S(2)}, u32[]{:S(2)}) collective-permute-start(f32[1024,128]{1,0:T(8,128)S(1)} %get-tuple-element.64.u_a_ref), channel_id=1, source_target_pairs={{0,8},{8,0},{1,9},{9,1},{2,10},{10,2},{3,11},{11,3},{4,12},{12,4},... | collective-permute-start | bytes 1572872 | tf_op jit(solution)/shard_map/ppermute | solution.py:350
  190.6 0.0 collective-permute-start.3
  190.6 0.7 shard_map.79
  191.4 18.4 %all_to_all.77 = f32[256,1,128]{2,1,0:T(1,128)S(1)} all-to-all(f32[256,1,128]{2,1,0:T(1,128)S(1)} %bitcast.21), channel_id=1, replica_groups=mesh['y'=4,'x'=4,'core'=2,'sec'=8] {'y','x','core','sec'}, dimensions={0} | all-to-all | bytes 262144 | tf_op jit(solution)/shard_map/all_to_all | solution.py:76
  209.8 0.0 collective-permute-done.2.u_far_ref
  209.8 0.0 collective-permute-done.3.corr_far_ref
  209.8 2.4 %shard_map.80 = (f32[2,1024,128]{2,1,0:T(8,128)}, f32[1,1]{1,0:T(1,128)}) custom-call(s32[4,2]{1,0:T(4,128)S(1)} %select_select_fusion.meta_ref, f32[256,128]{1,0:T(8,128)S(1)} %bitcast.20, f32[8,128]{1,0:T(8,128)S(1)} %get-tuple-element.63.theta_ref, f32[1024,128]{1,0:T(8,128)S(1)} %get-tuple-element.64.u_a_ref, ...), custom_call_target="tpu_custom_call" | custom-call | bytes 2232352 | tf_op jit(solution)/shard_map/pallas_call | solution.py:27
  (2 shorter events, 0.0 us)
Async XLA Ops:
  1.4 1.2 copy-start.3
  2.7 2.2 %copy-start = (bf16[1,2,1024,1024]{3,2,1,0:T(8,128)(2,1)S(1)}, bf16[1,2,1024,1024]{3,2,1,0:T(8,128)(2,1)}, u32[]{:S(2)}) copy-start(bf16[1,2,1024,1024]{3,2,1,0:T(8,128)(2,1)} %env_ref.4) | copy-start | bytes 12582916
  5.0 16.5 %collective-permute-start = (bf16[1024,1024]{1,0:T(8,128)(2,1)S(1)}, bf16[1024,1024]{1,0:T(8,128)(2,1)S(1)}, u32[]{:S(2)}, u32[]{:S(2)}) collective-permute-start(bf16[1024,1024]{1,0:T(8,128)(2,1)S(1)} %dynamic-slice_bitcast_fusion.1), channel_id=1, source_target_pairs={{0,8},{8,0},{1,9},{9,1},{2,10},{10,2},{3,11},{11,3},{4,12},{12,4},... | collective-permute-start | bytes 6291464 | tf_op jit(solution)/shard_map/ppermute | solution.py:293
  21.5 2.2 %copy-start.1 = (bf16[1,2,1024,1024]{3,2,1,0:T(8,128)(2,1)S(1)}, bf16[1,2,1024,1024]{3,2,1,0:T(8,128)(2,1)}, u32[]{:S(2)}) copy-start(bf16[1,2,1024,1024]{3,2,1,0:T(8,128)(2,1)} %env_ref.5) | copy-start | bytes 12582916
  23.9 22.0 %collective-permute-start.1 = (bf16[1024,1024]{1,0:T(8,128)(2,1)S(1)}, bf16[1024,1024]{1,0:T(8,128)(2,1)S(1)}, u32[]{:S(2)}, u32[]{:S(2)}) collective-permute-start(bf16[1024,1024]{1,0:T(8,128)(2,1)S(1)} %dynamic-slice_bitcast_fusion), channel_id=1, source_target_pairs={{0,8},{8,0},{1,9},{9,1},{2,10},{10,2},{3,11},{11,3},{4,12},{12,4},... | collective-permute-start | bytes 6291464 | tf_op jit(solution)/shard_map/ppermute | solution.py:293
  45.8 19.3 %copy-start.2 = (f32[2,1024,128]{2,1,0:T(8,128)S(1)}, f32[2,1024,128]{2,1,0:T(8,128)}, u32[]{:S(2)}) copy-start(f32[2,1024,128]{2,1,0:T(8,128)} %diag_ref.5) | copy-start | bytes 3145732
  185.9 23.8 %collective-permute-start.2 = (f32[1024,128]{1,0:T(8,128)S(1)}, f32[1024,128]{1,0:T(8,128)S(1)}, u32[]{:S(2)}, u32[]{:S(2)}) collective-permute-start(f32[1024,128]{1,0:T(8,128)S(1)} %get-tuple-element.64.u_a_ref), channel_id=1, source_target_pairs={{0,8},{8,0},{1,9},{9,1},{2,10},{10,2},{3,11},{11,3},{4,12},{12,4},... | collective-permute-start | bytes 1572872 | tf_op jit(solution)/shard_map/ppermute | solution.py:350
  190.6 19.1 %collective-permute-start.3 = (f32[1024,128]{1,0:T(8,128)S(1)}, f32[1024,128]{1,0:T(8,128)S(1)}, u32[]{:S(2)}, u32[]{:S(2)}) collective-permute-start(f32[1024,128]{1,0:T(8,128)S(1)} %get-tuple-element.65.corr_a_ref), channel_id=1, source_target_pairs={{0,8},{8,0},{1,9},{9,1},{2,10},{10,2},{3,11},{11,3},{4,12},{12,4},... | collective-permute-start | bytes 1572872 | tf_op jit(solution)/shard_map/ppermute | solution.py:351

commit v7 on v6

--- a/solution.py
+++ b/solution.py
@@ -13,7 +13,10 @@
 ALL = ("y", "x", "core", "sec")
 LANES = 128
 PIECE = 1024
-BROWS = 16
+TILE = 16
+RANGE = 32000.0
+DIGIT = 2.0**14
+I16 = jnp.int16
 LIMIT = 24
 START = 4 * 10**9
 F32 = jnp.float32
@@ -52,6 +55,64 @@
     return functools.reduce(lambda a, b: a + b, [ref[pl.ds(start + step * k, 1)] for k in range(count)])
 
 
+def powers():
+    lane = lax.broadcasted_iota(jnp.int32, (1, LANES), 1)
+    up, down = jnp.ones((1, LANES), F32), jnp.ones((1, LANES), F32)
+    for bit in range(7):
+        chosen = (lane >> bit) % 2 == 1
+        up = up * jnp.where(chosen, 2.0 ** (1 << bit), 1.0)
+        down = down * jnp.where(chosen & (lane < LANES - 1), 2.0 ** -(1 << bit), 1.0)
+    down = jnp.where(lane < LANES - 1, down, 0.0)
+    return lane.astype(F32), up, down
+
+
+def exponent_of(largest):
+    _, up, down = powers()
+    above = jnp.sum(jnp.where(up < largest, 1.0, 0.0), axis=1, keepdims=True)
+    below = jnp.sum(jnp.where((down >= largest) & (down > 0.0), 1.0, 0.0), axis=1, keepdims=True)
+    return jnp.clip(jnp.where(largest > 1.0, above, 1.0 - below), -126.0, 126.0)
+
+
+def power(exponent):
+    lane, up, down = powers()
+    chosen = jnp.where(lane == exponent, up, 0.0)
+    chosen = chosen + jnp.where((lane == -exponent) & (exponent < 0.0), down, 0.0)
+    return jnp.sum(chosen, axis=1, keepdims=True)
+
+
+def whole(values):
+    return jnp.floor(values + 0.5)
+
+
+def encode(block, line):
+    largest = jnp.max(jnp.max(jnp.abs(block), axis=0, keepdims=True), axis=1, keepdims=True)
+    exponent = exponent_of(largest)
+    rows = [jnp.broadcast_to(exponent, line.shape)]
+    block = whole(block * power(-exponent) * RANGE)
+    exponent = exponent_of(jnp.max(jnp.abs(line), axis=1, keepdims=True))
+    rows.append(jnp.broadcast_to(exponent, line.shape))
+    rest = line * power(-exponent)
+    for _ in range(3):
+        rest = rest * DIGIT
+        rows.append(whole(rest))
+        rest = rest - rows[-1]
+    rows.append(jnp.zeros((TILE - len(rows), LANES), F32))
+    return jnp.concatenate([block] + rows, axis=0).astype(jnp.int32).astype(I16)
+
+
+def decode(ref, count):
+    size = ref.shape[1] - TILE
+    tiles = [ref[j, size:].astype(jnp.int32).astype(F32) for j in range(count)]
+    rows = [jnp.concatenate([tile[k : k + 1] for tile in tiles], axis=0) for k in range(5)]
+    scales = power(rows[0][:, :1])
+    blocks = [
+        ref[j, :size].astype(jnp.int32).astype(F32) * (1.0 / RANGE) * scales[j : j + 1]
+        for j in range(count)
+    ]
+    line = ((rows[4] / DIGIT + rows[3]) / DIGIT + rows[2]) / DIGIT * power(rows[1][:, :1])
+    return blocks, jnp.sum(line, axis=0, keepdims=True)
+
+
 def make(n_y, n_x, n_z):
     n_xy = n_y * n_x
 
@@ -59,7 +120,7 @@
         sectors, size, cols = psi.shape
         sub = cols // n_xy
         shard_rows = n_z * sub
-        one, two = sub + 1, 2 * sub + 1
+        one = sub + 1
         scale = 1.0 / (size * size)
         core = lax.axis_index("core")
         swap = [(0, 1), (1, 0)]
@@ -163,56 +224,44 @@
             pairs = [(u, image), (corr, hu), (corr, image), (u, corr), (corr, corr), (u, u)]
             return line_of([fold(a * b) for a, b in pairs])
 
-        def put_image(meta_ref, got_ref, u_b_ref, more, image_ref, out_ref, step):
+        def first_image_kernel(meta_ref, got_ref, u_b_ref, diag_ref, image_ref, out_ref):
             image = image_of(meta_ref, got_ref)
             image_ref[...] = image
-            line = dots_line(image, u_b_ref, more)
+            line = dots_line(image, u_b_ref, ())
             for k in range(n_z):
                 for c in range(2):
-                    first = (c * n_z + k) * step
-                    out_ref[pl.ds(first, sub)] = image[:, k * cols : (k + 1) * cols]
-                    out_ref[pl.ds(first + sub, 1)] = line
-
-        def first_image_kernel(meta_ref, got_ref, u_b_ref, diag_ref, image_ref, out_ref):
-            put_image(meta_ref, got_ref, u_b_ref, (), image_ref, out_ref, two)
-            core = place(meta_ref)[0]
-            for k in range(n_z):
-                rows = diag_ref[core, own_rows(meta_ref, k)]
-                for c in range(2):
-                    out_ref[pl.ds((c * n_z + k) * two + one, sub)] = rows
+                    shard_k = image[:, k * cols : (k + 1) * cols]
+                    rows = jnp.where(place(meta_ref)[0] == c, shard_k, diag_ref[c, own_rows(meta_ref, k)])
+                    out_ref[pl.ds((c * n_z + k) * one, sub)] = rows
+                    out_ref[pl.ds((c * n_z + k) * one + sub, 1)] = line
 
         def image_kernel(meta_ref, got_ref, u_b_ref, corr_b_ref, hu_b_ref, image_ref, out_ref):
-            put_image(meta_ref, got_ref, u_b_ref, (corr_b_ref, hu_b_ref), image_ref, out_ref, one)
+            image = image_of(meta_ref, got_ref)
+            image_ref[...] = image
+            line = dots_line(image, u_b_ref, (corr_b_ref, hu_b_ref))
+            for k in range(2 * n_z):
+                out_ref[pl.ds(k * one, sub)] = image[:, (k % n_z) * cols : (k % n_z + 1) * cols]
+                out_ref[pl.ds(k * one + sub, 1)] = line
 
         def last_image_kernel(meta_ref, got_ref, u_b_ref, corr_b_ref, hu_b_ref, out_ref):
             image = image_of(meta_ref, got_ref)
             line = dots_line(image, u_b_ref, (corr_b_ref, hu_b_ref))
             out_ref[...] = jnp.broadcast_to(line, out_ref.shape)
 
-        def mine(meta_ref, got_ref, k, step, start):
-            rows = [got_ref[pl.ds((c * n_z + k) * step + start, sub)] for c in range(2)]
-            return jnp.where(place(meta_ref)[0] == 0, rows[0], rows[1])
-
-        def first_spread_kernel(meta_ref, got_ref, out_ref, diag_b_ref):
-            full = shard_rows + 1
-            line = add_rows(got_ref, sub, two, 2 * n_z)
+        def from_cores(meta_ref, got_ref, k):
+            zero, other = [got_ref[pl.ds((c * n_z + k) * one, sub)] for c in range(2)]
+            first = place(meta_ref)[0] == 0
+            return jnp.where(first, zero, other), jnp.where(first, other, zero)
+
+        def spread_kernel(meta_ref, got_ref, out_ref, *diag_b_ref):
+            line = add_rows(got_ref, sub, one, 2 * n_z)
+            shards = []
             for k in range(n_z):
-                rows = mine(meta_ref, got_ref, k, two, 0)
-                for j in range(n_xy):
-                    out_ref[pl.ds(j * full + k * sub, sub)] = rows
-                diag_b_ref[:, k * cols : (k + 1) * cols] = mine(meta_ref, got_ref, k, two, one)
-            for j in range(n_xy):
-                out_ref[pl.ds(j * full + shard_rows, 1)] = line
-
-        def spread_kernel(meta_ref, got_ref, out_ref):
-            line = add_rows(got_ref, sub, one, 2 * n_z)
-            pieces = []
-            for _ in range(3):
-                pieces.append(line.astype(BF16).astype(F32))
-                line = line - pieces[-1]
-            pieces.append(jnp.zeros((BROWS - 3, cols), F32))
-            rows = [mine(meta_ref, got_ref, k, one, 0) for k in range(n_z)]
-            block = jnp.concatenate(rows + pieces, axis=0).astype(BF16)
+                rows, far = from_cores(meta_ref, got_ref, k)
+                shards.append(rows)
+                for ref in diag_b_ref:
+                    ref[:, k * cols : (k + 1) * cols] = far
+            block = encode(jnp.concatenate(shards, axis=0), line)
             out_ref[...] = jnp.broadcast_to(block[None], out_ref.shape)
 
         def projected(theta, sums):
@@ -237,10 +286,10 @@
             return jnp.concatenate(parts, axis=1).reshape(share)
 
         def begin_kernel(meta_ref, got_ref, u_a_ref, u_b_ref, hu_b_ref, diag_ref, diag_b_ref, env_ref, env2_ref, hu_a_ref, corr_a_ref, corr_b_ref, theta_ref, left_ref):
-            full = shard_rows + 1
-            theta = add_rows(got_ref, shard_rows, full, n_xy)[:, :1] * scale
+            blocks, line = decode(got_ref, n_xy)
+            theta = line[:, :1] * scale
             theta_ref[...] = jnp.broadcast_to(theta, theta_ref.shape)
-            hu_a = share_of([got_ref[pl.ds(j * full, shard_rows)] for j in range(n_xy)])
+            hu_a = share_of(blocks)
             hu_a_ref[...] = hu_a
             corr_a = correction(theta, hu_a, u_a_ref[...], diag_ref[place(meta_ref)[0]])
             corr_a_ref[...] = corr_a
@@ -248,13 +297,12 @@
             left_matmul(meta_ref, env_ref, env2_ref, corr_a.astype(BF16), left_ref)
 
         def update_kernel(meta_ref, got_ref, old_theta_ref, u_a_ref, corr_a_ref, hu_a_ref, u_b_ref, corr_b_ref, hu_b_ref, hc_b_ref, diag_ref, diag_b_ref, env_ref, env2_ref, u_a_out, corr_a_out, u_b_out, corr_b_out, hu_b_out, theta_ref, left_ref, *hu_a_out):
-            lines = jnp.sum(got_ref[:, shard_rows:].astype(F32), axis=0)
-            line = jnp.sum(lines, axis=0, keepdims=True) * scale
-            sums = [line[:, k : k + 1] for k in range(6)]
+            blocks, line = decode(got_ref, n_xy)
+            sums = [line[:, k : k + 1] * scale for k in range(6)]
             old, new, theta, _ = projected(old_theta_ref[0:1, 0:1], sums)
             theta_ref[...] = jnp.broadcast_to(theta, theta_ref.shape)
             u_a = old * u_a_ref[...] + new * corr_a_ref[...]
-            hu_a = old * hu_a_ref[...] + new * share_of([got_ref[j, :shard_rows].astype(F32) for j in range(n_xy)])
+            hu_a = old * hu_a_ref[...] + new * share_of(blocks)
             corr_a = correction(theta, hu_a, u_a, diag_ref[place(meta_ref)[0]])
             u_a_out[...], corr_a_out[...] = u_a, corr_a
             for ref in hu_a_out:
@@ -312,29 +360,26 @@
         got = apply_right(left)
         hu_b, payload = call(
             first_image_kernel,
-            [b_out, ((2 * n_z * two, cols), F32)],
+            [b_out, payload_out],
             i_meta + v(got, u_b, diag),
         )
+        gathered = ((n_xy, shard_rows + TILE, cols), I16)
         payload, diag_b = call(
-            first_spread_kernel,
-            [((n_xy * (shard_rows + 1), cols), F32), b_out],
-            i_meta + v(a2a_rows(payload, 2 * n_z, CZ)),
-        )
-        got = a2a_rows(payload, n_xy, XY)
+            spread_kernel, [gathered, b_out], i_meta + v(a2a_rows(payload, 2 * n_z, CZ))
+        )
+        got = a2a(payload, XY)
         hu_a, corr_a, corr_b, theta, left = call(
             begin_kernel,
             [a_out, a_out, b_out, tile_out, left_out],
             i_meta + v(got, u_a, u_b, hu_b, diag, diag_b) + lefts, (), work,
         )
         for step in range(ITERS - 1):
-            got = apply_right(left)
+            got = apply_right(left, BF16)
             hc_b, payload = call(
                 image_kernel, [b_out, payload_out], i_meta + v(got, u_b, corr_b, hu_b)
             )
             (payload,) = call(
-                spread_kernel,
-                [((n_xy, shard_rows + BROWS, cols), BF16)],
-                i_meta + v(a2a_rows(payload, 2 * n_z, CZ)),
+                spread_kernel, [gathered], i_meta + v(a2a_rows(payload, 2 * n_z, CZ))
             )
             got = a2a(payload, XY)
             more = [a_out] * (step < ITERS - 2)

time: 213 us -> 209 us (0.981)
  blocking collectives: 179 us -> 173 us
    all_to_all x12, blocking collectives: 179 us -> 173 us  [a2a(): return lax.all_to_all(array, axes, 0, 0, tiled=True)]
where the time goes in v7:
time: 209 us; the launch traced here: 208 us
  blocking collectives  173 us (83%)
  Pallas kernels  20.3 us (10%)
  starting transfers between devices  9.62 us (5%)
  local copies, waits for them, and re-layouts  3 us (1%)
    all_to_all x12, blocking collectives, a2a(): return lax.all_to_all(array, axes, 0, 0, tiled=True)  173 us
    pallas_call x13, Pallas kernels, call(): pl.pallas_call(kernel, out_shape=[jax.ShapeDtypeStruct(s, d) for s, d in...  20.3 us
    ppermute x2, starting transfers between devices, swapped(): return lax.ppermute(give.reshape(size, size), 'core', swap)  4.87 us
    ppermute x1, starting transfers between devices, per_device(): u_far = lax.ppermute(u_send, 'core', swap)  4.75 us
  transfers between devices with their start and end apart: 4, of which 0 were waited for; matrix products, arithmetic and copies ran while one was open for 0% of the time, Pallas kernels for 0%

profile of v7, /device:TPU:1, one launch (start us, length us, event | category | flops | bytes accessed | tf_op | source)
XLA Modules:
  0.0 207.9 jit_solution(6451142049803147979)
XLA Ops:
  0.7 0.8 select_select_fusion.meta_ref
  1.4 0.0 copy-start.3
  1.4 1.2 copy-done.3
  2.7 0.0 copy-start
  2.7 1.0 shard_map.68
  3.7 1.2 copy-done
  4.8 0.2 dynamic-slice_bitcast_fusion.1
  5.0 3.3 %collective-permute-start = (bf16[1024,1024]{1,0:T(8,128)(2,1)S(1)}, bf16[1024,1024]{1,0:T(8,128)(2,1)S(1)}, u32[]{:S(2)}, u32[]{:S(2)}) collective-permute-start(bf16[1024,1024]{1,0:T(8,128)(2,1)S(1)} %dynamic-slice_bitcast_fusion.1), channel_id=1, source_target_pairs={{0,8},{8,0},{1,9},{9,1},{2,10},{10,2},{3,11},{11,3},{4,12},{12,4},... | collective-permute-start | bytes 6291464 | tf_op jit(solution)/shard_map/ppermute | solution.py:341
  8.3 13.2 %all_to_all.66 = f32[8,9,1,128]{3,2,1,0:T(1,128)S(1)} all-to-all(f32[8,9,1,128]{3,2,1,0:T(1,128)S(1)} %bitcast.22), channel_id=1, replica_groups=mesh['y'=4,'x'=4,'core'=2,'sec'=8] {'sec'}, dimensions={0} | all-to-all | bytes 73728 | tf_op jit(solution)/shard_map/all_to_all | solution.py:137
  21.5 0.0 collective-permute-done.env2_ref
  21.5 0.0 copy-start.1
  21.5 1.9 shard_map.69
  23.4 0.3 copy-done.1
  23.7 0.2 dynamic-slice_bitcast_fusion
  23.9 1.5 collective-permute-start.1
  25.4 20.4 %all_to_all.67.moved_ref = bf16[8,2,128,128]{3,2,1,0:T(8,128)(2,1)S(1)} all-to-all(bf16[8,2,128,128]{3,2,1,0:T(8,128)(2,1)S(1)} %get-tuple-element.41), channel_id=1, replica_groups=mesh['y'=4,'x'=4,'core'=2,'sec'=8] {'sec'}, dimensions={0} | all-to-all | bytes 1048576 | tf_op jit(solution)/shard_map/all_to_all | solution.py:137
  45.8 0.0 copy-start.2
  45.8 0.0 collective-permute-done.1.got_ref
  45.8 2.1 shard_map.70
  47.9 17.2 %all_to_all.68.got_ref = f32[16,8,1024]{2,1,0:T(8,128)S(1)} all-to-all(f32[16,8,1024]{2,1,0:T(8,128)S(1)} %shard_map.70), channel_id=1, replica_groups=mesh['y'=4,'x'=4,'core'=2,'sec'=8] {'y','x'}, dimensions={0} | all-to-all | bytes 1048576 | tf_op jit(solution)/shard_map/all_to_all | solution.py:137
  65.1 0.0 copy-done.2
  65.1 0.7 shard_map.71
  65.8 11.5 %all_to_all.69 = f32[16,9,1,128]{3,2,1,0:T(1,128)S(1)} all-to-all(f32[16,9,1,128]{3,2,1,0:T(1,128)S(1)} %bitcast.20), channel_id=1, replica_groups=mesh['y'=4,'x'=4,'core'=2,'sec'=8] {'core','sec'}, dimensions={0} | all-to-all | bytes 147456 | tf_op jit(solution)/shard_map/all_to_all | solution.py:137
  77.3 0.9 shard_map.72
  78.2 10.8 %all_to_all.70.got_ref = s16[16,80,128]{2,1,0:T(8,128)(2,1)S(1)} all-to-all(s16[16,80,128]{2,1,0:T(8,128)(2,1)S(1)} %get-tuple-element.45), channel_id=1, replica_groups=mesh['y'=4,'x'=4,'core'=2,'sec'=8] {'y','x'}, dimensions={0} | all-to-all | bytes 655360 | tf_op jit(solution)/shard_map/all_to_all | solution.py:137
  89.0 2.1 %shard_map.73 = (f32[1024,128]{1,0:T(8,128)S(1)}, f32[1024,128]{1,0:T(8,128)S(1)}, f32[8,1024]{1,0:T(8,128)S(1)}, f32[8,128]{1,0:T(8,128)S(1)}, bf16[8,2,128,128]{3,2,1,0:T(8,128)(2,1)S(1)}) custom-call(s32[4,2]{1,0:T(4,128)S(1)} %select_select_fusion.meta_ref, s16[16,80,128]{2,1,0:T(8,128)(2,1)S(1)} %all_to_all.70.got_ref, ...), custom_call_target="tpu_custom_call" | custom-call | flops 536870912 | bytes 8290336 | tf_op jit(solution)/shard_map/pallas_call | solution.py:30
  91.1 17.7 %all_to_all.71.moved_ref = bf16[8,2,128,128]{3,2,1,0:T(8,128)(2,1)S(1)} all-to-all(bf16[8,2,128,128]{3,2,1,0:T(8,128)(2,1)S(1)} %get-tuple-element.49), channel_id=1, replica_groups=mesh['y'=4,'x'=4,'core'=2,'sec'=8] {'sec'}, dimensions={0} | all-to-all | bytes 1048576 | tf_op jit(solution)/shard_map/all_to_all | solution.py:137
  108.8 2.1 shard_map.74
  110.9 10.7 %all_to_all.72.got_ref = bf16[16,8,1024]{2,1,0:T(8,128)(2,1)S(1)} all-to-all(bf16[16,8,1024]{2,1,0:T(8,128)(2,1)S(1)} %shard_map.74), channel_id=1, replica_groups=mesh['y'=4,'x'=4,'core'=2,'sec'=8] {'y','x'}, dimensions={0} | all-to-all | bytes 524288 | tf_op jit(solution)/shard_map/all_to_all | solution.py:137
  121.6 0.7 shard_map.75
  122.3 14.4 %all_to_all.73 = f32[16,9,1,128]{3,2,1,0:T(1,128)S(1)} all-to-all(f32[16,9,1,128]{3,2,1,0:T(1,128)S(1)} %bitcast.21), channel_id=1, replica_groups=mesh['y'=4,'x'=4,'core'=2,'sec'=8] {'core','sec'}, dimensions={0} | all-to-all | bytes 147456 | tf_op jit(solution)/shard_map/all_to_all | solution.py:137
  136.7 0.9 shard_map.76
  137.6 10.7 %all_to_all.74.got_ref = s16[16,80,128]{2,1,0:T(8,128)(2,1)S(1)} all-to-all(s16[16,80,128]{2,1,0:T(8,128)(2,1)S(1)} %shard_map.76), channel_id=1, replica_groups=mesh['y'=4,'x'=4,'core'=2,'sec'=8] {'y','x'}, dimensions={0} | all-to-all | bytes 655360 | tf_op jit(solution)/shard_map/all_to_all | solution.py:137
  148.3 2.7 %shard_map.77 = (f32[1024,128]{1,0:T(8,128)S(1)}, f32[1024,128]{1,0:T(8,128)S(1)}, f32[8,1024]{1,0:T(8,128)S(1)}, f32[8,1024]{1,0:T(8,128)S(1)}, f32[8,1024]{1,0...) custom-call(s32[4,2]{1,0:T(4,128)S(1)} %select_select_fusion.meta_ref, ...), custom_call_target="tpu_custom_call" | custom-call | flops 536870912 | bytes 9408544 | tf_op jit(solution)/shard_map/pallas_call | solution.py:30
  151.1 17.7 %all_to_all.75.moved_ref = bf16[8,2,128,128]{3,2,1,0:T(8,128)(2,1)S(1)} all-to-all(bf16[8,2,128,128]{3,2,1,0:T(8,128)(2,1)S(1)} %get-tuple-element.56), channel_id=1, replica_groups=mesh['y'=4,'x'=4,'core'=2,'sec'=8] {'sec'}, dimensions={0} | all-to-all | bytes 1048576 | tf_op jit(solution)/shard_map/all_to_all | solution.py:137
  168.8 2.1 shard_map.78
  170.9 10.7 %all_to_all.76.got_ref = bf16[16,8,1024]{2,1,0:T(8,128)(2,1)S(1)} all-to-all(bf16[16,8,1024]{2,1,0:T(8,128)(2,1)S(1)} %shard_map.78), channel_id=1, replica_groups=mesh['y'=4,'x'=4,'core'=2,'sec'=8] {'y','x'}, dimensions={0} | all-to-all | bytes 524288 | tf_op jit(solution)/shard_map/all_to_all | solution.py:137
  181.6 4.7 %collective-permute-start.2 = (f32[1024,128]{1,0:T(8,128)S(1)}, f32[1024,128]{1,0:T(8,128)S(1)}, u32[]{:S(2)}, u32[]{:S(2)}) collective-permute-start(f32[1024,128]{1,0:T(8,128)S(1)} %get-tuple-element.64.u_a_ref), channel_id=1, source_target_pairs={{0,8},{8,0},{1,9},{9,1},{2,10},{10,2},{3,11},{11,3},{4,12},{12,4},... | collective-permute-start | bytes 1572872 | tf_op jit(solution)/shard_map/ppermute | solution.py:395
  186.4 0.0 collective-permute-start.3
  186.4 0.7 shard_map.79
  187.1 18.4 %all_to_all.77 = f32[256,1,128]{2,1,0:T(1,128)S(1)} all-to-all(f32[256,1,128]{2,1,0:T(1,128)S(1)} %bitcast.16), channel_id=1, replica_groups=mesh['y'=4,'x'=4,'core'=2,'sec'=8] {'y','x','core','sec'}, dimensions={0} | all-to-all | bytes 262144 | tf_op jit(solution)/shard_map/all_to_all | solution.py:137
  205.5 0.0 collective-permute-done.2.u_far_ref
  205.5 0.0 collective-permute-done.3.corr_far_ref
  205.5 2.4 %shard_map.80 = (f32[2,1024,128]{2,1,0:T(8,128)}, f32[1,1]{1,0:T(1,128)}) custom-call(s32[4,2]{1,0:T(4,128)S(1)} %select_select_fusion.meta_ref, f32[256,128]{1,0:T(8,128)S(1)} %bitcast.15, f32[8,128]{1,0:T(8,128)S(1)} %get-tuple-element.63.theta_ref, f32[1024,128]{1,0:T(8,128)S(1)} %get-tuple-element.64.u_a_ref, ...), custom_call_target="tpu_custom_call" | custom-call | bytes 2232352 | tf_op jit(solution)/shard_map/pallas_call | solution.py:30
  (2 shorter events, 0.0 us)
Async XLA Ops:
  1.4 1.2 copy-start.3
  2.7 2.2 %copy-start = (bf16[1,2,1024,1024]{3,2,1,0:T(8,128)(2,1)S(1)}, bf16[1,2,1024,1024]{3,2,1,0:T(8,128)(2,1)}, u32[]{:S(2)}) copy-start(bf16[1,2,1024,1024]{3,2,1,0:T(8,128)(2,1)} %env_ref.4) | copy-start | bytes 12582916
  5.0 16.5 %collective-permute-start = (bf16[1024,1024]{1,0:T(8,128)(2,1)S(1)}, bf16[1024,1024]{1,0:T(8,128)(2,1)S(1)}, u32[]{:S(2)}, u32[]{:S(2)}) collective-permute-start(bf16[1024,1024]{1,0:T(8,128)(2,1)S(1)} %dynamic-slice_bitcast_fusion.1), channel_id=1, source_target_pairs={{0,8},{8,0},{1,9},{9,1},{2,10},{10,2},{3,11},{11,3},{4,12},{12,4},... | collective-permute-start | bytes 6291464 | tf_op jit(solution)/shard_map/ppermute | solution.py:341
  21.5 2.2 %copy-start.1 = (bf16[1,2,1024,1024]{3,2,1,0:T(8,128)(2,1)S(1)}, bf16[1,2,1024,1024]{3,2,1,0:T(8,128)(2,1)}, u32[]{:S(2)}) copy-start(bf16[1,2,1024,1024]{3,2,1,0:T(8,128)(2,1)} %env_ref.5) | copy-start | bytes 12582916
  23.9 22.0 %collective-permute-start.1 = (bf16[1024,1024]{1,0:T(8,128)(2,1)S(1)}, bf16[1024,1024]{1,0:T(8,128)(2,1)S(1)}, u32[]{:S(2)}, u32[]{:S(2)}) collective-permute-start(bf16[1024,1024]{1,0:T(8,128)(2,1)S(1)} %dynamic-slice_bitcast_fusion), channel_id=1, source_target_pairs={{0,8},{8,0},{1,9},{9,1},{2,10},{10,2},{3,11},{11,3},{4,12},{12,4},... | collective-permute-start | bytes 6291464 | tf_op jit(solution)/shard_map/ppermute | solution.py:341
  45.8 19.3 %copy-start.2 = (f32[2,1024,128]{2,1,0:T(8,128)S(1)}, f32[2,1024,128]{2,1,0:T(8,128)}, u32[]{:S(2)}) copy-start(f32[2,1024,128]{2,1,0:T(8,128)} %diag_ref.5) | copy-start | bytes 3145732
  181.6 23.9 %collective-permute-start.2 = (f32[1024,128]{1,0:T(8,128)S(1)}, f32[1024,128]{1,0:T(8,128)S(1)}, u32[]{:S(2)}, u32[]{:S(2)}) collective-permute-start(f32[1024,128]{1,0:T(8,128)S(1)} %get-tuple-element.64.u_a_ref), channel_id=1, source_target_pairs={{0,8},{8,0},{1,9},{9,1},{2,10},{10,2},{3,11},{11,3},{4,12},{12,4},... | collective-permute-start | bytes 1572872 | tf_op jit(solution)/shard_map/ppermute | solution.py:395
  186.4 19.1 %collective-permute-start.3 = (f32[1024,128]{1,0:T(8,128)S(1)}, f32[1024,128]{1,0:T(8,128)S(1)}, u32[]{:S(2)}, u32[]{:S(2)}) collective-permute-start(f32[1024,128]{1,0:T(8,128)S(1)} %get-tuple-element.65.corr_a_ref), channel_id=1, source_target_pairs={{0,8},{8,0},{1,9},{9,1},{2,10},{10,2},{3,11},{11,3},{4,12},{12,4},... | collective-permute-start | bytes 1572872 | tf_op jit(solution)/shard_map/ppermute | solution.py:396

commit v8 on v7

--- a/solution.py
+++ b/solution.py
@@ -208,9 +208,31 @@
             for rows, total in right_pieces(meta_ref, moved_ref, env_ref, got_ref):
                 out_ref[:, :, rows] = total.reshape(n_xy, sub, PIECE).astype(out_ref.dtype)
 
-        def image_of(meta_ref, got_ref):
+        def first_right_kernel(meta_ref, moved_ref, env_ref, got_ref, out_ref):
+            parts = [total for _, total in right_pieces(meta_ref, moved_ref, env_ref, got_ref)]
+            partial = jnp.concatenate(parts, axis=1)
+            largest = jnp.max(jnp.max(jnp.abs(partial), axis=0, keepdims=True), axis=1, keepdims=True)
+            exponent = exponent_of(largest)
+            partial = whole(partial * power(-exponent) * RANGE)
+            tile = jnp.broadcast_to(exponent, (TILE, cols)).astype(jnp.int32).astype(I16)
+            for j in range(n_xy):
+                rows = partial[j * sub : (j + 1) * sub]
+                rows = [rows[:, k * cols : (k + 1) * cols] for k in range(n_z)]
+                block = jnp.concatenate(rows, axis=0).astype(jnp.int32).astype(I16)
+                out_ref[j, :shard_rows] = block
+                out_ref[j, shard_rows:] = tile
+
+        def first_sum(got_ref):
+            tiles = [got_ref[j, shard_rows:].astype(jnp.int32).astype(F32) for j in range(n_xy)]
+            scales = power(jnp.concatenate([tile[:1] for tile in tiles], axis=0)[:, :1])
+            total = jnp.zeros((shard_rows, cols), F32)
+            for j in range(n_xy):
+                block = got_ref[j, :shard_rows].astype(jnp.int32).astype(F32)
+                total = total + block * (1.0 / RANGE) * scales[j : j + 1]
+            return jnp.concatenate([total[k * sub : (k + 1) * sub] for k in range(n_z)], axis=1)
+
+        def image_of(meta_ref, image):
             core, z, q = place(meta_ref)
-            image = jnp.sum(got_ref[...].astype(F32), axis=0)
             row = lax.broadcasted_iota(jnp.int32, shard, 0) + (z * cols + q * sub)
             col = lax.broadcasted_iota(jnp.int32, shard, 1)
             rows, columns = dims_of(meta_ref, core)
@@ -225,7 +247,7 @@
             return line_of([fold(a * b) for a, b in pairs])
 
         def first_image_kernel(meta_ref, got_ref, u_b_ref, diag_ref, image_ref, out_ref):
-            image = image_of(meta_ref, got_ref)
+            image = image_of(meta_ref, first_sum(got_ref))
             image_ref[...] = image
             line = dots_line(image, u_b_ref, ())
             for k in range(n_z):
@@ -236,7 +258,7 @@
                     out_ref[pl.ds((c * n_z + k) * one + sub, 1)] = line
 
         def image_kernel(meta_ref, got_ref, u_b_ref, corr_b_ref, hu_b_ref, image_ref, out_ref):
-            image = image_of(meta_ref, got_ref)
+            image = image_of(meta_ref, jnp.sum(got_ref[...].astype(F32), axis=0))
             image_ref[...] = image
             line = dots_line(image, u_b_ref, (corr_b_ref, hu_b_ref))
             for k in range(2 * n_z):
@@ -244,7 +266,7 @@
                 out_ref[pl.ds(k * one + sub, 1)] = line
 
         def last_image_kernel(meta_ref, got_ref, u_b_ref, corr_b_ref, hu_b_ref, out_ref):
-            image = image_of(meta_ref, got_ref)
+            image = image_of(meta_ref, jnp.sum(got_ref[...].astype(F32), axis=0))
             line = dots_line(image, u_b_ref, (corr_b_ref, hu_b_ref))
             out_ref[...] = jnp.broadcast_to(line, out_ref.shape)
 
@@ -349,21 +371,21 @@
         left, right_env = lax.optimization_barrier((left, right_env))
         rights = v(right_env, swapped(right_env, other))
 
-        def apply_right(left, kind=F32):
+        gathered = ((n_xy, shard_rows + TILE, cols), I16)
+
+        def apply_right(left, kernel, out):
             moved = a2a(left, "sec")
-            (partial,) = call(
-                right_kernel, [((n_xy, sub, size), kind)], i_meta + v(moved) + rights, (), work
-            )
+            (partial,) = call(kernel, [out], i_meta + v(moved) + rights, (), work)
             return a2a(partial, XY)
 
+        summed = ((n_xy, sub, size), BF16)
         payload_out = ((2 * n_z * one, cols), F32)
-        got = apply_right(left)
+        got = apply_right(left, first_right_kernel, gathered)
         hu_b, payload = call(
             first_image_kernel,
             [b_out, payload_out],
             i_meta + v(got, u_b, diag),
         )
-        gathered = ((n_xy, shard_rows + TILE, cols), I16)
         payload, diag_b = call(
             spread_kernel, [gathered, b_out], i_meta + v(a2a_rows(payload, 2 * n_z, CZ))
         )
@@ -374,7 +396,7 @@
             i_meta + v(got, u_a, u_b, hu_b, diag, diag_b) + lefts, (), work,
         )
         for step in range(ITERS - 1):
-            got = apply_right(left, BF16)
+            got = apply_right(left, right_kernel, summed)
             hc_b, payload = call(
                 image_kernel, [b_out, payload_out], i_meta + v(got, u_b, corr_b, hu_b)
             )
@@ -390,7 +412,7 @@
                 (), work,
             )
             (hu_a,) = more or (None,)
-        got = apply_right(left, BF16)
+        got = apply_right(left, right_kernel, summed)
         got, u_send, corr_send = lax.optimization_barrier((got, u_a, corr_a))
         u_far = lax.ppermute(u_send, "core", swap)
         corr_far = lax.ppermute(corr_send, "core", swap)

time: 209 us -> 207 us (level)
    all_to_all x12, blocking collectives: 173 us -> 171 us  [a2a(): return lax.all_to_all(array, axes, 0, 0, tiled=True)]
where the time goes in v8:
time: 207 us; the launch traced here: 206 us
  blocking collectives  171 us (83%)
  Pallas kernels  20.8 us (10%)
  starting transfers between devices  9.61 us (5%)
  local copies, waits for them, and re-layouts  2.99 us (1%)
    all_to_all x12, blocking collectives, a2a(): return lax.all_to_all(array, axes, 0, 0, tiled=True)  171 us
    pallas_call x13, Pallas kernels, call(): pl.pallas_call(kernel, out_shape=[jax.ShapeDtypeStruct(s, d) for s, d in...  20.8 us
    ppermute x2, starting transfers between devices, swapped(): return lax.ppermute(give.reshape(size, size), 'core', swap)  4.87 us
    ppermute x1, starting transfers between devices, per_device(): u_far = lax.ppermute(u_send, 'core', swap)  4.73 us
  transfers between devices with their start and end apart: 4, of which 0 were waited for; matrix products, arithmetic and copies ran while one was open for 0% of the time, Pallas kernels for 0%

profile of v8, /device:TPU:1, one launch (start us, length us, event | category | flops | bytes accessed | tf_op | source)
XLA Modules:
  0.0 206.2 jit_solution(2740612375607135790)
XLA Ops:
  0.7 0.8 select_select_fusion.meta_ref
  1.4 0.0 copy-start.3
  1.4 1.2 copy-done.3
  2.7 0.0 copy-start
  2.7 1.0 shard_map.68
  3.7 1.2 copy-done
  4.8 0.2 dynamic-slice_bitcast_fusion.1
  5.0 3.3 %collective-permute-start = (bf16[1024,1024]{1,0:T(8,128)(2,1)S(1)}, bf16[1024,1024]{1,0:T(8,128)(2,1)S(1)}, u32[]{:S(2)}, u32[]{:S(2)}) collective-permute-start(bf16[1024,1024]{1,0:T(8,128)(2,1)S(1)} %dynamic-slice_bitcast_fusion.1), channel_id=1, source_target_pairs={{0,8},{8,0},{1,9},{9,1},{2,10},{10,2},{3,11},{11,3},{4,12},{12,4},... | collective-permute-start | bytes 6291464 | tf_op jit(solution)/shard_map/ppermute | solution.py:363
  8.3 13.2 %all_to_all.66 = f32[8,9,1,128]{3,2,1,0:T(1,128)S(1)} all-to-all(f32[8,9,1,128]{3,2,1,0:T(1,128)S(1)} %bitcast.22), channel_id=1, replica_groups=mesh['y'=4,'x'=4,'core'=2,'sec'=8] {'sec'}, dimensions={0} | all-to-all | bytes 73728 | tf_op jit(solution)/shard_map/all_to_all | solution.py:137
  21.5 0.0 collective-permute-done.env2_ref
  21.5 0.0 copy-start.1
  21.5 1.9 shard_map.69
  23.4 0.3 copy-done.1
  23.7 0.2 dynamic-slice_bitcast_fusion
  23.9 1.5 collective-permute-start.1
  25.4 20.4 %all_to_all.67.moved_ref = bf16[8,2,128,128]{3,2,1,0:T(8,128)(2,1)S(1)} all-to-all(bf16[8,2,128,128]{3,2,1,0:T(8,128)(2,1)S(1)} %get-tuple-element.41), channel_id=1, replica_groups=mesh['y'=4,'x'=4,'core'=2,'sec'=8] {'sec'}, dimensions={0} | all-to-all | bytes 1048576 | tf_op jit(solution)/shard_map/all_to_all | solution.py:137
  45.8 0.0 copy-start.2
  45.8 0.0 collective-permute-done.1.got_ref
  45.8 2.5 %shard_map.70 = s16[16,80,128]{2,1,0:T(8,128)(2,1)S(1)} custom-call(s32[4,2]{1,0:T(4,128)S(1)} %select_select_fusion.meta_ref, bf16[8,2,128,128]{3,2,1,0:T(8,128)(2,1)S(1)} %all_to_all.67.moved_ref, bf16[1,2,1024,1024]{3,2,1,0:T(8,128)(2,1)S(1)} %copy-done.1, bf16[1024,1024]{1,0:T(8,128)(2,1)S(1)} %collective-permute-done.1.got_ref), custom_call_target="tpu_custom_call" | custom-call | flops 536870912 | bytes 6815776 | tf_op jit(solution)/shard_map/pallas_call | solution.py:30
  48.3 15.3 %all_to_all.68.got_ref = s16[16,80,128]{2,1,0:T(8,128)(2,1)S(1)} all-to-all(s16[16,80,128]{2,1,0:T(8,128)(2,1)S(1)} %shard_map.70), channel_id=1, replica_groups=mesh['y'=4,'x'=4,'core'=2,'sec'=8] {'y','x'}, dimensions={0} | all-to-all | bytes 655360 | tf_op jit(solution)/shard_map/all_to_all | solution.py:137
  63.6 0.0 copy-done.2
  63.6 0.9 shard_map.71
  64.5 11.3 %all_to_all.69 = f32[16,9,1,128]{3,2,1,0:T(1,128)S(1)} all-to-all(f32[16,9,1,128]{3,2,1,0:T(1,128)S(1)} %bitcast.20), channel_id=1, replica_groups=mesh['y'=4,'x'=4,'core'=2,'sec'=8] {'core','sec'}, dimensions={0} | all-to-all | bytes 147456 | tf_op jit(solution)/shard_map/all_to_all | solution.py:137
  75.7 0.9 shard_map.72
  76.6 10.8 %all_to_all.70.got_ref = s16[16,80,128]{2,1,0:T(8,128)(2,1)S(1)} all-to-all(s16[16,80,128]{2,1,0:T(8,128)(2,1)S(1)} %get-tuple-element.45), channel_id=1, replica_groups=mesh['y'=4,'x'=4,'core'=2,'sec'=8] {'y','x'}, dimensions={0} | all-to-all | bytes 655360 | tf_op jit(solution)/shard_map/all_to_all | solution.py:137
  87.4 2.1 %shard_map.73 = (f32[1024,128]{1,0:T(8,128)S(1)}, f32[1024,128]{1,0:T(8,128)S(1)}, f32[8,1024]{1,0:T(8,128)S(1)}, f32[8,128]{1,0:T(8,128)S(1)}, bf16[8,2,128,128]{3,2,1,0:T(8,128)(2,1)S(1)}) custom-call(s32[4,2]{1,0:T(4,128)S(1)} %select_select_fusion.meta_ref, s16[16,80,128]{2,1,0:T(8,128)(2,1)S(1)} %all_to_all.70.got_ref, ...), custom_call_target="tpu_custom_call" | custom-call | flops 536870912 | bytes 8290336 | tf_op jit(solution)/shard_map/pallas_call | solution.py:30
  89.6 17.6 %all_to_all.71.moved_ref = bf16[8,2,128,128]{3,2,1,0:T(8,128)(2,1)S(1)} all-to-all(bf16[8,2,128,128]{3,2,1,0:T(8,128)(2,1)S(1)} %get-tuple-element.49), channel_id=1, replica_groups=mesh['y'=4,'x'=4,'core'=2,'sec'=8] {'sec'}, dimensions={0} | all-to-all | bytes 1048576 | tf_op jit(solution)/shard_map/all_to_all | solution.py:137
  107.2 2.1 shard_map.74
  109.3 10.7 %all_to_all.72.got_ref = bf16[16,8,1024]{2,1,0:T(8,128)(2,1)S(1)} all-to-all(bf16[16,8,1024]{2,1,0:T(8,128)(2,1)S(1)} %shard_map.74), channel_id=1, replica_groups=mesh['y'=4,'x'=4,'core'=2,'sec'=8] {'y','x'}, dimensions={0} | all-to-all | bytes 524288 | tf_op jit(solution)/shard_map/all_to_all | solution.py:137
  120.0 0.7 shard_map.75
  120.7 14.4 %all_to_all.73 = f32[16,9,1,128]{3,2,1,0:T(1,128)S(1)} all-to-all(f32[16,9,1,128]{3,2,1,0:T(1,128)S(1)} %bitcast.21), channel_id=1, replica_groups=mesh['y'=4,'x'=4,'core'=2,'sec'=8] {'core','sec'}, dimensions={0} | all-to-all | bytes 147456 | tf_op jit(solution)/shard_map/all_to_all | solution.py:137
  135.1 0.9 shard_map.76
  136.0 10.7 %all_to_all.74.got_ref = s16[16,80,128]{2,1,0:T(8,128)(2,1)S(1)} all-to-all(s16[16,80,128]{2,1,0:T(8,128)(2,1)S(1)} %shard_map.76), channel_id=1, replica_groups=mesh['y'=4,'x'=4,'core'=2,'sec'=8] {'y','x'}, dimensions={0} | all-to-all | bytes 655360 | tf_op jit(solution)/shard_map/all_to_all | solution.py:137
  146.7 2.7 %shard_map.77 = (f32[1024,128]{1,0:T(8,128)S(1)}, f32[1024,128]{1,0:T(8,128)S(1)}, f32[8,1024]{1,0:T(8,128)S(1)}, f32[8,1024]{1,0:T(8,128)S(1)}, f32[8,1024]{1,0...) custom-call(s32[4,2]{1,0:T(4,128)S(1)} %select_select_fusion.meta_ref, ...), custom_call_target="tpu_custom_call" | custom-call | flops 536870912 | bytes 9408544 | tf_op jit(solution)/shard_map/pallas_call | solution.py:30
  149.4 17.7 %all_to_all.75.moved_ref = bf16[8,2,128,128]{3,2,1,0:T(8,128)(2,1)S(1)} all-to-all(bf16[8,2,128,128]{3,2,1,0:T(8,128)(2,1)S(1)} %get-tuple-element.56), channel_id=1, replica_groups=mesh['y'=4,'x'=4,'core'=2,'sec'=8] {'sec'}, dimensions={0} | all-to-all | bytes 1048576 | tf_op jit(solution)/shard_map/all_to_all | solution.py:137
  167.2 2.1 shard_map.78
  169.2 10.7 %all_to_all.76.got_ref = bf16[16,8,1024]{2,1,0:T(8,128)(2,1)S(1)} all-to-all(bf16[16,8,1024]{2,1,0:T(8,128)(2,1)S(1)} %shard_map.78), channel_id=1, replica_groups=mesh['y'=4,'x'=4,'core'=2,'sec'=8] {'y','x'}, dimensions={0} | all-to-all | bytes 524288 | tf_op jit(solution)/shard_map/all_to_all | solution.py:137
  180.0 4.7 %collective-permute-start.2 = (f32[1024,128]{1,0:T(8,128)S(1)}, f32[1024,128]{1,0:T(8,128)S(1)}, u32[]{:S(2)}, u32[]{:S(2)}) collective-permute-start(f32[1024,128]{1,0:T(8,128)S(1)} %get-tuple-element.64.u_a_ref), channel_id=1, source_target_pairs={{0,8},{8,0},{1,9},{9,1},{2,10},{10,2},{3,11},{11,3},{4,12},{12,4},... | collective-permute-start | bytes 1572872 | tf_op jit(solution)/shard_map/ppermute | solution.py:417
  184.7 0.0 collective-permute-start.3
  184.7 0.7 shard_map.79
  185.4 18.4 %all_to_all.77 = f32[256,1,128]{2,1,0:T(1,128)S(1)} all-to-all(f32[256,1,128]{2,1,0:T(1,128)S(1)} %bitcast.16), channel_id=1, replica_groups=mesh['y'=4,'x'=4,'core'=2,'sec'=8] {'y','x','core','sec'}, dimensions={0} | all-to-all | bytes 262144 | tf_op jit(solution)/shard_map/all_to_all | solution.py:137
  203.8 0.0 collective-permute-done.2.u_far_ref
  203.8 0.0 collective-permute-done.3.corr_far_ref
  203.8 2.4 %shard_map.80 = (f32[2,1024,128]{2,1,0:T(8,128)}, f32[1,1]{1,0:T(1,128)}) custom-call(s32[4,2]{1,0:T(4,128)S(1)} %select_select_fusion.meta_ref, f32[256,128]{1,0:T(8,128)S(1)} %bitcast.15, f32[8,128]{1,0:T(8,128)S(1)} %get-tuple-element.63.theta_ref, f32[1024,128]{1,0:T(8,128)S(1)} %get-tuple-element.64.u_a_ref, ...), custom_call_target="tpu_custom_call" | custom-call | bytes 2232352 | tf_op jit(solution)/shard_map/pallas_call | solution.py:30
  (2 shorter events, 0.0 us)
Async XLA Ops:
  1.4 1.2 copy-start.3
  2.7 2.2 %copy-start = (bf16[1,2,1024,1024]{3,2,1,0:T(8,128)(2,1)S(1)}, bf16[1,2,1024,1024]{3,2,1,0:T(8,128)(2,1)}, u32[]{:S(2)}) copy-start(bf16[1,2,1024,1024]{3,2,1,0:T(8,128)(2,1)} %env_ref.4) | copy-start | bytes 12582916
  5.0 16.5 %collective-permute-start = (bf16[1024,1024]{1,0:T(8,128)(2,1)S(1)}, bf16[1024,1024]{1,0:T(8,128)(2,1)S(1)}, u32[]{:S(2)}, u32[]{:S(2)}) collective-permute-start(bf16[1024,1024]{1,0:T(8,128)(2,1)S(1)} %dynamic-slice_bitcast_fusion.1), channel_id=1, source_target_pairs={{0,8},{8,0},{1,9},{9,1},{2,10},{10,2},{3,11},{11,3},{4,12},{12,4},... | collective-permute-start | bytes 6291464 | tf_op jit(solution)/shard_map/ppermute | solution.py:363
  21.5 2.2 %copy-start.1 = (bf16[1,2,1024,1024]{3,2,1,0:T(8,128)(2,1)S(1)}, bf16[1,2,1024,1024]{3,2,1,0:T(8,128)(2,1)}, u32[]{:S(2)}) copy-start(bf16[1,2,1024,1024]{3,2,1,0:T(8,128)(2,1)} %env_ref.5) | copy-start | bytes 12582916
  23.9 22.0 %collective-permute-start.1 = (bf16[1024,1024]{1,0:T(8,128)(2,1)S(1)}, bf16[1024,1024]{1,0:T(8,128)(2,1)S(1)}, u32[]{:S(2)}, u32[]{:S(2)}) collective-permute-start(bf16[1024,1024]{1,0:T(8,128)(2,1)S(1)} %dynamic-slice_bitcast_fusion), channel_id=1, source_target_pairs={{0,8},{8,0},{1,9},{9,1},{2,10},{10,2},{3,11},{11,3},{4,12},{12,4},... | collective-permute-start | bytes 6291464 | tf_op jit(solution)/shard_map/ppermute | solution.py:363
  45.8 17.8 %copy-start.2 = (f32[2,1024,128]{2,1,0:T(8,128)S(1)}, f32[2,1024,128]{2,1,0:T(8,128)}, u32[]{:S(2)}) copy-start(f32[2,1024,128]{2,1,0:T(8,128)} %diag_ref.5) | copy-start | bytes 3145732
  180.0 23.9 %collective-permute-start.2 = (f32[1024,128]{1,0:T(8,128)S(1)}, f32[1024,128]{1,0:T(8,128)S(1)}, u32[]{:S(2)}, u32[]{:S(2)}) collective-permute-start(f32[1024,128]{1,0:T(8,128)S(1)} %get-tuple-element.64.u_a_ref), channel_id=1, source_target_pairs={{0,8},{8,0},{1,9},{9,1},{2,10},{10,2},{3,11},{11,3},{4,12},{12,4},... | collective-permute-start | bytes 1572872 | tf_op jit(solution)/shard_map/ppermute | solution.py:417
  184.7 19.1 %collective-permute-start.3 = (f32[1024,128]{1,0:T(8,128)S(1)}, f32[1024,128]{1,0:T(8,128)S(1)}, u32[]{:S(2)}, u32[]{:S(2)}) collective-permute-start(f32[1024,128]{1,0:T(8,128)S(1)} %get-tuple-element.65.corr_a_ref), channel_id=1, source_target_pairs={{0,8},{8,0},{1,9},{9,1},{2,10},{10,2},{3,11},{11,3},{4,12},{12,4},... | collective-permute-start | bytes 1572872 | tf_op jit(solution)/shard_map/ppermute | solution.py:418

commit v9 on v8

--- a/solution.py
+++ b/solution.py
@@ -211,16 +211,19 @@
         def first_right_kernel(meta_ref, moved_ref, env_ref, got_ref, out_ref):
             parts = [total for _, total in right_pieces(meta_ref, moved_ref, env_ref, got_ref)]
             partial = jnp.concatenate(parts, axis=1)
-            largest = jnp.max(jnp.max(jnp.abs(partial), axis=0, keepdims=True), axis=1, keepdims=True)
-            exponent = exponent_of(largest)
-            partial = whole(partial * power(-exponent) * RANGE)
-            tile = jnp.broadcast_to(exponent, (TILE, cols)).astype(jnp.int32).astype(I16)
+            sizes = jnp.abs(partial)
+            rows = [
+                jnp.max(sizes[j * sub : (j + 1) * sub], axis=0, keepdims=True) for j in range(n_xy)
+            ]
+            exponents = exponent_of(jnp.max(jnp.concatenate(rows, axis=0), axis=1, keepdims=True))
+            scales = power(-exponents)
+            tiles = jnp.broadcast_to(exponents, (n_xy, cols))
             for j in range(n_xy):
-                rows = partial[j * sub : (j + 1) * sub]
+                rows = partial[j * sub : (j + 1) * sub] * scales[j : j + 1] * RANGE
                 rows = [rows[:, k * cols : (k + 1) * cols] for k in range(n_z)]
-                block = jnp.concatenate(rows, axis=0).astype(jnp.int32).astype(I16)
-                out_ref[j, :shard_rows] = block
-                out_ref[j, shard_rows:] = tile
+                tile = jnp.broadcast_to(tiles[j : j + 1], (TILE, cols))
+                block = jnp.concatenate([whole(jnp.concatenate(rows, axis=0)), tile], axis=0)
+                out_ref[j] = block.astype(jnp.int32).astype(I16)
 
         def first_sum(got_ref):
             tiles = [got_ref[j, shard_rows:].astype(jnp.int32).astype(F32) for j in range(n_xy)]

time: 207 us -> 207 us (level)
  no operation moved by 1% of the time
where the time goes in v9:
time: 207 us; the launch traced here: 206 us
  blocking collectives  171 us (83%)
  Pallas kernels  20.8 us (10%)
  starting transfers between devices  9.61 us (5%)
  local copies, waits for them, and re-layouts  2.99 us (1%)
    all_to_all x12, blocking collectives, a2a(): return lax.all_to_all(array, axes, 0, 0, tiled=True)  171 us
    pallas_call x13, Pallas kernels, call(): pl.pallas_call(kernel, out_shape=[jax.ShapeDtypeStruct(s, d) for s, d in...  20.8 us
    ppermute x2, starting transfers between devices, swapped(): return lax.ppermute(give.reshape(size, size), 'core', swap)  4.87 us
    ppermute x1, starting transfers between devices, per_device(): u_far = lax.ppermute(u_send, 'core', swap)  4.74 us
  transfers between devices with their start and end apart: 4, of which 0 were waited for; matrix products, arithmetic and copies ran while one was open for 0% of the time, Pallas kernels for 0%

profile of v9, /device:TPU:1, one launch (start us, length us, event | category | flops | bytes accessed | tf_op | source)
XLA Modules:
  0.0 206.3 jit_solution(17019256085353644156)
XLA Ops:
  0.7 0.8 select_select_fusion.meta_ref
  1.4 0.0 copy-start.3
  1.4 1.2 copy-done.3
  2.7 0.0 copy-start
  2.7 1.0 shard_map.68
  3.7 1.2 copy-done
  4.8 0.2 dynamic-slice_bitcast_fusion.1
  5.0 3.3 %collective-permute-start = (bf16[1024,1024]{1,0:T(8,128)(2,1)S(1)}, bf16[1024,1024]{1,0:T(8,128)(2,1)S(1)}, u32[]{:S(2)}, u32[]{:S(2)}) collective-permute-start(bf16[1024,1024]{1,0:T(8,128)(2,1)S(1)} %dynamic-slice_bitcast_fusion.1), channel_id=1, source_target_pairs={{0,8},{8,0},{1,9},{9,1},{2,10},{10,2},{3,11},{11,3},{4,12},{12,4},... | collective-permute-start | bytes 6291464 | tf_op jit(solution)/shard_map/ppermute | solution.py:366
  8.3 13.2 %all_to_all.66 = f32[8,9,1,128]{3,2,1,0:T(1,128)S(1)} all-to-all(f32[8,9,1,128]{3,2,1,0:T(1,128)S(1)} %bitcast.22), channel_id=1, replica_groups=mesh['y'=4,'x'=4,'core'=2,'sec'=8] {'sec'}, dimensions={0} | all-to-all | bytes 73728 | tf_op jit(solution)/shard_map/all_to_all | solution.py:137
  21.5 0.0 collective-permute-done.env2_ref
  21.5 0.0 copy-start.1
  21.5 1.9 shard_map.69
  23.4 0.3 copy-done.1
  23.7 0.2 dynamic-slice_bitcast_fusion
  23.9 1.5 collective-permute-start.1
  25.4 20.4 %all_to_all.67.moved_ref = bf16[8,2,128,128]{3,2,1,0:T(8,128)(2,1)S(1)} all-to-all(bf16[8,2,128,128]{3,2,1,0:T(8,128)(2,1)S(1)} %get-tuple-element.41), channel_id=1, replica_groups=mesh['y'=4,'x'=4,'core'=2,'sec'=8] {'sec'}, dimensions={0} | all-to-all | bytes 1048576 | tf_op jit(solution)/shard_map/all_to_all | solution.py:137
  45.8 0.0 copy-start.2
  45.8 0.0 collective-permute-done.1.got_ref
  45.8 2.5 %shard_map.70 = s16[16,80,128]{2,1,0:T(8,128)(2,1)S(1)} custom-call(s32[4,2]{1,0:T(4,128)S(1)} %select_select_fusion.meta_ref, bf16[8,2,128,128]{3,2,1,0:T(8,128)(2,1)S(1)} %all_to_all.67.moved_ref, bf16[1,2,1024,1024]{3,2,1,0:T(8,128)(2,1)S(1)} %copy-done.1, bf16[1024,1024]{1,0:T(8,128)(2,1)S(1)} %collective-permute-done.1.got_ref), custom_call_target="tpu_custom_call" | custom-call | flops 536870912 | bytes 6815776 | tf_op jit(solution)/shard_map/pallas_call | solution.py:30
  48.3 15.3 %all_to_all.68.got_ref = s16[16,80,128]{2,1,0:T(8,128)(2,1)S(1)} all-to-all(s16[16,80,128]{2,1,0:T(8,128)(2,1)S(1)} %shard_map.70), channel_id=1, replica_groups=mesh['y'=4,'x'=4,'core'=2,'sec'=8] {'y','x'}, dimensions={0} | all-to-all | bytes 655360 | tf_op jit(solution)/shard_map/all_to_all | solution.py:137
  63.6 0.0 copy-done.2
  63.6 0.9 shard_map.71
  64.5 11.3 %all_to_all.69 = f32[16,9,1,128]{3,2,1,0:T(1,128)S(1)} all-to-all(f32[16,9,1,128]{3,2,1,0:T(1,128)S(1)} %bitcast.20), channel_id=1, replica_groups=mesh['y'=4,'x'=4,'core'=2,'sec'=8] {'core','sec'}, dimensions={0} | all-to-all | bytes 147456 | tf_op jit(solution)/shard_map/all_to_all | solution.py:137
  75.7 0.9 shard_map.72
  76.6 10.8 %all_to_all.70.got_ref = s16[16,80,128]{2,1,0:T(8,128)(2,1)S(1)} all-to-all(s16[16,80,128]{2,1,0:T(8,128)(2,1)S(1)} %get-tuple-element.45), channel_id=1, replica_groups=mesh['y'=4,'x'=4,'core'=2,'sec'=8] {'y','x'}, dimensions={0} | all-to-all | bytes 655360 | tf_op jit(solution)/shard_map/all_to_all | solution.py:137
  87.5 2.1 %shard_map.73 = (f32[1024,128]{1,0:T(8,128)S(1)}, f32[1024,128]{1,0:T(8,128)S(1)}, f32[8,1024]{1,0:T(8,128)S(1)}, f32[8,128]{1,0:T(8,128)S(1)}, bf16[8,2,128,128]{3,2,1,0:T(8,128)(2,1)S(1)}) custom-call(s32[4,2]{1,0:T(4,128)S(1)} %select_select_fusion.meta_ref, s16[16,80,128]{2,1,0:T(8,128)(2,1)S(1)} %all_to_all.70.got_ref, ...), custom_call_target="tpu_custom_call" | custom-call | flops 536870912 | bytes 8290336 | tf_op jit(solution)/shard_map/pallas_call | solution.py:30
  89.6 17.6 %all_to_all.71.moved_ref = bf16[8,2,128,128]{3,2,1,0:T(8,128)(2,1)S(1)} all-to-all(bf16[8,2,128,128]{3,2,1,0:T(8,128)(2,1)S(1)} %get-tuple-element.49), channel_id=1, replica_groups=mesh['y'=4,'x'=4,'core'=2,'sec'=8] {'sec'}, dimensions={0} | all-to-all | bytes 1048576 | tf_op jit(solution)/shard_map/all_to_all | solution.py:137
  107.2 2.1 shard_map.74
  109.3 10.7 %all_to_all.72.got_ref = bf16[16,8,1024]{2,1,0:T(8,128)(2,1)S(1)} all-to-all(bf16[16,8,1024]{2,1,0:T(8,128)(2,1)S(1)} %shard_map.74), channel_id=1, replica_groups=mesh['y'=4,'x'=4,'core'=2,'sec'=8] {'y','x'}, dimensions={0} | all-to-all | bytes 524288 | tf_op jit(solution)/shard_map/all_to_all | solution.py:137
  120.0 0.7 shard_map.75
  120.7 14.4 %all_to_all.73 = f32[16,9,1,128]{3,2,1,0:T(1,128)S(1)} all-to-all(f32[16,9,1,128]{3,2,1,0:T(1,128)S(1)} %bitcast.21), channel_id=1, replica_groups=mesh['y'=4,'x'=4,'core'=2,'sec'=8] {'core','sec'}, dimensions={0} | all-to-all | bytes 147456 | tf_op jit(solution)/shard_map/all_to_all | solution.py:137
  135.1 0.9 shard_map.76
  136.0 10.7 %all_to_all.74.got_ref = s16[16,80,128]{2,1,0:T(8,128)(2,1)S(1)} all-to-all(s16[16,80,128]{2,1,0:T(8,128)(2,1)S(1)} %shard_map.76), channel_id=1, replica_groups=mesh['y'=4,'x'=4,'core'=2,'sec'=8] {'y','x'}, dimensions={0} | all-to-all | bytes 655360 | tf_op jit(solution)/shard_map/all_to_all | solution.py:137
  146.7 2.7 %shard_map.77 = (f32[1024,128]{1,0:T(8,128)S(1)}, f32[1024,128]{1,0:T(8,128)S(1)}, f32[8,1024]{1,0:T(8,128)S(1)}, f32[8,1024]{1,0:T(8,128)S(1)}, f32[8,1024]{1,0...) custom-call(s32[4,2]{1,0:T(4,128)S(1)} %select_select_fusion.meta_ref, ...), custom_call_target="tpu_custom_call" | custom-call | flops 536870912 | bytes 9408544 | tf_op jit(solution)/shard_map/pallas_call | solution.py:30
  149.5 17.7 %all_to_all.75.moved_ref = bf16[8,2,128,128]{3,2,1,0:T(8,128)(2,1)S(1)} all-to-all(bf16[8,2,128,128]{3,2,1,0:T(8,128)(2,1)S(1)} %get-tuple-element.56), channel_id=1, replica_groups=mesh['y'=4,'x'=4,'core'=2,'sec'=8] {'sec'}, dimensions={0} | all-to-all | bytes 1048576 | tf_op jit(solution)/shard_map/all_to_all | solution.py:137
  167.2 2.1 shard_map.78
  169.2 10.8 %all_to_all.76.got_ref = bf16[16,8,1024]{2,1,0:T(8,128)(2,1)S(1)} all-to-all(bf16[16,8,1024]{2,1,0:T(8,128)(2,1)S(1)} %shard_map.78), channel_id=1, replica_groups=mesh['y'=4,'x'=4,'core'=2,'sec'=8] {'y','x'}, dimensions={0} | all-to-all | bytes 524288 | tf_op jit(solution)/shard_map/all_to_all | solution.py:137
  180.0 4.7 %collective-permute-start.2 = (f32[1024,128]{1,0:T(8,128)S(1)}, f32[1024,128]{1,0:T(8,128)S(1)}, u32[]{:S(2)}, u32[]{:S(2)}) collective-permute-start(f32[1024,128]{1,0:T(8,128)S(1)} %get-tuple-element.64.u_a_ref), channel_id=1, source_target_pairs={{0,8},{8,0},{1,9},{9,1},{2,10},{10,2},{3,11},{11,3},{4,12},{12,4},... | collective-permute-start | bytes 1572872 | tf_op jit(solution)/shard_map/ppermute | solution.py:420
  184.7 0.0 collective-permute-start.3
  184.7 0.7 shard_map.79
  185.5 18.4 %all_to_all.77 = f32[256,1,128]{2,1,0:T(1,128)S(1)} all-to-all(f32[256,1,128]{2,1,0:T(1,128)S(1)} %bitcast.16), channel_id=1, replica_groups=mesh['y'=4,'x'=4,'core'=2,'sec'=8] {'y','x','core','sec'}, dimensions={0} | all-to-all | bytes 262144 | tf_op jit(solution)/shard_map/all_to_all | solution.py:137
  203.9 0.0 collective-permute-done.2.u_far_ref
  203.9 0.0 collective-permute-done.3.corr_far_ref
  203.9 2.4 %shard_map.80 = (f32[2,1024,128]{2,1,0:T(8,128)}, f32[1,1]{1,0:T(1,128)}) custom-call(s32[4,2]{1,0:T(4,128)S(1)} %select_select_fusion.meta_ref, f32[256,128]{1,0:T(8,128)S(1)} %bitcast.15, f32[8,128]{1,0:T(8,128)S(1)} %get-tuple-element.63.theta_ref, f32[1024,128]{1,0:T(8,128)S(1)} %get-tuple-element.64.u_a_ref, ...), custom_call_target="tpu_custom_call" | custom-call | bytes 2232352 | tf_op jit(solution)/shard_map/pallas_call | solution.py:30
  (2 shorter events, 0.0 us)
Async XLA Ops:
  1.4 1.2 copy-start.3
  2.7 2.2 %copy-start = (bf16[1,2,1024,1024]{3,2,1,0:T(8,128)(2,1)S(1)}, bf16[1,2,1024,1024]{3,2,1,0:T(8,128)(2,1)}, u32[]{:S(2)}) copy-start(bf16[1,2,1024,1024]{3,2,1,0:T(8,128)(2,1)} %env_ref.4) | copy-start | bytes 12582916
  5.0 16.5 %collective-permute-start = (bf16[1024,1024]{1,0:T(8,128)(2,1)S(1)}, bf16[1024,1024]{1,0:T(8,128)(2,1)S(1)}, u32[]{:S(2)}, u32[]{:S(2)}) collective-permute-start(bf16[1024,1024]{1,0:T(8,128)(2,1)S(1)} %dynamic-slice_bitcast_fusion.1), channel_id=1, source_target_pairs={{0,8},{8,0},{1,9},{9,1},{2,10},{10,2},{3,11},{11,3},{4,12},{12,4},... | collective-permute-start | bytes 6291464 | tf_op jit(solution)/shard_map/ppermute | solution.py:366
  21.5 2.2 %copy-start.1 = (bf16[1,2,1024,1024]{3,2,1,0:T(8,128)(2,1)S(1)}, bf16[1,2,1024,1024]{3,2,1,0:T(8,128)(2,1)}, u32[]{:S(2)}) copy-start(bf16[1,2,1024,1024]{3,2,1,0:T(8,128)(2,1)} %env_ref.5) | copy-start | bytes 12582916
  23.9 22.0 %collective-permute-start.1 = (bf16[1024,1024]{1,0:T(8,128)(2,1)S(1)}, bf16[1024,1024]{1,0:T(8,128)(2,1)S(1)}, u32[]{:S(2)}, u32[]{:S(2)}) collective-permute-start(bf16[1024,1024]{1,0:T(8,128)(2,1)S(1)} %dynamic-slice_bitcast_fusion), channel_id=1, source_target_pairs={{0,8},{8,0},{1,9},{9,1},{2,10},{10,2},{3,11},{11,3},{4,12},{12,4},... | collective-permute-start | bytes 6291464 | tf_op jit(solution)/shard_map/ppermute | solution.py:366
  45.8 17.8 %copy-start.2 = (f32[2,1024,128]{2,1,0:T(8,128)S(1)}, f32[2,1024,128]{2,1,0:T(8,128)}, u32[]{:S(2)}) copy-start(f32[2,1024,128]{2,1,0:T(8,128)} %diag_ref.5) | copy-start | bytes 3145732
  180.0 23.9 %collective-permute-start.2 = (f32[1024,128]{1,0:T(8,128)S(1)}, f32[1024,128]{1,0:T(8,128)S(1)}, u32[]{:S(2)}, u32[]{:S(2)}) collective-permute-start(f32[1024,128]{1,0:T(8,128)S(1)} %get-tuple-element.64.u_a_ref), channel_id=1, source_target_pairs={{0,8},{8,0},{1,9},{9,1},{2,10},{10,2},{3,11},{11,3},{4,12},{12,4},... | collective-permute-start | bytes 1572872 | tf_op jit(solution)/shard_map/ppermute | solution.py:420
  184.7 19.1 %collective-permute-start.3 = (f32[1024,128]{1,0:T(8,128)S(1)}, f32[1024,128]{1,0:T(8,128)S(1)}, u32[]{:S(2)}, u32[]{:S(2)}) collective-permute-start(f32[1024,128]{1,0:T(8,128)S(1)} %get-tuple-element.65.corr_a_ref), channel_id=1, source_target_pairs={{0,8},{8,0},{1,9},{9,1},{2,10},{10,2},{3,11},{11,3},{4,12},{12,4},... | collective-permute-start | bytes 1572872 | tf_op jit(solution)/shard_map/ppermute | solution.py:421

commit v10 on v9

--- a/solution.py
+++ b/solution.py
@@ -10,7 +10,7 @@
 ITERS = 2
 XY = ("y", "x")
 CZ = ("core", "sec")
-ALL = ("y", "x", "core", "sec")
+ALL = ("core", "sec", "y", "x")
 LANES = 128
 PIECE = 1024
 TILE = 16
@@ -321,7 +321,7 @@
             corr_b_ref[...] = correction(theta, hu_b_ref[...], u_b_ref[...], diag_b_ref[...])
             left_matmul(meta_ref, env_ref, env2_ref, corr_a.astype(BF16), left_ref)
 
-        def update_kernel(meta_ref, got_ref, old_theta_ref, u_a_ref, corr_a_ref, hu_a_ref, u_b_ref, corr_b_ref, hu_b_ref, hc_b_ref, diag_ref, diag_b_ref, env_ref, env2_ref, u_a_out, corr_a_out, u_b_out, corr_b_out, hu_b_out, theta_ref, left_ref, *hu_a_out):
+        def update_kernel(meta_ref, got_ref, old_theta_ref, u_a_ref, corr_a_ref, hu_a_ref, u_b_ref, corr_b_ref, hu_b_ref, hc_b_ref, diag_ref, diag_b_ref, env_ref, env2_ref, pair_out, u_b_out, corr_b_out, hu_b_out, theta_ref, left_ref, *hu_a_out):
             blocks, line = decode(got_ref, n_xy)
             sums = [line[:, k : k + 1] * scale for k in range(6)]
             old, new, theta, _ = projected(old_theta_ref[0:1, 0:1], sums)
@@ -329,7 +329,7 @@
             u_a = old * u_a_ref[...] + new * corr_a_ref[...]
             hu_a = old * hu_a_ref[...] + new * share_of(blocks)
             corr_a = correction(theta, hu_a, u_a, diag_ref[place(meta_ref)[0]])
-            u_a_out[...], corr_a_out[...] = u_a, corr_a
+            pair_out[0], pair_out[1] = u_a, corr_a
             for ref in hu_a_out:
                 ref[...] = hu_a
             u_b = old * u_b_ref[...] + new * corr_b_ref[...]
@@ -338,14 +338,14 @@
             corr_b_out[...] = correction(theta, hu_b, u_b, diag_b_ref[...])
             left_matmul(meta_ref, env_ref, env2_ref, corr_a.astype(BF16), left_ref)
 
-        def last_kernel(meta_ref, got_ref, theta_ref, u_a_ref, corr_a_ref, u_far_ref, corr_far_ref, out_ref, energy_ref):
+        def last_kernel(meta_ref, got_ref, theta_ref, pair_ref, far_ref, out_ref, energy_ref):
             line = jnp.sum(got_ref[...], axis=0, keepdims=True) * scale
             sums = [line[:, k : k + 1] for k in range(6)]
             old, new, _, lowest = projected(theta_ref[0:1, 0:1], sums)
             c = place(meta_ref)[0]
             energy_ref[...] = lowest
-            out_ref[c] = old * u_a_ref[...] + new * corr_a_ref[...]
-            out_ref[1 - c] = old * u_far_ref[...] + new * corr_far_ref[...]
+            out_ref[c] = old * pair_ref[0] + new * pair_ref[1]
+            out_ref[1 - c] = old * far_ref[0] + new * far_ref[1]
 
         def v(*arrays):
             return [(a, VMEM) for a in arrays]
@@ -408,24 +408,24 @@
             )
             got = a2a(payload, XY)
             more = [a_out] * (step < ITERS - 2)
-            u_a, corr_a, u_b, corr_b, hu_b, theta, left, *more = call(
+            pair, u_b, corr_b, hu_b, theta, left, *more = call(
                 update_kernel,
-                [a_out, a_out, b_out, b_out, b_out, tile_out, left_out] + more,
+                [((2, *share), F32), b_out, b_out, b_out, tile_out, left_out] + more,
                 i_meta + v(got, theta, u_a, corr_a, hu_a, u_b, corr_b, hu_b, hc_b, diag, diag_b) + lefts,
                 (), work,
             )
             (hu_a,) = more or (None,)
+            u_a, corr_a = pair[0], pair[1]
         got = apply_right(left, right_kernel, summed)
-        got, u_send, corr_send = lax.optimization_barrier((got, u_a, corr_a))
-        u_far = lax.ppermute(u_send, "core", swap)
-        corr_far = lax.ppermute(corr_send, "core", swap)
+        got, pair = lax.optimization_barrier((got, pair))
+        far = lax.ppermute(pair, "core", swap)
         (sums,) = call(
             last_image_kernel, [((2 * n_z * n_xy, cols), F32)], i_meta + v(got, u_b, corr_b, hu_b)
         )
         sums = a2a(sums, ALL)
         out, energy = call(
             last_kernel, [(psi.shape, F32), ((1, 1), F32)],
-            i_meta + v(sums, theta, u_a, corr_a, u_far, corr_far),
+            i_meta + v(sums, theta, pair, far),
         )
         return out, energy.reshape(())
 

time: 207 us -> 206 us (level)
    ppermute x2 -> x1, starting transfers between devices: 4.74 us -> 4.74 us  [per_device(): far = lax.ppermute(pair, 'core', swap)]
  transfers between devices with their start and end apart: 4 -> 3, of which waited for: 0 -> 0; matrix products, arithmetic and copies ran while one was open for 0% -> 0% of each run, Pallas kernels for 0% -> 0%
where the time goes in v10:
time: 206 us
  blocking collectives  171 us (83%)
  Pallas kernels  20.8 us (10%)
  starting transfers between devices  9.61 us (5%)
  local copies, waits for them, and re-layouts  2.99 us (1%)
    all_to_all x12, blocking collectives, a2a(): return lax.all_to_all(array, axes, 0, 0, tiled=True)  171 us
    pallas_call x13, Pallas kernels, call(): pl.pallas_call(kernel, out_shape=[jax.ShapeDtypeStruct(s, d) for s, d in...  20.8 us
    ppermute x2, starting transfers between devices, swapped(): return lax.ppermute(give.reshape(size, size), 'core', swap)  4.87 us
    ppermute x1, starting transfers between devices, per_device(): far = lax.ppermute(pair, 'core', swap)  4.74 us
  transfers between devices with their start and end apart: 3, of which 0 were waited for; matrix products, arithmetic and copies ran while one was open for 0% of the time, Pallas kernels for 0%

profile of v10, /device:TPU:1, one launch (start us, length us, event | category | flops | bytes accessed | tf_op | source)
XLA Modules:
  0.0 205.8 jit_solution(11540852256733573124)
XLA Ops:
  0.7 0.8 select_select_fusion.meta_ref
  1.4 0.0 copy-start.3
  1.4 1.2 copy-done.3
  2.7 0.0 copy-start
  2.7 1.0 shard_map.68
  3.7 1.2 copy-done
  4.8 0.2 dynamic-slice_bitcast_fusion.1
  5.0 3.3 %collective-permute-start = (bf16[1024,1024]{1,0:T(8,128)(2,1)S(1)}, bf16[1024,1024]{1,0:T(8,128)(2,1)S(1)}, u32[]{:S(2)}, u32[]{:S(2)}) collective-permute-start(bf16[1024,1024]{1,0:T(8,128)(2,1)S(1)} %dynamic-slice_bitcast_fusion.1), channel_id=1, source_target_pairs={{0,8},{8,0},{1,9},{9,1},{2,10},{10,2},{3,11},{11,3},{4,12},{12,4},... | collective-permute-start | bytes 6291464 | tf_op jit(solution)/shard_map/ppermute | solution.py:366
  8.3 13.2 %all_to_all.66 = f32[8,9,1,128]{3,2,1,0:T(1,128)S(1)} all-to-all(f32[8,9,1,128]{3,2,1,0:T(1,128)S(1)} %bitcast.22), channel_id=1, replica_groups=mesh['y'=4,'x'=4,'core'=2,'sec'=8] {'sec'}, dimensions={0} | all-to-all | bytes 73728 | tf_op jit(solution)/shard_map/all_to_all | solution.py:137
  21.5 0.0 collective-permute-done.env2_ref
  21.5 0.0 copy-start.1
  21.5 1.9 shard_map.69
  23.4 0.3 copy-done.1
  23.7 0.2 dynamic-slice_bitcast_fusion
  23.9 1.5 collective-permute-start.1
  25.4 20.4 %all_to_all.67.moved_ref = bf16[8,2,128,128]{3,2,1,0:T(8,128)(2,1)S(1)} all-to-all(bf16[8,2,128,128]{3,2,1,0:T(8,128)(2,1)S(1)} %get-tuple-element.39), channel_id=1, replica_groups=mesh['y'=4,'x'=4,'core'=2,'sec'=8] {'sec'}, dimensions={0} | all-to-all | bytes 1048576 | tf_op jit(solution)/shard_map/all_to_all | solution.py:137
  45.8 0.0 copy-start.2
  45.8 0.0 collective-permute-done.1.got_ref
  45.8 2.5 %shard_map.70 = s16[16,80,128]{2,1,0:T(8,128)(2,1)S(1)} custom-call(s32[4,2]{1,0:T(4,128)S(1)} %select_select_fusion.meta_ref, bf16[8,2,128,128]{3,2,1,0:T(8,128)(2,1)S(1)} %all_to_all.67.moved_ref, bf16[1,2,1024,1024]{3,2,1,0:T(8,128)(2,1)S(1)} %copy-done.1, bf16[1024,1024]{1,0:T(8,128)(2,1)S(1)} %collective-permute-done.1.got_ref), custom_call_target="tpu_custom_call" | custom-call | flops 536870912 | bytes 6815776 | tf_op jit(solution)/shard_map/pallas_call | solution.py:30
  48.3 15.3 %all_to_all.68.got_ref = s16[16,80,128]{2,1,0:T(8,128)(2,1)S(1)} all-to-all(s16[16,80,128]{2,1,0:T(8,128)(2,1)S(1)} %shard_map.70), channel_id=1, replica_groups=mesh['y'=4,'x'=4,'core'=2,'sec'=8] {'y','x'}, dimensions={0} | all-to-all | bytes 655360 | tf_op jit(solution)/shard_map/all_to_all | solution.py:137
  63.6 0.0 copy-done.2
  63.6 0.9 shard_map.71
  64.5 11.3 %all_to_all.69 = f32[16,9,1,128]{3,2,1,0:T(1,128)S(1)} all-to-all(f32[16,9,1,128]{3,2,1,0:T(1,128)S(1)} %bitcast.20), channel_id=1, replica_groups=mesh['y'=4,'x'=4,'core'=2,'sec'=8] {'core','sec'}, dimensions={0} | all-to-all | bytes 147456 | tf_op jit(solution)/shard_map/all_to_all | solution.py:137
  75.7 0.9 shard_map.72
  76.6 10.8 %all_to_all.70.got_ref = s16[16,80,128]{2,1,0:T(8,128)(2,1)S(1)} all-to-all(s16[16,80,128]{2,1,0:T(8,128)(2,1)S(1)} %get-tuple-element.43), channel_id=1, replica_groups=mesh['y'=4,'x'=4,'core'=2,'sec'=8] {'y','x'}, dimensions={0} | all-to-all | bytes 655360 | tf_op jit(solution)/shard_map/all_to_all | solution.py:137
  87.5 2.1 %shard_map.73 = (f32[1024,128]{1,0:T(8,128)S(1)}, f32[1024,128]{1,0:T(8,128)S(1)}, f32[8,1024]{1,0:T(8,128)S(1)}, f32[8,128]{1,0:T(8,128)S(1)}, bf16[8,2,128,128]{3,2,1,0:T(8,128)(2,1)S(1)}) custom-call(s32[4,2]{1,0:T(4,128)S(1)} %select_select_fusion.meta_ref, s16[16,80,128]{2,1,0:T(8,128)(2,1)S(1)} %all_to_all.70.got_ref, ...), custom_call_target="tpu_custom_call" | custom-call | flops 536870912 | bytes 8290336 | tf_op jit(solution)/shard_map/pallas_call | solution.py:30
  89.6 17.6 %all_to_all.71.moved_ref = bf16[8,2,128,128]{3,2,1,0:T(8,128)(2,1)S(1)} all-to-all(bf16[8,2,128,128]{3,2,1,0:T(8,128)(2,1)S(1)} %get-tuple-element.47), channel_id=1, replica_groups=mesh['y'=4,'x'=4,'core'=2,'sec'=8] {'sec'}, dimensions={0} | all-to-all | bytes 1048576 | tf_op jit(solution)/shard_map/all_to_all | solution.py:137
  107.2 2.1 %shard_map.74 = bf16[16,8,1024]{2,1,0:T(8,128)(2,1)S(1)} custom-call(s32[4,2]{1,0:T(4,128)S(1)} %select_select_fusion.meta_ref, bf16[8,2,128,128]{3,2,1,0:T(8,128)(2,1)S(1)} %all_to_all.71.moved_ref, bf16[1,2,1024,1024]{3,2,1,0:T(8,128)(2,1)S(1)} %copy-done.1, bf16[1024,1024]{1,0:T(8,128)(2,1)S(1)} %collective-permute-done.1.got_ref), custom_call_target="tpu_custom_call" | custom-call | flops 536870912 | bytes 6815776 | tf_op jit(solution)/shard_map/pallas_call | solution.py:30
  109.3 10.7 %all_to_all.72.got_ref = bf16[16,8,1024]{2,1,0:T(8,128)(2,1)S(1)} all-to-all(bf16[16,8,1024]{2,1,0:T(8,128)(2,1)S(1)} %shard_map.74), channel_id=1, replica_groups=mesh['y'=4,'x'=4,'core'=2,'sec'=8] {'y','x'}, dimensions={0} | all-to-all | bytes 524288 | tf_op jit(solution)/shard_map/all_to_all | solution.py:137
  120.0 0.7 shard_map.75
  120.7 14.4 %all_to_all.73 = f32[16,9,1,128]{3,2,1,0:T(1,128)S(1)} all-to-all(f32[16,9,1,128]{3,2,1,0:T(1,128)S(1)} %bitcast.21), channel_id=1, replica_groups=mesh['y'=4,'x'=4,'core'=2,'sec'=8] {'core','sec'}, dimensions={0} | all-to-all | bytes 147456 | tf_op jit(solution)/shard_map/all_to_all | solution.py:137
  135.1 0.9 shard_map.76
  136.0 10.7 %all_to_all.74.got_ref = s16[16,80,128]{2,1,0:T(8,128)(2,1)S(1)} all-to-all(s16[16,80,128]{2,1,0:T(8,128)(2,1)S(1)} %shard_map.76), channel_id=1, replica_groups=mesh['y'=4,'x'=4,'core'=2,'sec'=8] {'y','x'}, dimensions={0} | all-to-all | bytes 655360 | tf_op jit(solution)/shard_map/all_to_all | solution.py:137
  146.7 2.7 %shard_map.77 = (f32[2,1024,128]{2,1,0:T(8,128)S(1)}, f32[8,1024]{1,0:T(8,128)S(1)}, f32[8,1024]{1,0:T(8,128)S(1)}, f32[8,1024]{1,0:T(8,128)S(1)}, f32[8,128]{1,...) custom-call(s32[4,2]{1,0:T(4,128)S(1)} %select_select_fusion.meta_ref, s16[16,80,128]{2,1,0:T(8,128)(2,1)S(1)} %all_to_all.74.got_ref, ...), custom_call_target="tpu_custom_call" | custom-call | flops 536870912 | bytes 9408544 | tf_op jit(solution)/shard_map/pallas_call | solution.py:30
  149.5 17.7 %all_to_all.75.moved_ref = bf16[8,2,128,128]{3,2,1,0:T(8,128)(2,1)S(1)} all-to-all(bf16[8,2,128,128]{3,2,1,0:T(8,128)(2,1)S(1)} %get-tuple-element.54), channel_id=1, replica_groups=mesh['y'=4,'x'=4,'core'=2,'sec'=8] {'sec'}, dimensions={0} | all-to-all | bytes 1048576 | tf_op jit(solution)/shard_map/all_to_all | solution.py:137
  167.2 2.1 shard_map.78
  169.2 10.8 %all_to_all.76.got_ref = bf16[16,8,1024]{2,1,0:T(8,128)(2,1)S(1)} all-to-all(bf16[16,8,1024]{2,1,0:T(8,128)(2,1)S(1)} %shard_map.78), channel_id=1, replica_groups=mesh['y'=4,'x'=4,'core'=2,'sec'=8] {'y','x'}, dimensions={0} | all-to-all | bytes 524288 | tf_op jit(solution)/shard_map/all_to_all | solution.py:137
  180.0 4.7 %collective-permute-start.2 = (f32[2,1024,128]{2,1,0:T(8,128)S(1)}, f32[2,1024,128]{2,1,0:T(8,128)S(1)}, u32[]{:S(2)}, u32[]{:S(2)}) collective-permute-start(f32[2,1024,128]{2,1,0:T(8,128)S(1)} %get-tuple-element.61.pair_ref), channel_id=1, source_target_pairs={{0,8},{8,0},{1,9},{9,1},{2,10},{10,2},{3,11},{11,3},{4,12},{12,4},... | collective-permute-start | bytes 3145736 | tf_op jit(solution)/shard_map/ppermute | solution.py:421
  184.7 0.7 shard_map.79
  185.5 18.0 %all_to_all.77 = f32[256,1,128]{2,1,0:T(1,128)S(1)} all-to-all(f32[256,1,128]{2,1,0:T(1,128)S(1)} %bitcast.16), channel_id=1, replica_groups=mesh['y'=4,'x'=4,'core'=2,'sec'=8] {'core','sec','y','x'}, dimensions={0} | all-to-all | bytes 262144 | tf_op jit(solution)/shard_map/all_to_all | solution.py:137
  203.4 0.0 collective-permute-done.2.far_ref
  203.4 2.4 %shard_map.80 = (f32[2,1024,128]{2,1,0:T(8,128)}, f32[1,1]{1,0:T(1,128)}) custom-call(s32[4,2]{1,0:T(4,128)S(1)} %select_select_fusion.meta_ref, f32[256,128]{1,0:T(8,128)S(1)} %bitcast.15, f32[8,128]{1,0:T(8,128)S(1)} %get-tuple-element.60.theta_ref, f32[2,1024,128]{2,1,0:T(8,128)S(1)} %get-tuple-element.61.pair_ref, ...), custom_call_target="tpu_custom_call" | custom-call | bytes 2232352 | tf_op jit(solution)/shard_map/pallas_call | solution.py:30
  (2 shorter events, 0.0 us)
Async XLA Ops:
  1.4 1.2 copy-start.3
  2.7 2.2 %copy-start = (bf16[1,2,1024,1024]{3,2,1,0:T(8,128)(2,1)S(1)}, bf16[1,2,1024,1024]{3,2,1,0:T(8,128)(2,1)}, u32[]{:S(2)}) copy-start(bf16[1,2,1024,1024]{3,2,1,0:T(8,128)(2,1)} %env_ref.4) | copy-start | bytes 12582916
  5.0 16.5 %collective-permute-start = (bf16[1024,1024]{1,0:T(8,128)(2,1)S(1)}, bf16[1024,1024]{1,0:T(8,128)(2,1)S(1)}, u32[]{:S(2)}, u32[]{:S(2)}) collective-permute-start(bf16[1024,1024]{1,0:T(8,128)(2,1)S(1)} %dynamic-slice_bitcast_fusion.1), channel_id=1, source_target_pairs={{0,8},{8,0},{1,9},{9,1},{2,10},{10,2},{3,11},{11,3},{4,12},{12,4},... | collective-permute-start | bytes 6291464 | tf_op jit(solution)/shard_map/ppermute | solution.py:366
  21.5 2.2 %copy-start.1 = (bf16[1,2,1024,1024]{3,2,1,0:T(8,128)(2,1)S(1)}, bf16[1,2,1024,1024]{3,2,1,0:T(8,128)(2,1)}, u32[]{:S(2)}) copy-start(bf16[1,2,1024,1024]{3,2,1,0:T(8,128)(2,1)} %env_ref.5) | copy-start | bytes 12582916
  23.9 22.0 %collective-permute-start.1 = (bf16[1024,1024]{1,0:T(8,128)(2,1)S(1)}, bf16[1024,1024]{1,0:T(8,128)(2,1)S(1)}, u32[]{:S(2)}, u32[]{:S(2)}) collective-permute-start(bf16[1024,1024]{1,0:T(8,128)(2,1)S(1)} %dynamic-slice_bitcast_fusion), channel_id=1, source_target_pairs={{0,8},{8,0},{1,9},{9,1},{2,10},{10,2},{3,11},{11,3},{4,12},{12,4},... | collective-permute-start | bytes 6291464 | tf_op jit(solution)/shard_map/ppermute | solution.py:366
  45.8 17.8 %copy-start.2 = (f32[2,1024,128]{2,1,0:T(8,128)S(1)}, f32[2,1024,128]{2,1,0:T(8,128)}, u32[]{:S(2)}) copy-start(f32[2,1024,128]{2,1,0:T(8,128)} %diag_ref.5) | copy-start | bytes 3145732
  180.0 23.4 %collective-permute-start.2 = (f32[2,1024,128]{2,1,0:T(8,128)S(1)}, f32[2,1024,128]{2,1,0:T(8,128)S(1)}, u32[]{:S(2)}, u32[]{:S(2)}) collective-permute-start(f32[2,1024,128]{2,1,0:T(8,128)S(1)} %get-tuple-element.61.pair_ref), channel_id=1, source_target_pairs={{0,8},{8,0},{1,9},{9,1},{2,10},{10,2},{3,11},{11,3},{4,12},{12,4},... | collective-permute-start | bytes 3145736 | tf_op jit(solution)/shard_map/ppermute | solution.py:421

commit v11 on v10

--- a/solution.py
+++ b/solution.py
@@ -97,16 +97,16 @@
         rows.append(whole(rest))
         rest = rest - rows[-1]
     rows.append(jnp.zeros((TILE - len(rows), LANES), F32))
-    return jnp.concatenate([block] + rows, axis=0).astype(jnp.int32).astype(I16)
+    return jnp.concatenate([block] + rows, axis=0).astype(I16)
 
 
 def decode(ref, count):
     size = ref.shape[1] - TILE
-    tiles = [ref[j, size:].astype(jnp.int32).astype(F32) for j in range(count)]
+    tiles = [ref[j, size:].astype(F32) for j in range(count)]
     rows = [jnp.concatenate([tile[k : k + 1] for tile in tiles], axis=0) for k in range(5)]
     scales = power(rows[0][:, :1])
     blocks = [
-        ref[j, :size].astype(jnp.int32).astype(F32) * (1.0 / RANGE) * scales[j : j + 1]
+        ref[j, :size].astype(F32) * (1.0 / RANGE) * scales[j : j + 1]
         for j in range(count)
     ]
     line = ((rows[4] / DIGIT + rows[3]) / DIGIT + rows[2]) / DIGIT * power(rows[1][:, :1])
@@ -223,14 +223,14 @@
                 rows = [rows[:, k * cols : (k + 1) * cols] for k in range(n_z)]
                 tile = jnp.broadcast_to(tiles[j : j + 1], (TILE, cols))
                 block = jnp.concatenate([whole(jnp.concatenate(rows, axis=0)), tile], axis=0)
-                out_ref[j] = block.astype(jnp.int32).astype(I16)
+                out_ref[j] = block.astype(I16)
 
         def first_sum(got_ref):
-            tiles = [got_ref[j, shard_rows:].astype(jnp.int32).astype(F32) for j in range(n_xy)]
+            tiles = [got_ref[j, shard_rows:].astype(F32) for j in range(n_xy)]
             scales = power(jnp.concatenate([tile[:1] for tile in tiles], axis=0)[:, :1])
             total = jnp.zeros((shard_rows, cols), F32)
             for j in range(n_xy):
-                block = got_ref[j, :shard_rows].astype(jnp.int32).astype(F32)
+                block = got_ref[j, :shard_rows].astype(F32)
                 total = total + block * (1.0 / RANGE) * scales[j : j + 1]
             return jnp.concatenate([total[k * sub : (k + 1) * sub] for k in range(n_z)], axis=1)
 

time: 206 us -> 207 us (level)
  no operation moved by 1% of the time
where the time goes in v11:
time: 207 us; the launch traced here: 206 us
  blocking collectives  171 us (83%)
  Pallas kernels  20.9 us (10%)
  starting transfers between devices  9.63 us (5%)
  local copies, waits for them, and re-layouts  2.99 us (1%)
    all_to_all x12, blocking collectives, a2a(): return lax.all_to_all(array, axes, 0, 0, tiled=True)  171 us
    pallas_call x13, Pallas kernels, call(): pl.pallas_call(kernel, out_shape=[jax.ShapeDtypeStruct(s, d) for s, d in...  20.9 us
    ppermute x2, starting transfers between devices, swapped(): return lax.ppermute(give.reshape(size, size), 'core', swap)  4.87 us
    ppermute x1, starting transfers between devices, per_device(): far = lax.ppermute(pair, 'core', swap)  4.76 us
  transfers between devices with their start and end apart: 3, of which 0 were waited for; matrix products, arithmetic and copies ran while one was open for 0% of the time, Pallas kernels for 0%

profile of v11, /device:TPU:1, one launch (start us, length us, event | category | flops | bytes accessed | tf_op | source)
XLA Modules:
  0.0 205.9 jit_solution(11909543219945117)
XLA Ops:
  0.7 0.8 select_select_fusion.meta_ref
  1.4 0.0 copy-start.3
  1.4 1.2 copy-done.3
  2.7 0.0 copy-start
  2.7 1.0 shard_map.68
  3.7 1.2 copy-done
  4.8 0.2 dynamic-slice_bitcast_fusion.1
  5.0 3.3 %collective-permute-start = (bf16[1024,1024]{1,0:T(8,128)(2,1)S(1)}, bf16[1024,1024]{1,0:T(8,128)(2,1)S(1)}, u32[]{:S(2)}, u32[]{:S(2)}) collective-permute-start(bf16[1024,1024]{1,0:T(8,128)(2,1)S(1)} %dynamic-slice_bitcast_fusion.1), channel_id=1, source_target_pairs={{0,8},{8,0},{1,9},{9,1},{2,10},{10,2},{3,11},{11,3},{4,12},{12,4},... | collective-permute-start | bytes 6291464 | tf_op jit(solution)/shard_map/ppermute | solution.py:366
  8.3 13.2 %all_to_all.66 = f32[8,9,1,128]{3,2,1,0:T(1,128)S(1)} all-to-all(f32[8,9,1,128]{3,2,1,0:T(1,128)S(1)} %bitcast.22), channel_id=1, replica_groups=mesh['y'=4,'x'=4,'core'=2,'sec'=8] {'sec'}, dimensions={0} | all-to-all | bytes 73728 | tf_op jit(solution)/shard_map/all_to_all | solution.py:137
  21.5 0.0 collective-permute-done.env2_ref
  21.5 0.0 copy-start.1
  21.5 1.9 shard_map.69
  23.4 0.3 copy-done.1
  23.7 0.2 dynamic-slice_bitcast_fusion
  23.9 1.5 collective-permute-start.1
  25.4 20.4 %all_to_all.67.moved_ref = bf16[8,2,128,128]{3,2,1,0:T(8,128)(2,1)S(1)} all-to-all(bf16[8,2,128,128]{3,2,1,0:T(8,128)(2,1)S(1)} %get-tuple-element.39), channel_id=1, replica_groups=mesh['y'=4,'x'=4,'core'=2,'sec'=8] {'sec'}, dimensions={0} | all-to-all | bytes 1048576 | tf_op jit(solution)/shard_map/all_to_all | solution.py:137
  45.8 0.0 copy-start.2
  45.8 0.0 collective-permute-done.1.got_ref
  45.8 2.5 %shard_map.70 = s16[16,80,128]{2,1,0:T(8,128)(2,1)S(1)} custom-call(s32[4,2]{1,0:T(4,128)S(1)} %select_select_fusion.meta_ref, bf16[8,2,128,128]{3,2,1,0:T(8,128)(2,1)S(1)} %all_to_all.67.moved_ref, bf16[1,2,1024,1024]{3,2,1,0:T(8,128)(2,1)S(1)} %copy-done.1, bf16[1024,1024]{1,0:T(8,128)(2,1)S(1)} %collective-permute-done.1.got_ref), custom_call_target="tpu_custom_call" | custom-call | flops 536870912 | bytes 6815776 | tf_op jit(solution)/shard_map/pallas_call | solution.py:30
  48.3 15.3 %all_to_all.68.got_ref = s16[16,80,128]{2,1,0:T(8,128)(2,1)S(1)} all-to-all(s16[16,80,128]{2,1,0:T(8,128)(2,1)S(1)} %shard_map.70), channel_id=1, replica_groups=mesh['y'=4,'x'=4,'core'=2,'sec'=8] {'y','x'}, dimensions={0} | all-to-all | bytes 655360 | tf_op jit(solution)/shard_map/all_to_all | solution.py:137
  63.6 0.0 copy-done.2
  63.6 0.9 shard_map.71
  64.5 11.3 %all_to_all.69 = f32[16,9,1,128]{3,2,1,0:T(1,128)S(1)} all-to-all(f32[16,9,1,128]{3,2,1,0:T(1,128)S(1)} %bitcast.20), channel_id=1, replica_groups=mesh['y'=4,'x'=4,'core'=2,'sec'=8] {'core','sec'}, dimensions={0} | all-to-all | bytes 147456 | tf_op jit(solution)/shard_map/all_to_all | solution.py:137
  75.8 0.9 shard_map.72
  76.6 10.8 %all_to_all.70.got_ref = s16[16,80,128]{2,1,0:T(8,128)(2,1)S(1)} all-to-all(s16[16,80,128]{2,1,0:T(8,128)(2,1)S(1)} %get-tuple-element.43), channel_id=1, replica_groups=mesh['y'=4,'x'=4,'core'=2,'sec'=8] {'y','x'}, dimensions={0} | all-to-all | bytes 655360 | tf_op jit(solution)/shard_map/all_to_all | solution.py:137
  87.5 2.1 %shard_map.73 = (f32[1024,128]{1,0:T(8,128)S(1)}, f32[1024,128]{1,0:T(8,128)S(1)}, f32[8,1024]{1,0:T(8,128)S(1)}, f32[8,128]{1,0:T(8,128)S(1)}, bf16[8,2,128,128]{3,2,1,0:T(8,128)(2,1)S(1)}) custom-call(s32[4,2]{1,0:T(4,128)S(1)} %select_select_fusion.meta_ref, s16[16,80,128]{2,1,0:T(8,128)(2,1)S(1)} %all_to_all.70.got_ref, ...), custom_call_target="tpu_custom_call" | custom-call | flops 536870912 | bytes 8290336 | tf_op jit(solution)/shard_map/pallas_call | solution.py:30
  89.6 17.6 %all_to_all.71.moved_ref = bf16[8,2,128,128]{3,2,1,0:T(8,128)(2,1)S(1)} all-to-all(bf16[8,2,128,128]{3,2,1,0:T(8,128)(2,1)S(1)} %get-tuple-element.47), channel_id=1, replica_groups=mesh['y'=4,'x'=4,'core'=2,'sec'=8] {'sec'}, dimensions={0} | all-to-all | bytes 1048576 | tf_op jit(solution)/shard_map/all_to_all | solution.py:137
  107.2 2.1 %shard_map.74 = bf16[16,8,1024]{2,1,0:T(8,128)(2,1)S(1)} custom-call(s32[4,2]{1,0:T(4,128)S(1)} %select_select_fusion.meta_ref, bf16[8,2,128,128]{3,2,1,0:T(8,128)(2,1)S(1)} %all_to_all.71.moved_ref, bf16[1,2,1024,1024]{3,2,1,0:T(8,128)(2,1)S(1)} %copy-done.1, bf16[1024,1024]{1,0:T(8,128)(2,1)S(1)} %collective-permute-done.1.got_ref), custom_call_target="tpu_custom_call" | custom-call | flops 536870912 | bytes 6815776 | tf_op jit(solution)/shard_map/pallas_call | solution.py:30
  109.3 10.7 %all_to_all.72.got_ref = bf16[16,8,1024]{2,1,0:T(8,128)(2,1)S(1)} all-to-all(bf16[16,8,1024]{2,1,0:T(8,128)(2,1)S(1)} %shard_map.74), channel_id=1, replica_groups=mesh['y'=4,'x'=4,'core'=2,'sec'=8] {'y','x'}, dimensions={0} | all-to-all | bytes 524288 | tf_op jit(solution)/shard_map/all_to_all | solution.py:137
  120.0 0.7 shard_map.75
  120.7 14.4 %all_to_all.73 = f32[16,9,1,128]{3,2,1,0:T(1,128)S(1)} all-to-all(f32[16,9,1,128]{3,2,1,0:T(1,128)S(1)} %bitcast.21), channel_id=1, replica_groups=mesh['y'=4,'x'=4,'core'=2,'sec'=8] {'core','sec'}, dimensions={0} | all-to-all | bytes 147456 | tf_op jit(solution)/shard_map/all_to_all | solution.py:137
  135.1 0.9 shard_map.76
  136.0 10.7 %all_to_all.74.got_ref = s16[16,80,128]{2,1,0:T(8,128)(2,1)S(1)} all-to-all(s16[16,80,128]{2,1,0:T(8,128)(2,1)S(1)} %shard_map.76), channel_id=1, replica_groups=mesh['y'=4,'x'=4,'core'=2,'sec'=8] {'y','x'}, dimensions={0} | all-to-all | bytes 655360 | tf_op jit(solution)/shard_map/all_to_all | solution.py:137
  146.8 2.7 %shard_map.77 = (f32[2,1024,128]{2,1,0:T(8,128)S(1)}, f32[8,1024]{1,0:T(8,128)S(1)}, f32[8,1024]{1,0:T(8,128)S(1)}, f32[8,1024]{1,0:T(8,128)S(1)}, f32[8,128]{1,...) custom-call(s32[4,2]{1,0:T(4,128)S(1)} %select_select_fusion.meta_ref, s16[16,80,128]{2,1,0:T(8,128)(2,1)S(1)} %all_to_all.74.got_ref, ...), custom_call_target="tpu_custom_call" | custom-call | flops 536870912 | bytes 9408544 | tf_op jit(solution)/shard_map/pallas_call | solution.py:30
  149.5 17.7 %all_to_all.75.moved_ref = bf16[8,2,128,128]{3,2,1,0:T(8,128)(2,1)S(1)} all-to-all(bf16[8,2,128,128]{3,2,1,0:T(8,128)(2,1)S(1)} %get-tuple-element.54), channel_id=1, replica_groups=mesh['y'=4,'x'=4,'core'=2,'sec'=8] {'sec'}, dimensions={0} | all-to-all | bytes 1048576 | tf_op jit(solution)/shard_map/all_to_all | solution.py:137
  167.2 2.1 %shard_map.78 = bf16[16,8,1024]{2,1,0:T(8,128)(2,1)S(1)} custom-call(s32[4,2]{1,0:T(4,128)S(1)} %select_select_fusion.meta_ref, bf16[8,2,128,128]{3,2,1,0:T(8,128)(2,1)S(1)} %all_to_all.75.moved_ref, bf16[1,2,1024,1024]{3,2,1,0:T(8,128)(2,1)S(1)} %copy-done.1, bf16[1024,1024]{1,0:T(8,128)(2,1)S(1)} %collective-permute-done.1.got_ref), custom_call_target="tpu_custom_call" | custom-call | flops 536870912 | bytes 6815776 | tf_op jit(solution)/shard_map/pallas_call | solution.py:30
  169.3 10.7 %all_to_all.76.got_ref = bf16[16,8,1024]{2,1,0:T(8,128)(2,1)S(1)} all-to-all(bf16[16,8,1024]{2,1,0:T(8,128)(2,1)S(1)} %shard_map.78), channel_id=1, replica_groups=mesh['y'=4,'x'=4,'core'=2,'sec'=8] {'y','x'}, dimensions={0} | all-to-all | bytes 524288 | tf_op jit(solution)/shard_map/all_to_all | solution.py:137
  180.0 4.8 %collective-permute-start.2 = (f32[2,1024,128]{2,1,0:T(8,128)S(1)}, f32[2,1024,128]{2,1,0:T(8,128)S(1)}, u32[]{:S(2)}, u32[]{:S(2)}) collective-permute-start(f32[2,1024,128]{2,1,0:T(8,128)S(1)} %get-tuple-element.61.pair_ref), channel_id=1, source_target_pairs={{0,8},{8,0},{1,9},{9,1},{2,10},{10,2},{3,11},{11,3},{4,12},{12,4},... | collective-permute-start | bytes 3145736 | tf_op jit(solution)/shard_map/ppermute | solution.py:421
  184.8 0.7 shard_map.79
  185.5 18.0 %all_to_all.77 = f32[256,1,128]{2,1,0:T(1,128)S(1)} all-to-all(f32[256,1,128]{2,1,0:T(1,128)S(1)} %bitcast.16), channel_id=1, replica_groups=mesh['y'=4,'x'=4,'core'=2,'sec'=8] {'core','sec','y','x'}, dimensions={0} | all-to-all | bytes 262144 | tf_op jit(solution)/shard_map/all_to_all | solution.py:137
  203.5 0.0 collective-permute-done.2.far_ref
  203.5 2.4 %shard_map.80 = (f32[2,1024,128]{2,1,0:T(8,128)}, f32[1,1]{1,0:T(1,128)}) custom-call(s32[4,2]{1,0:T(4,128)S(1)} %select_select_fusion.meta_ref, f32[256,128]{1,0:T(8,128)S(1)} %bitcast.15, f32[8,128]{1,0:T(8,128)S(1)} %get-tuple-element.60.theta_ref, f32[2,1024,128]{2,1,0:T(8,128)S(1)} %get-tuple-element.61.pair_ref, ...), custom_call_target="tpu_custom_call" | custom-call | bytes 2232352 | tf_op jit(solution)/shard_map/pallas_call | solution.py:30
  (2 shorter events, 0.0 us)
Async XLA Ops:
  1.4 1.2 copy-start.3
  2.7 2.2 %copy-start = (bf16[1,2,1024,1024]{3,2,1,0:T(8,128)(2,1)S(1)}, bf16[1,2,1024,1024]{3,2,1,0:T(8,128)(2,1)}, u32[]{:S(2)}) copy-start(bf16[1,2,1024,1024]{3,2,1,0:T(8,128)(2,1)} %env_ref.4) | copy-start | bytes 12582916
  5.0 16.5 %collective-permute-start = (bf16[1024,1024]{1,0:T(8,128)(2,1)S(1)}, bf16[1024,1024]{1,0:T(8,128)(2,1)S(1)}, u32[]{:S(2)}, u32[]{:S(2)}) collective-permute-start(bf16[1024,1024]{1,0:T(8,128)(2,1)S(1)} %dynamic-slice_bitcast_fusion.1), channel_id=1, source_target_pairs={{0,8},{8,0},{1,9},{9,1},{2,10},{10,2},{3,11},{11,3},{4,12},{12,4},... | collective-permute-start | bytes 6291464 | tf_op jit(solution)/shard_map/ppermute | solution.py:366
  21.5 2.2 %copy-start.1 = (bf16[1,2,1024,1024]{3,2,1,0:T(8,128)(2,1)S(1)}, bf16[1,2,1024,1024]{3,2,1,0:T(8,128)(2,1)}, u32[]{:S(2)}) copy-start(bf16[1,2,1024,1024]{3,2,1,0:T(8,128)(2,1)} %env_ref.5) | copy-start | bytes 12582916
  23.9 22.0 %collective-permute-start.1 = (bf16[1024,1024]{1,0:T(8,128)(2,1)S(1)}, bf16[1024,1024]{1,0:T(8,128)(2,1)S(1)}, u32[]{:S(2)}, u32[]{:S(2)}) collective-permute-start(bf16[1024,1024]{1,0:T(8,128)(2,1)S(1)} %dynamic-slice_bitcast_fusion), channel_id=1, source_target_pairs={{0,8},{8,0},{1,9},{9,1},{2,10},{10,2},{3,11},{11,3},{4,12},{12,4},... | collective-permute-start | bytes 6291464 | tf_op jit(solution)/shard_map/ppermute | solution.py:366
  45.8 17.8 %copy-start.2 = (f32[2,1024,128]{2,1,0:T(8,128)S(1)}, f32[2,1024,128]{2,1,0:T(8,128)}, u32[]{:S(2)}) copy-start(f32[2,1024,128]{2,1,0:T(8,128)} %diag_ref.5) | copy-start | bytes 3145732
  180.0 23.5 %collective-permute-start.2 = (f32[2,1024,128]{2,1,0:T(8,128)S(1)}, f32[2,1024,128]{2,1,0:T(8,128)S(1)}, u32[]{:S(2)}, u32[]{:S(2)}) collective-permute-start(f32[2,1024,128]{2,1,0:T(8,128)S(1)} %get-tuple-element.61.pair_ref), channel_id=1, source_target_pairs={{0,8},{8,0},{1,9},{9,1},{2,10},{10,2},{3,11},{11,3},{4,12},{12,4},... | collective-permute-start | bytes 3145736 | tf_op jit(solution)/shard_map/ppermute | solution.py:421
